TPU v7x, 128 devices: a whole 4x4x4 slice. The times are simulated.
128 devices in a mesh: az: 32 (over y, x_hi, z), ax: 4 (over x_lo, core).
Axes of the slice: x: 4 (x_hi: 2, x_lo: 2; x = x_hi * 2 + x_lo), y: 4, z: 4, core: 2. Of those that a mesh axis runs over, the one named last changes fastest.
Arguments:
- start_field: float32 [16, 3, 64, 32, 512], P(None, None, 'az', 'ax'), may hold values from -4 to 4
- reluctivity: float32 [3, 64, 32, 512], P(None, 'az', 'ax'), may hold values from 0.05 to 1
- lamination: int32 [64, 32, 512], P('az', 'ax'), may hold values 0 or 1
- magnets: int32 [64, 32, 512], P('az', 'ax'), may hold values 0 or 1
- region_ids: int32 [64, 32, 512], P('az', 'ax'), may hold values from 0 to 127, as said below
- pieces: float32 [3, 16, 128], P(None, None, 'az'), may hold values from -5 to 5
- slot_map: int32 [16, 128], replicated, may hold values from 0 to 127, each once within a row
Outputs:
- solution_field: float32 [16, 3, 64, 32, 512], P(None, None, 'az', 'ax')
- residual: float32 [16, 3, 64, 32, 512], P(None, None, 'az', 'ax')
Inputs may be any that keep to these rules, and one draw needn't show every extreme that they name: `region_ids`: a cell of azimuthal sector s, the cells s * 2 to (s + 1) * 2 - 1 along the azimuth, holds a slot from s * 4 to (s + 1) * 4 - 1. `slot_map`: each row is a permutation.
All inputs are finite; a program needn't handle non-finite values. No bound on the sum of `lamination` or of `magnets` on one device may be relied on, other than what follows from the above.
Results may differ from a plain program's by a relative error of at most 0.00002.
Values sent between devices are 32-bit elements; how exact they have to be, the bound alone decides.
No kernel may reach another device: no remote copies, remote signals or barrier semaphores. Data moves between devices by JAX's collectives and lax.ppermute only.
A program may use at most 128 MiB of HBM per device.

v0:
```python
import jax
import jax.numpy as jnp
from jax import lax
from jax.sharding import PartitionSpec as P

mass_term = 1.0
cheb_centre = 8.5
cheb_halfwidth = 7.5
cheb_sigma = cheb_centre / cheb_halfwidth
rho_first = 1.0 / cheb_sigma
rho_second = 1.0 / (2.0 * cheb_sigma - rho_first)


def passed_along(value, axis, steps):
    count = lax.axis_size(axis)
    pairs = [(source, (source + steps) % count) for source in range(count)]
    return lax.ppermute(value, axis, pairs)


def from_behind(value, axis, steps):
    count = lax.axis_size(axis)
    first, last = (max(0, -steps), min(count, count - steps))
    return lax.ppermute(value, axis, [(source, source + steps) for source in range(first, last)])


def radial_forward(values):
    return jnp.concatenate([values[..., 1:], jnp.zeros_like(values[..., :1])], axis=-1) - values


def radial_backward(values):
    return values - jnp.concatenate([jnp.zeros_like(values[..., :1]), values[..., :-1]], axis=-1)


def curl_forward(core, along_a1, along_a2, along_z0, along_z2):
    return jnp.stack(
        [
            along_z2 - radial_forward(core[:, 1]),
            radial_forward(core[:, 0]) - along_a2,
            along_a1 - along_z0,
        ],
        axis=1,
    )


def curl_backward(core, along_a1, along_a2, along_z0, along_z2):
    return jnp.stack(
        [
            along_z2 - radial_backward(core[:, 1]),
            radial_backward(core[:, 0]) - along_a2,
            along_a1 - along_z0,
        ],
        axis=1,
    )


def residual_shifts(field, reluct, source):
    ahead_az = passed_along(field[:, 1:3, 0:1], "az", -1)
    ahead_ax = from_behind(jnp.stack([field[:, 0, :, 0:1], field[:, 2, :, 0:1]], axis=1), "ax", -1)
    step_az = jnp.concatenate([field[:, 1:3, 1:], ahead_az], axis=2) - field[:, 1:3]
    pair_field = jnp.stack([field[:, 0], field[:, 2]], axis=1)
    step_ax = jnp.concatenate([pair_field[:, :, :, 1:], ahead_ax], axis=3) - pair_field
    flux = curl_forward(field, step_az[:, 0], step_az[:, 1], step_ax[:, 0], step_ax[:, 1])
    intensity = reluct[None] * (flux - source)
    behind_az = passed_along(intensity[:, 1:3, -1:], "az", 1)
    behind_ax = from_behind(
        jnp.stack([intensity[:, 0, :, -1:], intensity[:, 2, :, -1:]], axis=1), "ax", 1
    )
    back_step_az = intensity[:, 1:3] - jnp.concatenate([behind_az, intensity[:, 1:3, :-1]], axis=2)
    pair_inten = jnp.stack([intensity[:, 0], intensity[:, 2]], axis=1)
    back_step_ax = pair_inten - jnp.concatenate([behind_ax, pair_inten[:, :, :, :-1]], axis=3)
    curl = curl_backward(
        intensity, back_step_az[:, 0], back_step_az[:, 1], back_step_ax[:, 0], back_step_ax[:, 1]
    )
    return -curl - mass_term * field


def shards(start_field, reluctivity, lamination, magnets, region_ids, pieces, slot_map):
    devs, comps, cells_az, cells_ax, radial = start_field.shape
    axial = jnp.array([0.0, 1.0, 0.0], jnp.float32)
    reluct = reluctivity * (
        1.0 + 3.0 * lamination.astype(jnp.float32)[None] * axial[:, None, None, None]
    )
    every_piece = lax.all_gather(pieces, "az", axis=2, tiled=True)
    slots_here = pieces.shape[2]
    base = lax.axis_index("az") * slots_here
    local_map = lax.dynamic_slice_in_dim(slot_map, base, slots_here, 1)
    local_table = jnp.take_along_axis(
        every_piece, jnp.broadcast_to(local_map[None], (comps, devs, slots_here)), axis=2
    )
    offset = (region_ids - base)[None, None]
    source = jnp.zeros(start_field.shape, jnp.float32)
    for slot in range(slots_here):
        values = jnp.transpose(local_table[:, :, slot])[:, :, None, None, None]
        source = jnp.where(offset == slot, values, source)
    source = source * magnets.astype(jnp.float32)[None, None]

    def residual_fn(field):
        return residual_shifts(field, reluct, source)

    first_res = residual_fn(start_field)
    first_dir = first_res / cheb_centre
    middle = start_field + first_dir
    second_res = residual_fn(middle)
    second_dir = rho_second * rho_first * first_dir + 2.0 * rho_second / cheb_halfwidth * second_res
    final = middle + second_dir
    return (final, residual_fn(final))


def solution(mesh):
    placed = (
        P(None, None, "az", "ax", None),
        P(None, "az", "ax", None),
        P("az", "ax", None),
        P("az", "ax", None),
        P("az", "ax", None),
        P(None, None, "az"),
        P(),
    )
    return jax.shard_map(
        shards,
        mesh=mesh,
        in_specs=placed,
        out_specs=(P(None, None, "az", "ax", None), P(None, None, "az", "ax", None)),
        check_vma=False,
    )
```

profile of v0, /device:TPU:0, one launch (start us, length us, event | category | flops | bytes accessed | tf_op | source)
XLA Modules:
  0.0 234.6 jit_solution(2493041710991904258)
XLA Ops:
  0.6 1.4 fusion.57
  2.8 1.3 collective-permute-start
  4.1 2.3 fusion.56
  6.4 9.0 %collective-permute-start.1 = (f32[16,2,1,8,512]{4,3,2,0,1:T(8,128)}, f32[16,2,1,8,512]{4,3,2,0,1:T(8,128)}, u32[]{:S(2)}, u32[]{:S(2)}) collective-permute-start(f32[16,2,1,8,512]{4,3,2,0,1:T(8,128)} %get-tuple-element.77), channel_id=1, source_target_pairs={{0,124},{4,0},{8,4},{12,8},{16,12},{20,16},{24,20},{28,24},{32,28}... | collective-permute-start | bytes 1572872 | tf_op jit(solution)/shard_map/ppermute | solution.py:17
  15.4 1.1 slice_bitcast_fusion.17
  16.5 98.3 %all_gather.3 = f32[3,16,128]{1,0,2:T(4,128)S(1)} all-gather(f32[3,16,4]{1,0,2:T(4,128)S(1)} %copy.91), channel_id=1, replica_groups=mesh['az'=32,'ax'=4] {'az'}, dimensions={2}, use_global_device_ids=true | all-gather | bytes 25344 | tf_op jit(solution)/shard_map/all_gather | solution.py:83
  116.9 2.1 gather_fusion
  121.6 1.2 slice.393
  124.4 1.3 slice_subtract_fusion.5
  126.1 1.0 fusion
  127.4 1.3 collective-permute-start.2
  130.1 18.5 %collective-permute-done.3 = f32[16,2,1,8,512]{4,3,2,0,1:T(8,128)S(1)} collective-permute-done((f32[16,2,1,8,512]{4,3,2,0,1:T(8,128)S(1)}, f32[16,2,1,8,512]{4,3,2,0,1:T(8,128)S(1)}, u32[]{:S(2)}, u32[]{:S(2)}) %collective-permute-start.3) | collective-permute-done | bytes 524320 | tf_op jit(solution)/shard_map/ppermute | solution.py:17
  150.0 1.3 collective-permute-start.4
  152.2 1.1 collective-permute-done.4
  153.6 12.3 %collective-permute-done.5 = f32[16,2,1,8,512]{4,3,2,0,1:T(8,128)S(1)} collective-permute-done((f32[16,2,1,8,512]{4,3,2,0,1:T(8,128)S(1)}, f32[16,2,1,8,512]{4,3,2,0,1:T(8,128)S(1)}, u32[]{:S(2)}, u32[]{:S(2)}) %collective-permute-start.5) | collective-permute-done | bytes 524320 | tf_op jit(solution)/shard_map/ppermute | solution.py:17
  166.6 1.0 fusion.2
  167.9 2.0 collective-permute-start.6
  171.3 18.5 %collective-permute-done.7 = f32[16,2,1,8,512]{4,3,2,0,1:T(8,128)S(1)} collective-permute-done((f32[16,2,1,8,512]{4,3,2,0,1:T(8,128)S(1)}, f32[16,2,1,8,512]{4,3,2,0,1:T(8,128)S(1)}, u32[]{:S(2)}, u32[]{:S(2)}) %collective-permute-start.7) | collective-permute-done | bytes 524320 | tf_op jit(solution)/shard_map/ppermute | solution.py:17
  191.4 1.3 collective-permute-start.8
  193.6 1.0 collective-permute-done.8
  194.9 12.5 %collective-permute-done.9 = f32[16,2,1,8,512]{4,3,2,0,1:T(8,128)S(1)} collective-permute-done((f32[16,2,1,8,512]{4,3,2,0,1:T(8,128)S(1)}, f32[16,2,1,8,512]{4,3,2,0,1:T(8,128)S(1)}, u32[]{:S(2)}, u32[]{:S(2)}) %collective-permute-start.9) | collective-permute-done | bytes 524320 | tf_op jit(solution)/shard_map/ppermute | solution.py:17
  209.4 2.0 collective-permute-start.10
  212.8 18.3 %collective-permute-done.11 = f32[16,2,1,8,512]{4,3,2,0,1:T(8,128)S(1)} collective-permute-done((f32[16,2,1,8,512]{4,3,2,0,1:T(8,128)S(1)}, f32[16,2,1,8,512]{4,3,2,0,1:T(8,128)S(1)}, u32[]{:S(2)}, u32[]{:S(2)}) %collective-permute-start.11) | collective-permute-done | bytes 524320 | tf_op jit(solution)/shard_map/ppermute | solution.py:17
  231.8 2.8 %fusion.8 = (f32[16,3,2,8,512]{4,3,2,1,0:T(8,128)}, f32[16,3,2,8,512]{4,3,2,1,0:T(8,128)}) fusion(f32[16,1,2,8,512]{4,3,2,1,0:T(8,128)S(1)} %slice_subtract_fusion.6, f32[16,1,2,8,512]{4,3,2,1,0:T(8,128)S(1)} %get-tuple-element.21, f32[16,1,2,8,512]{4,3,2,1,0:T(8,128)S(1)} %get-tuple-element.20, f32[16,1,2,8,512]{4,3,2,0,1:T(8,128)S(1)} %slice_subtract_fusion.8, ...), kind=kLoop, calls=%fused_computation.15 | loop fusion | flops 7077888 | bytes 9437184 | tf_op jit(solution)/shard_map/sub | solution.py:74
  (98 shorter events, 20.5 us)
Async XLA Ops:
  0.6 14.8 %copy-start = (f32[16,3,2,8,512]{4,3,2,1,0:T(8,128)S(1)}, f32[16,3,2,8,512]{4,3,2,1,0:T(8,128)}, u32[]{:S(2)}) copy-start(f32[16,3,2,8,512]{4,3,2,1,0:T(8,128)} %param.8) | copy-start | bytes 4718596
  2.8 120.6 %collective-permute-start = (f32[16,2,2,1,512]{4,3,2,0,1:T(1,128)}, f32[16,2,2,1,512]{4,3,2,0,1:T(1,128)S(1)}, u32[]{:S(2)}, u32[]{:S(2)}) collective-permute-start(f32[16,2,2,1,512]{4,3,2,0,1:T(1,128)} %pad_maximum_fusion.7), channel_id=1, source_target_pairs={{1,0},{2,1},{3,2},{5,4},{6,5},{7,6},{9,8},{10,9},{11,10},{13,12},{... | collective-permute-start | bytes 393224 | tf_op jit(solution)/shard_map/ppermute | solution.py:23
  6.4 10.1 %copy-start.7 = (f32[3,16,4]{1,2,0:T(4,128)S(1)}, f32[3,16,4]{1,2,0:T(4,128)}, u32[]{:S(2)}) copy-start(f32[3,16,4]{1,2,0:T(4,128)} %param.13) | copy-start | bytes 2308
  6.4 108.4 %copy-start.6 = (s32[16,128]{1,0:T(8,128)S(1)}, s32[16,128]{1,0:T(8,128)}, u32[]{:S(2)}) copy-start(s32[16,128]{1,0:T(8,128)} %param.14) | copy-start | bytes 24580
  6.4 117.3 %collective-permute-start.1 = (f32[16,2,1,8,512]{4,3,2,0,1:T(8,128)}, f32[16,2,1,8,512]{4,3,2,0,1:T(8,128)}, u32[]{:S(2)}, u32[]{:S(2)}) collective-permute-start(f32[16,2,1,8,512]{4,3,2,0,1:T(8,128)} %get-tuple-element.77), channel_id=1, source_target_pairs={{0,124},{4,0},{8,4},{12,8},{16,12},{20,16},{24,20},{28,24},{32,28}... | collective-permute-start | bytes 1572872 | tf_op jit(solution)/shard_map/ppermute | solution.py:17
  114.9 0.6 copy-start.5
  114.9 0.6 copy-start.3
  119.1 4.0 %copy-start.4 = (s32[2,8,512]{2,1,0:T(8,128)S(1)}, s32[2,8,512]{2,1,0:T(8,128)}, u32[]{:S(2)}) copy-start(s32[2,8,512]{2,1,0:T(8,128)} %param.11) | copy-start | bytes 98308
  119.1 4.0 %copy-start.2 = (f32[3,2,8,512]{3,2,1,0:T(8,128)S(1)}, f32[3,2,8,512]{3,2,1,0:T(8,128)}, u32[]{:S(2)}) copy-start(f32[3,2,8,512]{3,2,1,0:T(8,128)} %param.9) | copy-start | bytes 294916
  119.1 4.0 %copy-start.8 = (f32[3]{0:T(128)S(1)}, f32[3]{0:T(128)}, u32[]{:S(2)}) copy-start(f32[3]{0:T(128)} %constant.50.clone) | copy-start | bytes 40
  123.3 1.0 copy-start.1
  127.4 2.3 collective-permute-start.2
  128.7 19.9 %collective-permute-start.3 = (f32[16,2,1,8,512]{4,3,2,0,1:T(8,128)S(1)}, f32[16,2,1,8,512]{4,3,2,0,1:T(8,128)S(1)}, u32[]{:S(2)}, u32[]{:S(2)}) collective-permute-start(f32[16,2,1,8,512]{4,3,2,0,1:T(8,128)S(1)} %get-tuple-element.66), channel_id=1, source_target_pairs={{0,4},{4,8},{8,12},{12,16},{16,20},{20,24},{24,28},{28,32},{32,36}... | collective-permute-start | bytes 1572872 | tf_op jit(solution)/shard_map/ppermute | solution.py:17
  150.0 3.3 %collective-permute-start.4 = (f32[16,2,2,1,512]{4,3,2,0,1:T(1,128)S(1)}, f32[16,2,2,1,512]{4,3,2,0,1:T(1,128)S(1)}, u32[]{:S(2)}, u32[]{:S(2)}) collective-permute-start(f32[16,2,2,1,512]{4,3,2,0,1:T(1,128)S(1)} %pad_maximum_fusion.9), channel_id=1, source_target_pairs={{1,0},{2,1},{3,2},{5,4},{6,5},{7,6},{9,8},{10,9},{11,10},{13,12},{... | collective-permute-start | bytes 393224 | tf_op jit(solution)/shard_map/ppermute | solution.py:23
  151.3 14.6 %collective-permute-start.5 = (f32[16,2,1,8,512]{4,3,2,0,1:T(8,128)S(1)}, f32[16,2,1,8,512]{4,3,2,0,1:T(8,128)S(1)}, u32[]{:S(2)}, u32[]{:S(2)}) collective-permute-start(f32[16,2,1,8,512]{4,3,2,0,1:T(8,128)S(1)} %get-tuple-element.57), channel_id=1, source_target_pairs={{0,124},{4,0},{8,4},{12,8},{16,12},{20,16},{24,20},{28,24},{32,28}... | collective-permute-start | bytes 1572872 | tf_op jit(solution)/shard_map/ppermute | solution.py:17
  167.9 3.0 %collective-permute-start.6 = (f32[16,2,2,1,512]{4,3,2,0,1:T(1,128)S(1)}, f32[16,2,2,1,512]{4,3,2,0,1:T(1,128)S(1)}, u32[]{:S(2)}, u32[]{:S(2)}) collective-permute-start(f32[16,2,2,1,512]{4,3,2,0,1:T(1,128)S(1)} %pad_maximum_fusion.10), channel_id=1, source_target_pairs={{0,1},{1,2},{2,3},{4,5},{5,6},{6,7},{8,9},{9,10},{10,11},{12,13},{... | collective-permute-start | bytes 393224 | tf_op jit(solution)/shard_map/ppermute | solution.py:23
  170.0 19.8 %collective-permute-start.7 = (f32[16,2,1,8,512]{4,3,2,0,1:T(8,128)S(1)}, f32[16,2,1,8,512]{4,3,2,0,1:T(8,128)S(1)}, u32[]{:S(2)}, u32[]{:S(2)}) collective-permute-start(f32[16,2,1,8,512]{4,3,2,0,1:T(8,128)S(1)} %get-tuple-element.46), channel_id=1, source_target_pairs={{0,4},{4,8},{8,12},{12,16},{16,20},{20,24},{24,28},{28,32},{32,36}... | collective-permute-start | bytes 1572872 | tf_op jit(solution)/shard_map/ppermute | solution.py:17
  191.4 3.2 %collective-permute-start.8 = (f32[16,2,2,1,512]{4,3,2,0,1:T(1,128)S(1)}, f32[16,2,2,1,512]{4,3,2,0,1:T(1,128)S(1)}, u32[]{:S(2)}, u32[]{:S(2)}) collective-permute-start(f32[16,2,2,1,512]{4,3,2,0,1:T(1,128)S(1)} %pad_maximum_fusion.11), channel_id=1, source_target_pairs={{1,0},{2,1},{3,2},{5,4},{6,5},{7,6},{9,8},{10,9},{11,10},{13,12},{... | collective-permute-start | bytes 393224 | tf_op jit(solution)/shard_map/ppermute | solution.py:23
  192.7 14.7 %collective-permute-start.9 = (f32[16,2,1,8,512]{4,3,2,0,1:T(8,128)S(1)}, f32[16,2,1,8,512]{4,3,2,0,1:T(8,128)S(1)}, u32[]{:S(2)}, u32[]{:S(2)}) collective-permute-start(f32[16,2,1,8,512]{4,3,2,0,1:T(8,128)S(1)} %get-tuple-element.37), channel_id=1, source_target_pairs={{0,124},{4,0},{8,4},{12,8},{16,12},{20,16},{24,20},{28,24},{32,28}... | collective-permute-start | bytes 1572872 | tf_op jit(solution)/shard_map/ppermute | solution.py:17
  209.4 3.0 %collective-permute-start.10 = (f32[16,2,2,1,512]{4,3,2,0,1:T(1,128)S(1)}, f32[16,2,2,1,512]{4,3,2,0,1:T(1,128)S(1)}, u32[]{:S(2)}, u32[]{:S(2)}) collective-permute-start(f32[16,2,2,1,512]{4,3,2,0,1:T(1,128)S(1)} %pad_maximum_fusion.12), channel_id=1, source_target_pairs={{0,1},{1,2},{2,3},{4,5},{5,6},{6,7},{8,9},{9,10},{10,11},{12,13},{... | collective-permute-start | bytes 393224 | tf_op jit(solution)/shard_map/ppermute | solution.py:23
  211.5 19.6 %collective-permute-start.11 = (f32[16,2,1,8,512]{4,3,2,0,1:T(8,128)S(1)}, f32[16,2,1,8,512]{4,3,2,0,1:T(8,128)S(1)}, u32[]{:S(2)}, u32[]{:S(2)}) collective-permute-start(f32[16,2,1,8,512]{4,3,2,0,1:T(8,128)S(1)} %get-tuple-element.26), channel_id=1, source_target_pairs={{0,4},{4,8},{8,12},{12,16},{16,20},{20,24},{24,28},{28,32},{32,36}... | collective-permute-start | bytes 1572872 | tf_op jit(solution)/shard_map/ppermute | solution.py:17
where the time goes:
time: 235 us
  blocking collectives  98.3 us (42%)
  waiting for transfers between devices  83.6 us (36%)
  other arithmetic  19 us (8%)
  starting transfers between devices  18.8 us (8%)
  local copies, waits for them, and re-layouts  13.7 us (6%)
    all_gather x1, blocking collectives, shards(): every_piece = lax.all_gather(pieces, 'az', axis=2, tiled=True)  98.3 us
    ppermute x6, waiting for transfers between devices, passed_along(): return lax.ppermute(value, axis, pairs)  80.1 us
    ppermute x6, starting transfers between devices, passed_along(): return lax.ppermute(value, axis, pairs)  9.59 us
    ppermute x6, starting transfers between devices, from_behind(): lax.ppermute(value, axis, [(source, source + steps) for source in range(f...  9.22 us
  transfers between devices with their start and end apart: 12, of which 10 were waited for; matrix products, arithmetic and copies ran while one was open for 7% of the time, Pallas kernels for 0%

commit v1 on v0

v1 whole, which is shorter than its diff:
```python
import functools

import jax
import jax.numpy as jnp
from jax import lax
from jax.experimental import pallas as pl
from jax.experimental.pallas import tpu as pltpu
from jax.sharding import PartitionSpec as P

mass_term = 1.0
cheb_centre = 8.5
cheb_halfwidth = 7.5
cheb_sigma = cheb_centre / cheb_halfwidth
rho_first = 1.0 / cheb_sigma
rho_second = 1.0 / (2.0 * cheb_sigma - rho_first)

VMEM = pl.BlockSpec(memory_space=pltpu.VMEM)
SMEM = pl.BlockSpec(memory_space=pltpu.SMEM)
PARAMS = pltpu.CompilerParams(vmem_limit_bytes=48 * 1024 * 1024)


def moved(value, shift_az, shift_ax):
    count_az, count_ax = lax.axis_size("az"), lax.axis_size("ax")
    pairs = [
        (a * count_ax + q, (a + shift_az) % count_az * count_ax + q + shift_ax)
        for a in range(count_az)
        for q in range(count_ax)
        if 0 <= q + shift_ax < count_ax
    ]
    return lax.ppermute(value, ("az", "ax"), pairs)


def lanes(shape):
    return lax.broadcasted_iota(jnp.int32, shape, 1)


def rows(shape):
    return lax.broadcasted_iota(jnp.int32, shape, 0)


def radial_next(v):
    n = v.shape[1]
    return jnp.where(lanes(v.shape) == n - 1, 0.0, pltpu.roll(v, n - 1, 1))


def radial_prev(v):
    return jnp.where(lanes(v.shape) == 0, 0.0, pltpu.roll(v, 1, 1))


def axial_next(v, row):
    n = v.shape[0]
    return jnp.where(rows(v.shape) == n - 1, row, pltpu.roll(v, n - 1, 0))


def axial_prev(v, row):
    return jnp.where(rows(v.shape) == 0, row, pltpu.roll(v, 1, 0))


def pack(d, devs, a, minus, plus, ax_minus, ax_plus, corner_a, corner_b):
    top = a[0][0].shape[0] - 1
    minus[2 * d] = a[1][0]
    minus[2 * d + 1] = a[2][0]
    plus[2 * d] = radial_next(a[0][1]) - a[0][1] + a[2][1]
    plus[2 * d + 1] = a[0][1] - axial_next(a[0][1], 0.0) - a[1][1]
    for i in range(2):
        ax_minus[pl.ds(i * devs + d, 1)] = a[0][i][0:1]
        ax_minus[pl.ds((2 + i) * devs + d, 1)] = a[2][i][0:1]
        end = a[1][i][top:]
        ax_plus[pl.ds(i * devs + d, 1)] = end - radial_next(end) - a[2][i][top:]
    ax_plus[pl.ds(2 * devs + d, 1)] = a[1][1][top:] - a[1][0][top:] + a[0][0][top:]
    ax_plus[pl.ds(3 * devs + d, 1)] = a[0][1][top:] - a[1][1][top:]
    corner_a[pl.ds(d, 1)] = a[0][1][0:1]
    corner_b[pl.ds(d, 1)] = a[1][0][top:]


def first_kernel(
    a_ref, reluct_ref, lam_ref, mag_ref, reg_ref, base_ref,
    minus, plus, ax_minus, ax_plus, corner_a, corner_b, nu_ref, code_ref,
):
    devs = a_ref.shape[0]
    last = a_ref.shape[3] - 1
    base = base_ref[0]
    for i in range(2):
        axial = 1.0 + 3.0 * lam_ref[i].astype(jnp.float32)
        nu_ref[0, i] = reluct_ref[0, i]
        nu_ref[1, i] = reluct_ref[1, i] * axial
        nu_ref[2, i] = reluct_ref[2, i]
        code_ref[i] = jnp.where(mag_ref[i] == 1, reg_ref[i] - base + 1, 0).astype(jnp.float32)
    plus[2 * devs] = nu_ref[1, 1]
    plus[2 * devs + 1] = nu_ref[2, 1]
    plus[2 * devs + 2] = code_ref[1]
    for i in range(2):
        ax_plus[pl.ds(4 * devs + i, 1)] = nu_ref[0, i, last:]
        ax_plus[pl.ds(4 * devs + 2 + i, 1)] = nu_ref[2, i, last:]
        ax_plus[pl.ds(4 * devs + 4 + i, 1)] = code_ref[i, last:]
        ax_plus[pl.ds(4 * devs + 6 + i, 1)] = jnp.zeros_like(code_ref[i, last:])

    @pl.loop(0, devs)
    def _(d):
        a = [[a_ref[d, c, i] for i in range(2)] for c in range(3)]
        pack(d, devs, a, minus, plus, ax_minus, ax_plus, corner_a, corner_b)


def picked(code, values):
    out = jnp.zeros_like(code)
    for k, value in enumerate(values):
        out = jnp.where(code == k + 1.0, value, out)
    return out


def source_kernel(
    table_ref, slots_ref, where_ref, nu_ref, code_ref, halo_ref, ax_halo_ref,
    src_ref, src_az_ref, src_ax_ref,
):
    devs = src_ref.shape[0]
    here, behind, per = where_ref[0], where_ref[1], where_ref[2]
    count = table_ref.shape[1] // (3 * devs)

    @pl.loop(0, devs)
    def _(d):
        def value(c, first, k):
            slot = slots_ref[d, first + k]
            return table_ref[slot // count, (c * devs + d) * count + slot % count]

        for c in range(3):
            own = [value(c, here, k) for k in range(count)]
            for i in range(2):
                src_ref[d, c, i] = nu_ref[c, i] * picked(code_ref[i], own)
                if c != 1:
                    at = (c + i) * devs
                    src_ax_ref[pl.ds(at + d, 1)] = ax_halo_ref[pl.ds(4 * devs + c + i, 1)] * picked(
                        ax_halo_ref[pl.ds(4 * devs + 4 + i, 1)], own
                    )
            if c != 0:
                before = [value(c, behind, k) for k in range(count)]
                src_az_ref[2 * d + c - 1] = halo_ref[2 * devs + c - 1] * picked(halo_ref[2 * devs + 2], before)


def step_kernel(
    stage, a_ref, start_ref, nu_ref, src_ref, nu_az_ref, src_az_ref, nu_ax_ref, src_ax_ref,
    ahead, behind, ax_ahead, ax_behind, mine, corner_c, corner_d, out_ref, *rest,
):
    devs = a_ref.shape[0]
    *packed, edge = rest
    nu_az = 2 * devs
    for at, own, sign in ((0, 2, 1.0), (1, 3, 1.0), (2, 0, -1.0), (3, 1, -1.0)):
        part = pl.ds(at * devs, devs)
        flux = ax_behind[part] + sign * mine[pl.ds(own * devs, devs)]
        if at == 3:
            flux = flux + corner_d[...]
        edge[part] = nu_ax_ref[pl.ds(4 * devs + at, 1)] * flux - src_ax_ref[part]

    @pl.loop(0, devs)
    def _(d):
        a = [[a_ref[d, c, i] for i in range(2)] for c in range(3)]
        up = [None, ahead[2 * d], ahead[2 * d + 1]]
        inten = [[None, None], [None, None], [None, None]]
        for i in range(2):
            next1 = a[1][1] if i == 0 else up[1]
            next2 = a[2][1] if i == 0 else up[2]
            row0 = ax_ahead[pl.ds(i * devs + d, 1)]
            row2 = ax_ahead[pl.ds((2 + i) * devs + d, 1)]
            flux = (
                (axial_next(a[2][i], row2) - a[2][i]) - (radial_next(a[1][i]) - a[1][i]),
                (radial_next(a[0][i]) - a[0][i]) - (next2 - a[2][i]),
                (next1 - a[1][i]) - (axial_next(a[0][i], row0) - a[0][i]),
            )
            for c in range(3):
                inten[c][i] = nu_ref[c, i] * flux[c] - src_ref[d, c, i]
        corner = jnp.where(rows(a[1][0].shape) == a[1][0].shape[0] - 1, corner_c[pl.ds(d, 1)], 0.0)
        back1 = nu_az_ref[nu_az] * (behind[2 * d] - a[2][0]) - src_az_ref[2 * d]
        back2 = nu_az_ref[nu_az + 1] * (behind[2 * d + 1] + a[1][0] - corner) - src_az_ref[2 * d + 1]
        new = [[None, None], [None, None], [None, None]]
        for i in range(2):
            prev1 = back1 if i == 0 else inten[1][0]
            prev2 = back2 if i == 0 else inten[2][0]
            row0 = edge[pl.ds(i * devs + d, 1)]
            row2 = edge[pl.ds((2 + i) * devs + d, 1)]
            i0, i1, i2 = inten[0][i], inten[1][i], inten[2][i]
            curl = (
                (i2 - axial_prev(i2, row2)) - (i1 - radial_prev(i1)),
                (i0 - radial_prev(i0)) - (i2 - prev2),
                (i1 - prev1) - (i0 - axial_prev(i0, row0)),
            )
            for c in range(3):
                res = -curl[c] - mass_term * a[c][i]
                if stage == 0:
                    value = a[c][i] + res * (1.0 / cheb_centre)
                elif stage == 1:
                    first_dir = a[c][i] - start_ref[d, c, i]
                    value = a[c][i] + (
                        rho_second * rho_first * first_dir + 2.0 * rho_second / cheb_halfwidth * res
                    )
                else:
                    value = res
                out_ref[d, c, i] = value
                new[c][i] = value
        if stage < 2:
            pack(d, devs, new, *packed)


def f32(*shape):
    return jax.ShapeDtypeStruct(shape, jnp.float32)


def shards(start_field, reluctivity, lamination, magnets, region_ids, pieces, slot_map):
    devs, comps, cells_az, cells_ax, radial = start_field.shape
    count_az = lax.axis_size("az")
    per = pieces.shape[2]
    me = lax.axis_index("az")
    here = me * per
    behind_slots = (me + count_az - 1) % count_az * per
    where = jnp.stack([here, behind_slots, jnp.int32(per)]).astype(jnp.int32)

    messages = [
        f32(2 * devs, cells_ax, radial),
        f32(2 * devs, cells_ax, radial),
        f32(4 * devs, radial),
        f32(4 * devs, radial),
        f32(devs, radial),
        f32(devs, radial),
    ]
    first = list(messages)
    first[1] = f32(2 * devs + 3, cells_ax, radial)
    first[3] = f32(4 * devs + 8, radial)
    *packed, nu, code = pl.pallas_call(
        first_kernel,
        out_shape=first + [f32(*reluctivity.shape), f32(*lamination.shape)],
        in_specs=[VMEM] * 5 + [SMEM],
        out_specs=[VMEM] * 8,
        compiler_params=PARAMS,
    )(start_field, reluctivity, lamination, magnets, region_ids, where)

    def exchange(minus, plus, ax_minus, ax_plus, corner_a, corner_b):
        return (
            moved(minus, -1, 0),
            moved(plus, 1, 0),
            moved(ax_minus, 0, -1),
            moved(ax_plus, 0, 1),
            moved(corner_a, 1, -1),
            moved(corner_b, -1, 1),
        )

    halos = exchange(*packed)
    flat = pieces.reshape(1, comps * devs * per)
    table = lax.all_to_all(
        jnp.broadcast_to(flat, (count_az, comps * devs * per)), "az", 0, 0, tiled=True
    )
    nu_az, nu_ax = halos[1], halos[3]
    src, src_az, src_ax = pl.pallas_call(
        source_kernel,
        out_shape=[f32(*start_field.shape), f32(2 * devs, cells_ax, radial), f32(4 * devs, radial)],
        in_specs=[SMEM] * 3 + [VMEM] * 4,
        out_specs=[VMEM] * 3,
        compiler_params=PARAMS,
    )(table, slot_map, where, nu, code, nu_az, nu_ax)

    field, outs = start_field, []
    for stage in range(3):
        ahead, behind, ax_ahead, ax_behind, corner_c, corner_d = halos
        field, *new_packed = pl.pallas_call(
            functools.partial(step_kernel, stage),
            out_shape=[f32(*start_field.shape)] + (messages if stage < 2 else []),
            in_specs=[VMEM] * 15,
            out_specs=[VMEM] * (7 if stage < 2 else 1),
            scratch_shapes=[pltpu.VMEM((4 * devs, radial), jnp.float32)],
            compiler_params=PARAMS,
        )(
            field, start_field, nu, src, nu_az, src_az, nu_ax, src_ax,
            ahead, behind, ax_ahead, ax_behind, packed[2], corner_c, corner_d,
        )
        outs.append(field)
        if stage < 2:
            packed = new_packed
            halos = exchange(*packed)
    return outs[1], outs[2]


def solution(mesh):
    placed = (
        P(None, None, "az", "ax", None),
        P(None, "az", "ax", None),
        P("az", "ax", None),
        P("az", "ax", None),
        P("az", "ax", None),
        P(None, None, "az"),
        P(),
    )
    return jax.shard_map(
        shards,
        mesh=mesh,
        in_specs=placed,
        out_specs=(P(None, None, "az", "ax", None), P(None, None, "az", "ax", None)),
        check_vma=False,
    )
```

time: 235 us -> 129 us (0.55)
  blocking collectives: 98.3 us -> 13.6 us
  waiting for transfers between devices: 83.6 us -> 31.2 us
  starting transfers between devices: 18.8 us -> 48.8 us
  Pallas kernels: 0 us -> 25.4 us
  other arithmetic: 19 us -> 0.08 us
  local copies, waits for them, and re-layouts: 13.7 us -> 7.4 us
    all_gather x1 -> x0, blocking collectives: 98.3 us -> none  [shards(): every_piece = lax.all_gather(pieces, 'az', axis=2, tiled=True)]
    ppermute x12 -> x18, waiting for transfers between devices: 83.6 us -> 31.2 us  [moved(): return lax.ppermute(value, ('az', 'ax'), pairs)]
    ppermute x12 -> x18, starting transfers between devices: 18.8 us -> 48.8 us  [moved(): return lax.ppermute(value, ('az', 'ax'), pairs)]
    pallas_call x0 -> x5, Pallas kernels: none -> 25.4 us  [the longest x3 19 us: shards(): pl.pallas_call(functools.partial(step_kernel, stage), out_shape=[f32(*sta...]
    all_to_all x0 -> x1, blocking collectives: none -> 13.6 us  [shards(): lax.all_to_all(jnp.broadcast_to(flat, (count_az, comps * devs * per)), 'a...]
    sub x19 -> x0, other arithmetic: 7.69 us -> none  [the longest x1 2.79 us: residual_shifts(): return -curl - mass_term * field]
    slice x19 -> x0, local copies, waits for them, and re-layouts: 7.02 us -> none  [the longest x3 2.43 us: residual_shifts(): field[:, 1:3, 1:]]
    unnamed x19 -> x22, local copies, waits for them, and re-layouts: 1.33 us -> 7.28 us
  transfers between devices with their start and end apart: 12 -> 18, of which waited for: 10 -> 4; matrix products, arithmetic and copies ran while one was open for 7% -> 0% of each run, Pallas kernels for 0% -> 3%
where the time goes in v1:
time: 129 us; the launch traced here: 127 us
  starting transfers between devices  48.8 us (38%)
  waiting for transfers between devices  31.2 us (24%)
  Pallas kernels  25.4 us (20%)
  blocking collectives  13.6 us (11%)
  local copies, waits for them, and re-layouts  7.4 us (6%)
    ppermute x18, starting transfers between devices, moved(): return lax.ppermute(value, ('az', 'ax'), pairs)  48.8 us
    ppermute x18, waiting for transfers between devices, moved(): return lax.ppermute(value, ('az', 'ax'), pairs)  31.2 us
    pallas_call x3, Pallas kernels, shards(): pl.pallas_call(functools.partial(step_kernel, stage), out_shape=[f32(*sta...  19 us
    all_to_all x1, blocking collectives, shards(): lax.all_to_all(jnp.broadcast_to(flat, (count_az, comps * devs * per)), 'a...  13.6 us
    unnamed x22, local copies, waits for them, and re-layouts  7.28 us
    pallas_call x1, Pallas kernels, shards(): pl.pallas_call(source_kernel, out_shape=[f32(*start_field.shape), f32(2 *...  4.4 us
  transfers between devices with their start and end apart: 18, of which 4 were waited for; matrix products, arithmetic and copies ran while one was open for 0% of the time, Pallas kernels for 3%

profile of v1, /device:TPU:0, one launch (start us, length us, event | category | flops | bytes accessed | tf_op | source)
XLA Modules:
  0.0 127.4 jit_solution(14145154261714978062)
XLA Ops:
  0.7 1.4 %copy-done = f32[16,3,2,8,512]{4,3,2,1,0:T(8,128)S(1)} copy-done((f32[16,3,2,8,512]{4,3,2,1,0:T(8,128)S(1)}, f32[16,3,2,8,512]{4,3,2,1,0:T(8,128)}, u32[]{:S(2)}) %copy-start) | copy-done | bytes 1572888
  5.3 2.0 %shard_map.86 = (f32[32,8,512]{2,1,0:T(8,128)S(1)}, f32[35,8,512]{2,1,0:T(8,128)S(1)}, f32[64,512]{1,0:T(8,128)S(1)}, f32[72,512]{1,0:T(8,128)S(1)}, f32[16,512]...) custom-call(f32[16,3,2,8,512]{4,3,2,1,0:T(8,128)S(1)} %copy-done, ...), custom_call_target="tpu_custom_call" | custom-call | tf_op jit(solution)/shard_map/pallas_call | solution.py:226
  7.3 2.1 %collective-permute-start = (f32[35,8,512]{2,1,0:T(8,128)S(1)}, f32[35,8,512]{2,1,0:T(8,128)S(1)}, u32[]{:S(2)}, u32[]{:S(2)}) collective-permute-start(f32[35,8,512]{2,1,0:T(8,128)S(1)} %get-tuple-element.29), channel_id=1, source_target_pairs={{0,4},{1,5},{2,6},{3,7},{4,8},{5,9},{6,10},{7,11},{8,12},{9,13},{1... | collective-permute-start | bytes 1720328 | tf_op jit(solution)/shard_map/ppermute | solution.py:30
  9.4 7.1 %collective-permute-start.2 = (f32[32,8,512]{2,1,0:T(8,128)S(1)}, f32[32,8,512]{2,1,0:T(8,128)S(1)}, u32[]{:S(2)}, u32[]{:S(2)}) collective-permute-start(f32[32,8,512]{2,1,0:T(8,128)S(1)} %get-tuple-element.34), channel_id=1, source_target_pairs={{0,124},{1,125},{2,126},{3,127},{4,0},{5,1},{6,2},{7,3},{8,4},{9,5... | collective-permute-start | bytes 1572872 | tf_op jit(solution)/shard_map/ppermute | solution.py:30
  16.5 1.5 %collective-permute-start.1 = (f32[72,512]{1,0:T(8,128)S(1)}, f32[72,512]{1,0:T(8,128)S(1)}, u32[]{:S(2)}, u32[]{:S(2)}) collective-permute-start(f32[72,512]{1,0:T(8,128)S(1)} %get-tuple-element.30), channel_id=1, source_target_pairs={{0,1},{1,2},{2,3},{4,5},{5,6},{6,7},{8,9},{9,10},{10,11},{12,13},{... | collective-permute-start | bytes 442376 | tf_op jit(solution)/shard_map/ppermute | solution.py:30
  17.9 1.3 %collective-permute-start.3 = (f32[64,512]{1,0:T(8,128)S(1)}, f32[64,512]{1,0:T(8,128)S(1)}, u32[]{:S(2)}, u32[]{:S(2)}) collective-permute-start(f32[64,512]{1,0:T(8,128)S(1)} %get-tuple-element.35.mine), channel_id=1, source_target_pairs={{1,0},{2,1},{3,2},{5,4},{6,5},{7,6},{9,8},{10,9},{11,10},{13,12},{... | collective-permute-start | bytes 393224 | tf_op jit(solution)/shard_map/ppermute | solution.py:30
  19.2 1.3 %collective-permute-start.4 = (f32[16,512]{1,0:T(8,128)S(1)}, f32[16,512]{1,0:T(8,128)S(1)}, u32[]{:S(2)}, u32[]{:S(2)}) collective-permute-start(f32[16,512]{1,0:T(8,128)S(1)} %get-tuple-element.36), channel_id=1, source_target_pairs={{1,4},{2,5},{3,6},{5,8},{6,9},{7,10},{9,12},{10,13},{11,14},{13,16... | collective-permute-start | bytes 98312 | tf_op jit(solution)/shard_map/ppermute | solution.py:30
  20.5 11.6 %collective-permute-start.5 = (f32[16,512]{1,0:T(8,128)S(1)}, f32[16,512]{1,0:T(8,128)S(1)}, u32[]{:S(2)}, u32[]{:S(2)}) collective-permute-start(f32[16,512]{1,0:T(8,128)S(1)} %get-tuple-element.37), channel_id=1, source_target_pairs={{0,125},{1,126},{2,127},{4,1},{5,2},{6,3},{8,5},{9,6},{10,7},{12,9... | collective-permute-start | bytes 98312 | tf_op jit(solution)/shard_map/ppermute | solution.py:30
  32.4 13.6 %all_to_all.8 = f32[32,1,192]{2,1,0:T(1,128)S(1)} all-to-all(f32[32,1,192]{2,1,0:T(1,128)S(1)} %broadcast_in_dim.8), channel_id=1, replica_groups=mesh['az'=32,'ax'=4] {'az'}, dimensions={0} | all-to-all | bytes 49152 | tf_op jit(solution)/shard_map/all_to_all | solution.py:246
  45.9 4.4 %shard_map.87 = (f32[16,3,2,8,512]{4,3,2,1,0:T(8,128)S(1)}, f32[32,8,512]{2,1,0:T(8,128)S(1)}, f32[64,512]{1,0:T(8,128)S(1)}) custom-call(f32[32,192]{1,0:T(8,128)S(1)} %bitcast.5, s32[16,128]{1,0:T(8,128)S(1)} %copy-done.8, s32[3]{0:T(128)S(1)} %pad_add_fusion.base_ref.where_ref, f32[3,2,8,512]{3,2,1,0:T(8,128)S(1)} %get-tuple-element.27.nu_ref, ...), custom_call_target="tpu_custom_call" | custom-call | tf_op jit(solution)/shard_map/pallas_call | solution.py:250
  51.6 6.4 %shard_map.88 = (f32[16,3,2,8,512]{4,3,2,1,0:T(8,128)S(1)}, f32[32,8,512]{2,1,0:T(8,128)S(1)}, f32[32,8,512]{2,1,0:T(8,128)S(1)}, f32[64,512]{1,0:T(8,128)S(1)},...) custom-call(f32[16,3,2,8,512]{4,3,2,1,0:T(8,128)} %start_ref.5, ...), custom_call_target="tpu_custom_call" | custom-call | tf_op jit(solution)/shard_map/pallas_call | solution.py:261
  58.0 1.8 %collective-permute-start.6 = (f32[32,8,512]{2,1,0:T(8,128)S(1)}, f32[32,8,512]{2,1,0:T(8,128)S(1)}, u32[]{:S(2)}, u32[]{:S(2)}) collective-permute-start(f32[32,8,512]{2,1,0:T(8,128)S(1)} %get-tuple-element.39), channel_id=1, source_target_pairs={{0,124},{1,125},{2,126},{3,127},{4,0},{5,1},{6,2},{7,3},{8,4},{9,5... | collective-permute-start | bytes 1572872 | tf_op jit(solution)/shard_map/ppermute | solution.py:30
  60.1 2.2 %collective-permute-start.9 = (f32[64,512]{1,0:T(8,128)S(1)}, f32[64,512]{1,0:T(8,128)S(1)}, u32[]{:S(2)}, u32[]{:S(2)}) collective-permute-start(f32[64,512]{1,0:T(8,128)S(1)} %get-tuple-element.42), channel_id=1, source_target_pairs={{0,1},{1,2},{2,3},{4,5},{5,6},{6,7},{8,9},{9,10},{10,11},{12,13},{... | collective-permute-start | bytes 393224 | tf_op jit(solution)/shard_map/ppermute | solution.py:30
  62.2 1.3 %collective-permute-start.8 = (f32[64,512]{1,0:T(8,128)S(1)}, f32[64,512]{1,0:T(8,128)S(1)}, u32[]{:S(2)}, u32[]{:S(2)}) collective-permute-start(f32[64,512]{1,0:T(8,128)S(1)} %get-tuple-element.41.mine), channel_id=1, source_target_pairs={{1,0},{2,1},{3,2},{5,4},{6,5},{7,6},{9,8},{10,9},{11,10},{13,12},{... | collective-permute-start | bytes 393224 | tf_op jit(solution)/shard_map/ppermute | solution.py:30
  64.8 16.8 %collective-permute-done.10.corner_c = f32[16,512]{1,0:T(8,128)S(1)} collective-permute-done((f32[16,512]{1,0:T(8,128)S(1)}, f32[16,512]{1,0:T(8,128)S(1)}, u32[]{:S(2)}, u32[]{:S(2)}) %collective-permute-start.10) | collective-permute-done | bytes 32800 | tf_op jit(solution)/shard_map/ppermute | solution.py:30
  83.0 1.6 %collective-permute-done.11.corner_d = f32[16,512]{1,0:T(8,128)S(1)} collective-permute-done((f32[16,512]{1,0:T(8,128)S(1)}, f32[16,512]{1,0:T(8,128)S(1)}, u32[]{:S(2)}, u32[]{:S(2)}) %collective-permute-start.11) | collective-permute-done | bytes 32800 | tf_op jit(solution)/shard_map/ppermute | solution.py:30
  84.6 7.2 %shard_map.89 = (f32[16,3,2,8,512]{4,3,2,1,0:T(8,128)}, f32[32,8,512]{2,1,0:T(8,128)S(1)}, f32[32,8,512]{2,1,0:T(8,128)S(1)}, f32[64,512]{1,0:T(8,128)S(1)}, f32...) custom-call(f32[16,3,2,8,512]{4,3,2,1,0:T(8,128)S(1)} %get-tuple-element.38.a_ref, ...), custom_call_target="tpu_custom_call" | custom-call | tf_op jit(solution)/shard_map/pallas_call | solution.py:261
  91.8 2.0 %collective-permute-start.13 = (f32[32,8,512]{2,1,0:T(8,128)S(1)}, f32[32,8,512]{2,1,0:T(8,128)S(1)}, u32[]{:S(2)}, u32[]{:S(2)}) collective-permute-start(f32[32,8,512]{2,1,0:T(8,128)S(1)} %get-tuple-element.47), channel_id=1, source_target_pairs={{0,4},{1,5},{2,6},{3,7},{4,8},{5,9},{6,10},{7,11},{8,12},{9,13},{1... | collective-permute-start | bytes 1572872 | tf_op jit(solution)/shard_map/ppermute | solution.py:30
  93.9 7.5 %collective-permute-start.15 = (f32[64,512]{1,0:T(8,128)S(1)}, f32[64,512]{1,0:T(8,128)S(1)}, u32[]{:S(2)}, u32[]{:S(2)}) collective-permute-start(f32[64,512]{1,0:T(8,128)S(1)} %get-tuple-element.49), channel_id=1, source_target_pairs={{0,1},{1,2},{2,3},{4,5},{5,6},{6,7},{8,9},{9,10},{10,11},{12,13},{... | collective-permute-start | bytes 393224 | tf_op jit(solution)/shard_map/ppermute | solution.py:30
  103.9 11.2 %collective-permute-done.16.corner_c = f32[16,512]{1,0:T(8,128)S(1)} collective-permute-done((f32[16,512]{1,0:T(8,128)S(1)}, f32[16,512]{1,0:T(8,128)S(1)}, u32[]{:S(2)}, u32[]{:S(2)}) %collective-permute-start.16) | collective-permute-done | bytes 32800 | tf_op jit(solution)/shard_map/ppermute | solution.py:30
  115.1 3.8 %collective-permute-start.17 = (f32[16,512]{1,0:T(8,128)S(1)}, f32[16,512]{1,0:T(8,128)S(1)}, u32[]{:S(2)}, u32[]{:S(2)}) collective-permute-start(f32[16,512]{1,0:T(8,128)S(1)} %get-tuple-element.51), channel_id=1, source_target_pairs={{0,125},{1,126},{2,127},{4,1},{5,2},{6,3},{8,5},{9,6},{10,7},{12,9... | collective-permute-start | bytes 98312 | tf_op jit(solution)/shard_map/ppermute | solution.py:30
  119.0 1.6 %collective-permute-done.17.corner_d = f32[16,512]{1,0:T(8,128)S(1)} collective-permute-done((f32[16,512]{1,0:T(8,128)S(1)}, f32[16,512]{1,0:T(8,128)S(1)}, u32[]{:S(2)}, u32[]{:S(2)}) %collective-permute-start.17) | collective-permute-done | bytes 32800 | tf_op jit(solution)/shard_map/ppermute | solution.py:30
  120.6 1.4 %copy-done.3 = f32[16,3,2,8,512]{4,3,2,1,0:T(8,128)S(1)} copy-done((f32[16,3,2,8,512]{4,3,2,1,0:T(8,128)S(1)}, f32[16,3,2,8,512]{4,3,2,1,0:T(8,128)}, u32[]{:S(2)}) %copy-start.3) | copy-done | bytes 1572888
  122.0 5.4 %shard_map.90 = f32[16,3,2,8,512]{4,3,2,1,0:T(8,128)} custom-call(f32[16,3,2,8,512]{4,3,2,1,0:T(8,128)S(1)} %copy-done.3, f32[16,3,2,8,512]{4,3,2,1,0:T(8,128)S(1)} %copy-done.1, f32[3,2,8,512]{3,2,1,0:T(8,128)S(1)} %get-tuple-element.27.nu_ref, f32[16,3,2,8,512]{4,3,2,1,0:T(8,128)} %copy-done.2, ...), custom_call_target="tpu_custom_call" | custom-call | tf_op jit(solution)/shard_map/pallas_call | solution.py:261
  (43 shorter events, 10.1 us)
Async XLA Ops:
  0.6 31.5 %copy-start.9 = (f32[3,16,4]{1,2,0:T(4,128)S(1)}, f32[3,16,4]{1,2,0:T(4,128)}, u32[]{:S(2)}) copy-start(f32[3,16,4]{1,2,0:T(4,128)} %param.12) | copy-start | bytes 2308
  0.6 45.3 %copy-start.8 = (s32[16,128]{1,0:T(8,128)S(1)}, s32[16,128]{1,0:T(8,128)}, u32[]{:S(2)}) copy-start(s32[16,128]{1,0:T(8,128)} %slots_ref.1) | copy-start | bytes 24580
  0.7 1.4 %copy-start = (f32[16,3,2,8,512]{4,3,2,1,0:T(8,128)S(1)}, f32[16,3,2,8,512]{4,3,2,1,0:T(8,128)}, u32[]{:S(2)}) copy-start(f32[16,3,2,8,512]{4,3,2,1,0:T(8,128)} %start_ref.5) | copy-start | bytes 4718596
  7.3 38.6 %collective-permute-start = (f32[35,8,512]{2,1,0:T(8,128)S(1)}, f32[35,8,512]{2,1,0:T(8,128)S(1)}, u32[]{:S(2)}, u32[]{:S(2)}) collective-permute-start(f32[35,8,512]{2,1,0:T(8,128)S(1)} %get-tuple-element.29), channel_id=1, source_target_pairs={{0,4},{1,5},{2,6},{3,7},{4,8},{5,9},{6,10},{7,11},{8,12},{9,13},{1... | collective-permute-start | bytes 1720328 | tf_op jit(solution)/shard_map/ppermute | solution.py:30
  9.4 42.2 %collective-permute-start.2 = (f32[32,8,512]{2,1,0:T(8,128)S(1)}, f32[32,8,512]{2,1,0:T(8,128)S(1)}, u32[]{:S(2)}, u32[]{:S(2)}) collective-permute-start(f32[32,8,512]{2,1,0:T(8,128)S(1)} %get-tuple-element.34), channel_id=1, source_target_pairs={{0,124},{1,125},{2,126},{3,127},{4,0},{5,1},{6,2},{7,3},{8,4},{9,5... | collective-permute-start | bytes 1572872 | tf_op jit(solution)/shard_map/ppermute | solution.py:30
  16.5 4.1 %collective-permute-start.1 = (f32[72,512]{1,0:T(8,128)S(1)}, f32[72,512]{1,0:T(8,128)S(1)}, u32[]{:S(2)}, u32[]{:S(2)}) collective-permute-start(f32[72,512]{1,0:T(8,128)S(1)} %get-tuple-element.30), channel_id=1, source_target_pairs={{0,1},{1,2},{2,3},{4,5},{5,6},{6,7},{8,9},{9,10},{10,11},{12,13},{... | collective-permute-start | bytes 442376 | tf_op jit(solution)/shard_map/ppermute | solution.py:30
  17.9 33.6 %collective-permute-start.3 = (f32[64,512]{1,0:T(8,128)S(1)}, f32[64,512]{1,0:T(8,128)S(1)}, u32[]{:S(2)}, u32[]{:S(2)}) collective-permute-start(f32[64,512]{1,0:T(8,128)S(1)} %get-tuple-element.35.mine), channel_id=1, source_target_pairs={{1,0},{2,1},{3,2},{5,4},{6,5},{7,6},{9,8},{10,9},{11,10},{13,12},{... | collective-permute-start | bytes 393224 | tf_op jit(solution)/shard_map/ppermute | solution.py:30
  19.2 32.3 %collective-permute-start.4 = (f32[16,512]{1,0:T(8,128)S(1)}, f32[16,512]{1,0:T(8,128)S(1)}, u32[]{:S(2)}, u32[]{:S(2)}) collective-permute-start(f32[16,512]{1,0:T(8,128)S(1)} %get-tuple-element.36), channel_id=1, source_target_pairs={{1,4},{2,5},{3,6},{5,8},{6,9},{7,10},{9,12},{10,13},{11,14},{13,16... | collective-permute-start | bytes 98312 | tf_op jit(solution)/shard_map/ppermute | solution.py:30
  20.5 31.0 %collective-permute-start.5 = (f32[16,512]{1,0:T(8,128)S(1)}, f32[16,512]{1,0:T(8,128)S(1)}, u32[]{:S(2)}, u32[]{:S(2)}) collective-permute-start(f32[16,512]{1,0:T(8,128)S(1)} %get-tuple-element.37), channel_id=1, source_target_pairs={{0,125},{1,126},{2,127},{4,1},{5,2},{6,3},{8,5},{9,6},{10,7},{12,9... | collective-permute-start | bytes 98312 | tf_op jit(solution)/shard_map/ppermute | solution.py:30
  50.4 1.2 copy-start.2
  58.0 26.6 %collective-permute-start.6 = (f32[32,8,512]{2,1,0:T(8,128)S(1)}, f32[32,8,512]{2,1,0:T(8,128)S(1)}, u32[]{:S(2)}, u32[]{:S(2)}) collective-permute-start(f32[32,8,512]{2,1,0:T(8,128)S(1)} %get-tuple-element.39), channel_id=1, source_target_pairs={{0,124},{1,125},{2,126},{3,127},{4,0},{5,1},{6,2},{7,3},{8,4},{9,5... | collective-permute-start | bytes 1572872 | tf_op jit(solution)/shard_map/ppermute | solution.py:30
  59.8 24.8 %collective-permute-start.7 = (f32[32,8,512]{2,1,0:T(8,128)S(1)}, f32[32,8,512]{2,1,0:T(8,128)S(1)}, u32[]{:S(2)}, u32[]{:S(2)}) collective-permute-start(f32[32,8,512]{2,1,0:T(8,128)S(1)} %get-tuple-element.40), channel_id=1, source_target_pairs={{0,4},{1,5},{2,6},{3,7},{4,8},{5,9},{6,10},{7,11},{8,12},{9,13},{1... | collective-permute-start | bytes 1572872 | tf_op jit(solution)/shard_map/ppermute | solution.py:30
  60.1 24.5 %collective-permute-start.9 = (f32[64,512]{1,0:T(8,128)S(1)}, f32[64,512]{1,0:T(8,128)S(1)}, u32[]{:S(2)}, u32[]{:S(2)}) collective-permute-start(f32[64,512]{1,0:T(8,128)S(1)} %get-tuple-element.42), channel_id=1, source_target_pairs={{0,1},{1,2},{2,3},{4,5},{5,6},{6,7},{8,9},{9,10},{10,11},{12,13},{... | collective-permute-start | bytes 393224 | tf_op jit(solution)/shard_map/ppermute | solution.py:30
  62.2 22.3 %collective-permute-start.8 = (f32[64,512]{1,0:T(8,128)S(1)}, f32[64,512]{1,0:T(8,128)S(1)}, u32[]{:S(2)}, u32[]{:S(2)}) collective-permute-start(f32[64,512]{1,0:T(8,128)S(1)} %get-tuple-element.41.mine), channel_id=1, source_target_pairs={{1,0},{2,1},{3,2},{5,4},{6,5},{7,6},{9,8},{10,9},{11,10},{13,12},{... | collective-permute-start | bytes 393224 | tf_op jit(solution)/shard_map/ppermute | solution.py:30
  63.5 18.1 %collective-permute-start.10 = (f32[16,512]{1,0:T(8,128)S(1)}, f32[16,512]{1,0:T(8,128)S(1)}, u32[]{:S(2)}, u32[]{:S(2)}) collective-permute-start(f32[16,512]{1,0:T(8,128)S(1)} %get-tuple-element.43), channel_id=1, source_target_pairs={{1,4},{2,5},{3,6},{5,8},{6,9},{7,10},{9,12},{10,13},{11,14},{13,16... | collective-permute-start | bytes 98312 | tf_op jit(solution)/shard_map/ppermute | solution.py:30
  81.7 2.9 %collective-permute-start.11 = (f32[16,512]{1,0:T(8,128)S(1)}, f32[16,512]{1,0:T(8,128)S(1)}, u32[]{:S(2)}, u32[]{:S(2)}) collective-permute-start(f32[16,512]{1,0:T(8,128)S(1)} %get-tuple-element.44), channel_id=1, source_target_pairs={{0,125},{1,126},{2,127},{4,1},{5,2},{6,3},{8,5},{9,6},{10,7},{12,9... | collective-permute-start | bytes 98312 | tf_op jit(solution)/shard_map/ppermute | solution.py:30
  84.6 36.0 %copy-start.1 = (f32[16,3,2,8,512]{4,3,2,1,0:T(8,128)S(1)}, f32[16,3,2,8,512]{4,3,2,1,0:T(8,128)}, u32[]{:S(2)}) copy-start(f32[16,3,2,8,512]{4,3,2,1,0:T(8,128)} %start_ref.5) | copy-start | bytes 4718596
  91.8 28.7 %collective-permute-start.12 = (f32[32,8,512]{2,1,0:T(8,128)S(1)}, f32[32,8,512]{2,1,0:T(8,128)S(1)}, u32[]{:S(2)}, u32[]{:S(2)}) collective-permute-start(f32[32,8,512]{2,1,0:T(8,128)S(1)} %get-tuple-element.46), channel_id=1, source_target_pairs={{0,124},{1,125},{2,126},{3,127},{4,0},{5,1},{6,2},{7,3},{8,4},{9,5... | collective-permute-start | bytes 1572872 | tf_op jit(solution)/shard_map/ppermute | solution.py:30
  91.8 28.7 %collective-permute-start.13 = (f32[32,8,512]{2,1,0:T(8,128)S(1)}, f32[32,8,512]{2,1,0:T(8,128)S(1)}, u32[]{:S(2)}, u32[]{:S(2)}) collective-permute-start(f32[32,8,512]{2,1,0:T(8,128)S(1)} %get-tuple-element.47), channel_id=1, source_target_pairs={{0,4},{1,5},{2,6},{3,7},{4,8},{5,9},{6,10},{7,11},{8,12},{9,13},{1... | collective-permute-start | bytes 1572872 | tf_op jit(solution)/shard_map/ppermute | solution.py:30
  93.9 26.7 %collective-permute-start.15 = (f32[64,512]{1,0:T(8,128)S(1)}, f32[64,512]{1,0:T(8,128)S(1)}, u32[]{:S(2)}, u32[]{:S(2)}) collective-permute-start(f32[64,512]{1,0:T(8,128)S(1)} %get-tuple-element.49), channel_id=1, source_target_pairs={{0,1},{1,2},{2,3},{4,5},{5,6},{6,7},{8,9},{9,10},{10,11},{12,13},{... | collective-permute-start | bytes 393224 | tf_op jit(solution)/shard_map/ppermute | solution.py:30
  101.3 19.2 %collective-permute-start.14 = (f32[64,512]{1,0:T(8,128)S(1)}, f32[64,512]{1,0:T(8,128)S(1)}, u32[]{:S(2)}, u32[]{:S(2)}) collective-permute-start(f32[64,512]{1,0:T(8,128)S(1)} %get-tuple-element.48.mine), channel_id=1, source_target_pairs={{1,0},{2,1},{3,2},{5,4},{6,5},{7,6},{9,8},{10,9},{11,10},{13,12},{... | collective-permute-start | bytes 393224 | tf_op jit(solution)/shard_map/ppermute | solution.py:30
  102.6 12.5 %collective-permute-start.16 = (f32[16,512]{1,0:T(8,128)S(1)}, f32[16,512]{1,0:T(8,128)S(1)}, u32[]{:S(2)}, u32[]{:S(2)}) collective-permute-start(f32[16,512]{1,0:T(8,128)S(1)} %get-tuple-element.50), channel_id=1, source_target_pairs={{1,4},{2,5},{3,6},{5,8},{6,9},{7,10},{9,12},{10,13},{11,14},{13,16... | collective-permute-start | bytes 98312 | tf_op jit(solution)/shard_map/ppermute | solution.py:30
  115.1 5.4 %collective-permute-start.17 = (f32[16,512]{1,0:T(8,128)S(1)}, f32[16,512]{1,0:T(8,128)S(1)}, u32[]{:S(2)}, u32[]{:S(2)}) collective-permute-start(f32[16,512]{1,0:T(8,128)S(1)} %get-tuple-element.51), channel_id=1, source_target_pairs={{0,125},{1,126},{2,127},{4,1},{5,2},{6,3},{8,5},{9,6},{10,7},{12,9... | collective-permute-start | bytes 98312 | tf_op jit(solution)/shard_map/ppermute | solution.py:30
  120.6 1.4 %copy-start.3 = (f32[16,3,2,8,512]{4,3,2,1,0:T(8,128)S(1)}, f32[16,3,2,8,512]{4,3,2,1,0:T(8,128)}, u32[]{:S(2)}) copy-start(f32[16,3,2,8,512]{4,3,2,1,0:T(8,128)} %get-tuple-element.25.a_ref) | copy-start | bytes 4718596
  (4 other events, 3.2 us)

commit v2 on v1

v2 whole, which is shorter than its diff:
```python
import functools

import jax
import jax.numpy as jnp
from jax import lax
from jax.experimental import pallas as pl
from jax.experimental.pallas import tpu as pltpu
from jax.sharding import PartitionSpec as P

mass_term = 1.0
cheb_centre = 8.5
cheb_halfwidth = 7.5
cheb_sigma = cheb_centre / cheb_halfwidth
rho_first = 1.0 / cheb_sigma
rho_second = 1.0 / (2.0 * cheb_sigma - rho_first)

mix_second = rho_second * rho_first
step_second = 2.0 * rho_second / cheb_halfwidth

VMEM = pl.BlockSpec(memory_space=pltpu.VMEM)
SMEM = pl.BlockSpec(memory_space=pltpu.SMEM)
HBM = pl.BlockSpec(memory_space=pltpu.HBM)
MIB = 1024 * 1024
LIMIT = 16 * MIB
LIMIT_FIRST = 63 * MIB


def moved(value, shift_az, shift_ax):
    count_az, count_ax = lax.axis_size("az"), lax.axis_size("ax")
    pairs = [
        (a * count_ax + q, (a + shift_az) % count_az * count_ax + q + shift_ax)
        for a in range(count_az)
        for q in range(count_ax)
        if 0 <= q + shift_ax < count_ax
    ]
    return lax.ppermute(value, ("az", "ax"), pairs)


def lanes(shape):
    return lax.broadcasted_iota(jnp.int32, shape, 1)


def rows(shape):
    return lax.broadcasted_iota(jnp.int32, shape, 0)


def radial_next(v):
    tile = 128
    rolled = [pltpu.roll(v[:, at : at + tile], tile - 1, 1) for at in range(0, v.shape[1], tile)]
    last = lanes(rolled[0].shape) == tile - 1
    rolled.append(jnp.zeros_like(rolled[0]))
    return jnp.concatenate(
        [jnp.where(last, later, part) for part, later in zip(rolled, rolled[1:])], axis=1
    )


def radial_prev(v):
    tile = 128
    rolled = [pltpu.roll(v[:, at : at + tile], 1, 1) for at in range(0, v.shape[1], tile)]
    first = lanes(rolled[0].shape) == 0
    rolled.insert(0, jnp.zeros_like(rolled[0]))
    return jnp.concatenate(
        [jnp.where(first, sooner, part) for sooner, part in zip(rolled, rolled[1:])], axis=1
    )


def axial_next(v, row):
    n = v.shape[0]
    return jnp.where(rows(v.shape) == n - 1, row, pltpu.roll(v, n - 1, 0))


def axial_prev(v, row):
    return jnp.where(rows(v.shape) == 0, row, pltpu.roll(v, 1, 0))


def block(k, height):
    return pl.ds(pl.multiple_of(k * height, height), height)


def pack_az(d, height, a, minus, plus):
    minus[block(2 * d, height)] = a[1][0]
    minus[block(2 * d + 1, height)] = a[2][0]
    plus[block(2 * d, height)] = radial_next(a[0][1]) - a[0][1] + a[2][1]
    plus[block(2 * d + 1, height)] = a[0][1] - axial_next(a[0][1], 0.0) - a[1][1]


def pack_ax(d, devs, a, ax_minus, ax_plus):
    top = a[0][0].shape[0] - 1
    for i in range(2):
        ax_minus[pl.ds(i * devs + d, 1)] = a[0][i][0:1]
        ax_minus[pl.ds((2 + i) * devs + d, 1)] = a[2][i][0:1]
        end = a[1][i][top:]
        ax_plus[pl.ds(i * devs + d, 1)] = end - radial_next(end) - a[2][i][top:]
    ax_plus[pl.ds(2 * devs + d, 1)] = a[1][1][top:] - a[1][0][top:] + a[0][0][top:]
    ax_plus[pl.ds(3 * devs + d, 1)] = a[0][1][top:] - a[1][1][top:]


def edge_kernel(
    per, a_hbm, reluct_hbm, lam_hbm, mag_hbm, reg_hbm, slots_hbm,
    ax_minus, ax_plus, nu_ref, code_ref, offset_ref,
    a_ref, lam_ref, mag_ref, reg_ref, slots_ref, sems,
):
    devs = a_ref.shape[0]
    top = a_ref.shape[3] - 1
    parts = 2
    some = devs // parts
    copies = [
        pltpu.make_async_copy(reluct_hbm, nu_ref, sems.at[0]),
        pltpu.make_async_copy(lam_hbm, lam_ref, sems.at[1]),
        pltpu.make_async_copy(mag_hbm, mag_ref, sems.at[2]),
        pltpu.make_async_copy(reg_hbm, reg_ref, sems.at[3]),
        pltpu.make_async_copy(slots_hbm, slots_ref, sems.at[4]),
    ]
    for part in range(parts):
        at = pl.ds(part * some, some)
        copies.append(pltpu.make_async_copy(a_hbm.at[at], a_ref.at[at], sems.at[5 + part]))
    for copy in copies:
        copy.start()
    for copy in copies[:5]:
        copy.wait()

    base = lax.axis_index("az") * per
    slots = slots_ref[...]
    count = slots.shape[1]
    slots = pltpu.roll(slots, lax.rem(2 * count - base + per, count), 1)
    row = lax.div(slots, jnp.int32(per))
    offset_ref[...] = row * (3 * devs * per) + (slots - row * per)
    for i in range(2):
        nu_ref[1, i] = nu_ref[1, i] * (1.0 + 3.0 * lam_ref[i].astype(jnp.float32))
        code_ref[i] = jnp.where(mag_ref[i] == 1, reg_ref[i] - base + 1, 0).astype(jnp.float32)
    for i in range(2):
        at = 5 * devs + i
        ax_plus[pl.ds(at, 1)] = nu_ref[0, i, top:]
        ax_plus[pl.ds(at + 2, 1)] = nu_ref[2, i, top:]
        ax_plus[pl.ds(at + 4, 1)] = code_ref[i, top:]
        ax_plus[pl.ds(at + 6, 1)] = jnp.zeros_like(code_ref[i, top:])

    for part in range(parts):
        copies[5 + part].wait()

        @pl.loop(part * some, (part + 1) * some)
        def _(d):
            a = [[a_ref[d, c, i] for i in range(2)] for c in range(3)]
            pack_ax(d, devs, a, ax_minus, ax_plus)
            ax_plus[pl.ds(4 * devs + d, 1)] = a[1][0][top:]


def plane_kernel(a_ref, nu_ref, code_ref, ax_ahead, ax_behind, minus, plus):
    devs, height = a_ref.shape[0], a_ref.shape[3]
    end = 2 * devs * height
    minus[pl.ds(end, devs)] = ax_behind[pl.ds(4 * devs, devs)]
    plus[pl.ds(end, devs)] = ax_ahead[pl.ds(devs, devs)]
    plus[pl.ds(end + devs, height)] = nu_ref[1, 1]
    plus[pl.ds(end + devs + height, height)] = nu_ref[2, 1]
    plus[pl.ds(end + devs + 2 * height, height)] = code_ref[1]

    @pl.loop(0, devs)
    def _(d):
        a = [[a_ref[d, c, i] for i in range(2)] for c in range(3)]
        pack_az(d, height, a, minus, plus)


def picked(code, values):
    out = jnp.zeros_like(code)
    for k, value in enumerate(values):
        out = jnp.where(code == k + 1.0, value, out)
    return out


def advanced(stage, value, start, curl):
    if stage == 0:
        return value * (1.0 - mass_term / cheb_centre) - curl * (1.0 / cheb_centre)
    if stage == 1:
        return (
            value * (1.0 + mix_second - mass_term * step_second) - start * mix_second - curl * step_second
        )
    return -curl - mass_term * value


def step_kernel(stage, per, *refs):
    it = iter(refs)
    a_ref, nu_ref, nu_az_ref, nu_ax_ref = next(it), next(it), next(it), next(it)
    ahead, behind, ax_ahead, ax_behind, mine = [next(it) for _ in range(5)]
    if stage == 0:
        code_ref, offset_ref, table_ref = next(it), next(it), next(it)
    else:
        src_ref, src_az_ref, src_ax_ref, track0 = [next(it) for _ in range(4)]
    track = track0 if stage == 1 else None
    if stage == 1:
        start_ref = next(it)
    if stage == 2:
        track = next(it)
    out_ref = next(it)
    if stage < 2:
        minus, plus, ax_minus, ax_plus, next_track = [next(it) for _ in range(5)]
    if stage == 0:
        src_ref, src_az_ref, src_ax_ref = next(it), next(it), next(it)
    edge, corner = next(it), next(it)
    devs, height = a_ref.shape[0], a_ref.shape[3]
    top = height - 1
    end = 2 * devs * height
    nu_az = end + devs
    nu_ax = 5 * devs
    every = pl.ds(0, devs)
    after = pl.ds(devs, devs)

    if stage == 0:
        corner[every] = behind[pl.ds(end, devs)]
        corner[after] = ahead[pl.ds(end, devs)]
    else:
        curl = ax_ahead[pl.ds(4 * devs, devs)] - track[pl.ds(2 * devs, devs)]
        value = advanced(stage - 1, track[every], track0[every], curl)
        open_end = lax.axis_index("ax") == lax.axis_size("ax") - 1
        corner[every] = jnp.where(open_end, 0.0, value)
        curl = ahead[pl.ds(end, devs)] + track[pl.ds(3 * devs, devs)]
        corner[after] = advanced(stage - 1, track[after], track0[after], curl)

    def values(d, c, first):
        return [
            table_ref[offset_ref[d, first + k] + (c * devs + d) * per] for k in range(per)
        ]

    if stage == 0:

        @pl.loop(0, devs)
        def _(d):
            for c in (0, 2):
                own = values(d, c, per)
                for i in range(2):
                    src_ax_ref[pl.ds((c + i) * devs + d, 1)] = nu_ax_ref[pl.ds(nu_ax + c + i, 1)] * picked(
                        nu_ax_ref[pl.ds(nu_ax + 4 + i, 1)], own
                    )

    for at, own, sign in ((0, 2, 1.0), (1, 3, 1.0), (2, 0, -1.0), (3, 1, -1.0)):
        part = pl.ds(at * devs, devs)
        flux = ax_behind[part] + sign * mine[pl.ds(own * devs, devs)]
        if at == 3:
            flux = flux + corner[after]
        edge[part] = nu_ax_ref[pl.ds(nu_ax + at, 1)] * flux - src_ax_ref[part]
    if stage < 2:
        before = edge[every]
        minus[pl.ds(end, devs)] = before - radial_prev(before) - edge[pl.ds(2 * devs, devs)]
        next_track[pl.ds(0, 2 * devs)] = corner[...]
        next_track[pl.ds(3 * devs, devs)] = edge[pl.ds(3 * devs, devs)]

    @pl.loop(0, devs)
    def _(d):
        a = [[a_ref[d, c, i] for i in range(2)] for c in range(3)]
        up = [None, ahead[block(2 * d, height)], ahead[block(2 * d + 1, height)]]
        inten = [[None, None], [None, None], [None, None]]
        own = [values(d, c, per) for c in range(3)] if stage == 0 else None
        for i in range(2):
            next1 = a[1][1] if i == 0 else up[1]
            next2 = a[2][1] if i == 0 else up[2]
            row0 = ax_ahead[pl.ds(i * devs + d, 1)]
            row2 = ax_ahead[pl.ds((2 + i) * devs + d, 1)]
            flux = (
                (axial_next(a[2][i], row2) - a[2][i]) - (radial_next(a[1][i]) - a[1][i]),
                (radial_next(a[0][i]) - a[0][i]) - (next2 - a[2][i]),
                (next1 - a[1][i]) - (axial_next(a[0][i], row0) - a[0][i]),
            )
            for c in range(3):
                if stage == 0:
                    src = nu_ref[c, i] * picked(code_ref[i], own[c])
                    src_ref[d, c, i] = src
                else:
                    src = src_ref[d, c, i]
                inten[c][i] = nu_ref[c, i] * flux[c] - src
        back_src = [None, None]
        for c in range(1, 3):
            if stage == 0:
                src = nu_az_ref[block(2 * devs + 1 + c, height)] * picked(
                    nu_az_ref[pl.ds(nu_az + 2 * height, height)], values(d, c, 0)
                )
                src_az_ref[2 * d + c - 1] = src
            else:
                src = src_az_ref[2 * d + c - 1]
            back_src[c - 1] = src
        beyond = jnp.where(rows(a[1][0].shape) == top, corner[pl.ds(d, 1)], 0.0)
        back1 = nu_az_ref[pl.ds(nu_az, height)] * (behind[block(2 * d, height)] - a[2][0]) - back_src[0]
        back2 = (
            nu_az_ref[pl.ds(nu_az + height, height)]
            * (behind[block(2 * d + 1, height)] + a[1][0] - beyond)
            - back_src[1]
        )
        new = [[None, None], [None, None], [None, None]]
        for i in range(2):
            prev1 = back1 if i == 0 else inten[1][0]
            prev2 = back2 if i == 0 else inten[2][0]
            row0 = edge[pl.ds(i * devs + d, 1)]
            row2 = edge[pl.ds((2 + i) * devs + d, 1)]
            i0, i1, i2 = inten[0][i], inten[1][i], inten[2][i]
            curl = (
                (i2 - axial_prev(i2, row2)) - (i1 - radial_prev(i1)),
                (i0 - radial_prev(i0)) - (i2 - prev2),
                (i1 - prev1) - (i0 - axial_prev(i0, row0)),
            )
            for c in range(3):
                start = start_ref[d, c, i] if stage == 1 else None
                value = advanced(stage, a[c][i], start, curl[c])
                out_ref[d, c, i] = value
                new[c][i] = value
        if stage < 2:
            first1, first2 = back1[0:1], back2[0:1]
            ax_minus[pl.ds(4 * devs + d, 1)] = first2 - (first1 - radial_prev(first1))
            next_track[pl.ds(2 * devs + d, 1)] = back2[top:]
            pack_az(d, height, new, minus, plus)
            pack_ax(d, devs, new, ax_minus, ax_plus)


def f32(*shape):
    return jax.ShapeDtypeStruct(shape, jnp.float32)


def shards(start_field, reluctivity, lamination, magnets, region_ids, pieces, slot_map):
    devs, comps, cells_az, cells_ax, radial = start_field.shape
    count_az = lax.axis_size("az")
    per = pieces.shape[2]
    whole = 2 * devs * cells_ax

    field_like = f32(*start_field.shape)
    edges = [
        f32(4 * devs, radial),
        f32(5 * devs + 8, radial),
        f32(*reluctivity.shape),
        f32(*lamination.shape),
        jax.ShapeDtypeStruct(slot_map.shape, jnp.int32),
    ]
    ax_minus, ax_plus, nu, code, offset = pl.pallas_call(
        functools.partial(edge_kernel, per),
        out_shape=edges,
        in_specs=[HBM] * 6,
        out_specs=[VMEM] * len(edges),
        scratch_shapes=[pltpu.VMEM(start_field.shape, jnp.float32)]
        + [pltpu.VMEM(lamination.shape, jnp.int32)] * 3
        + [pltpu.VMEM(slot_map.shape, jnp.int32), pltpu.SemaphoreType.DMA((7,))],
        compiler_params=pltpu.CompilerParams(vmem_limit_bytes=LIMIT_FIRST),
    )(start_field, reluctivity, lamination, magnets, region_ids, slot_map)
    ax_ahead, ax_behind = moved(ax_minus, 0, -1), moved(ax_plus, 0, 1)
    planes = [f32(whole + devs, radial), f32(whole + devs + 3 * cells_ax, radial)]
    minus, plus = pl.pallas_call(
        plane_kernel,
        out_shape=planes,
        in_specs=[VMEM] * 5,
        out_specs=[VMEM] * 2,
        compiler_params=pltpu.CompilerParams(vmem_limit_bytes=LIMIT),
    )(start_field, nu, code, ax_ahead, ax_behind)
    halos = (moved(minus, -1, 0), moved(plus, 1, 0), ax_ahead, ax_behind, ax_minus)
    flat = pieces.reshape(1, comps * devs * per)
    table = lax.all_to_all(
        jnp.broadcast_to(flat, (count_az, comps * devs * per)), "az", 0, 0, tiled=True
    ).reshape(-1)
    nu_az, nu_ax = halos[1], halos[3]

    def exchange(minus, plus, ax_minus, ax_plus):
        ahead, behind = moved(minus, -1, 0), moved(plus, 1, 0)
        return ahead, behind, moved(ax_minus, 0, -1), moved(ax_plus, 0, 1), ax_minus

    def step(stage, field, halos, more, more_specs):
        outs = [field_like]
        if stage < 2:
            outs += [
                f32(whole + devs, radial),
                f32(whole, radial),
                f32(5 * devs, radial),
                f32(4 * devs, radial),
                f32(4 * devs, radial),
            ]
        if stage == 0:
            outs += [field_like, f32(2 * devs, cells_ax, radial), f32(4 * devs, radial)]
        return pl.pallas_call(
            functools.partial(step_kernel, stage, per),
            out_shape=outs,
            in_specs=[VMEM] * 9 + more_specs,
            out_specs=[VMEM] * len(outs),
            scratch_shapes=[
                pltpu.VMEM((4 * devs, radial), jnp.float32),
                pltpu.VMEM((2 * devs, radial), jnp.float32),
            ],
            compiler_params=pltpu.CompilerParams(vmem_limit_bytes=LIMIT),
        )(field, nu, nu_az, nu_ax, *halos, *more)

    middle, *rest = step(0, start_field, halos, [code, offset, table], [VMEM, SMEM, SMEM])
    packed, track0, src = rest[:4], rest[4], rest[5:]
    final, *rest = step(1, middle, exchange(*packed), [*src, track0, start_field], [VMEM] * 5)
    packed, track1 = rest[:4], rest[4]
    (residual,) = step(2, final, exchange(*packed), [*src, track0, track1], [VMEM] * 5)
    return final, residual


def solution(mesh):
    placed = (
        P(None, None, "az", "ax", None),
        P(None, "az", "ax", None),
        P("az", "ax", None),
        P("az", "ax", None),
        P("az", "ax", None),
        P(None, None, "az"),
        P(),
    )
    return jax.shard_map(
        shards,
        mesh=mesh,
        in_specs=placed,
        out_specs=(P(None, None, "az", "ax", None), P(None, None, "az", "ax", None)),
        check_vma=False,
    )
```

time: 129 us -> 101 us (0.78)
  starting transfers between devices: 48.8 us -> 28.9 us
  Pallas kernels: 25.4 us -> 19.9 us
  local copies, waits for them, and re-layouts: 7.4 us -> 4.79 us
    ppermute x18 -> x12, starting transfers between devices: 48.8 us -> 28.9 us  [moved(): return lax.ppermute(value, ('az', 'ax'), pairs)]
    pallas_call x5, Pallas kernels: 25.4 us -> 19.9 us  [the longest x3 14.3 us: step(): pl.pallas_call(functools.partial(step_kernel, stage, per), out_shape=outs...]
    unnamed x22 -> x21, local copies, waits for them, and re-layouts: 7.28 us -> 4.58 us
    ppermute x18 -> x12, waiting for transfers between devices: 31.2 us -> 31.3 us  [moved(): return lax.ppermute(value, ('az', 'ax'), pairs)]
  transfers between devices with their start and end apart: 18 -> 12, of which waited for: 4 -> 5; matrix products, arithmetic and copies ran while one was open for 0% -> 0% of each run, Pallas kernels for 3% -> 0%
where the time goes in v2:
time: 101 us; the launch traced here: 99.5 us
  waiting for transfers between devices  31.3 us (31%)
  starting transfers between devices  28.9 us (29%)
  Pallas kernels  19.9 us (20%)
  blocking collectives  13.8 us (14%)
  local copies, waits for them, and re-layouts  4.79 us (5%)
    ppermute x12, waiting for transfers between devices, moved(): return lax.ppermute(value, ('az', 'ax'), pairs)  31.3 us
    ppermute x12, starting transfers between devices, moved(): return lax.ppermute(value, ('az', 'ax'), pairs)  28.9 us
    pallas_call x3, Pallas kernels, step(): pl.pallas_call(functools.partial(step_kernel, stage, per), out_shape=outs...  14.3 us
    all_to_all x1, blocking collectives, shards(): lax.all_to_all(jnp.broadcast_to(flat, (count_az, comps * devs * per)), 'a...  13.8 us
    unnamed x21, local copies, waits for them, and re-layouts  4.58 us
    pallas_call x1, Pallas kernels, shards(): pl.pallas_call(functools.partial(edge_kernel, per), out_shape=edges, in_s...  3.44 us
    pallas_call x1, Pallas kernels, shards(): pl.pallas_call(plane_kernel, out_shape=planes, in_specs=[VMEM] * 5, out_s...  2.16 us
  transfers between devices with their start and end apart: 12, of which 5 were waited for; matrix products, arithmetic and copies ran while one was open for 0% of the time, Pallas kernels for 0%

profile of v2, /device:TPU:0, one launch (start us, length us, event | category | flops | bytes accessed | tf_op | source)
XLA Modules:
  0.0 99.5 jit_solution(6028396638480565668)
XLA Ops:
  0.6 3.4 %shard_map.86 = (f32[64,512]{1,0:T(8,128)}, f32[88,512]{1,0:T(8,128)}, f32[3,2,8,512]{3,2,1,0:T(8,128)}, f32[2,8,512]{2,1,0:T(8,128)}, s32[16,128]{1,0:T(8,128)}) custom-call(f32[16,3,2,8,512]{4,3,2,1,0:T(8,128)} %refs_13_.1, f32[3,2,8,512]{3,2,1,0:T(8,128)} %reluct_hbm.1, s32[2,8,512]{2,1,0:T(8,128)} %lam_hbm.1, s32[2,8,512]{2,1,0:T(8,128)} %mag_hbm.1, ...), custom_call_target="tpu_custom_call" | custom-call | tf_op jit(solution)/shard_map/pallas_call | solution.py:329
  4.1 1.3 %collective-permute-start.1 = (f32[88,512]{1,0:T(8,128)}, f32[88,512]{1,0:T(8,128)S(1)}, u32[]{:S(2)}, u32[]{:S(2)}) collective-permute-start(f32[88,512]{1,0:T(8,128)} %get-tuple-element.27), channel_id=1, source_target_pairs={{0,1},{1,2},{2,3},{4,5},{5,6},{6,7},{8,9},{9,10},{10,11},{12,13},{... | collective-permute-start | bytes 540680 | tf_op jit(solution)/shard_map/ppermute | solution.py:36
  5.4 1.3 %collective-permute-start = (f32[64,512]{1,0:T(8,128)}, f32[64,512]{1,0:T(8,128)S(1)}, u32[]{:S(2)}, u32[]{:S(2)}) collective-permute-start(f32[64,512]{1,0:T(8,128)} %get-tuple-element.26.refs_8_), channel_id=1, source_target_pairs={{1,0},{2,1},{3,2},{5,4},{6,5},{7,6},{9,8},{10,9},{11,10},{13,12},{... | collective-permute-start | bytes 393224 | tf_op jit(solution)/shard_map/ppermute | solution.py:36
  6.7 4.0 %collective-permute-done.ax_ahead.refs_6_ = f32[64,512]{1,0:T(8,128)S(1)} collective-permute-done((f32[64,512]{1,0:T(8,128)}, f32[64,512]{1,0:T(8,128)S(1)}, u32[]{:S(2)}, u32[]{:S(2)}) %collective-permute-start) | collective-permute-done | bytes 131104 | tf_op jit(solution)/shard_map/ppermute | solution.py:36
  10.7 1.4 %copy-done = f32[16,3,2,8,512]{4,3,2,1,0:T(8,128)S(1)} copy-done((f32[16,3,2,8,512]{4,3,2,1,0:T(8,128)S(1)}, f32[16,3,2,8,512]{4,3,2,1,0:T(8,128)}, u32[]{:S(2)}) %copy-start) | copy-done | bytes 1572888
  12.1 0.9 copy-done.2
  13.7 2.2 %shard_map.87 = (f32[272,512]{1,0:T(8,128)}, f32[296,512]{1,0:T(8,128)}) custom-call(f32[16,3,2,8,512]{4,3,2,1,0:T(8,128)S(1)} %copy-done, f32[3,2,8,512]{3,2,1,0:T(8,128)S(1)} %copy-done.2, f32[2,8,512]{2,1,0:T(8,128)S(1)} %copy-done.5, f32[64,512]{1,0:T(8,128)S(1)} %collective-permute-done.ax_ahead.refs_6_, ...), custom_call_target="tpu_custom_call" | custom-call | tf_op jit(solution)/shard_map/pallas_call | solution.py:341
  15.9 1.9 %collective-permute-start.2 = (f32[296,512]{1,0:T(8,128)}, f32[296,512]{1,0:T(8,128)S(1)}, u32[]{:S(2)}, u32[]{:S(2)}) collective-permute-start(f32[296,512]{1,0:T(8,128)} %get-tuple-element.28), channel_id=1, source_target_pairs={{0,4},{1,5},{2,6},{3,7},{4,8},{5,9},{6,10},{7,11},{8,12},{9,13},{1... | collective-permute-start | bytes 1818632 | tf_op jit(solution)/shard_map/ppermute | solution.py:36
  17.8 6.7 %collective-permute-start.3 = (f32[272,512]{1,0:T(8,128)}, f32[272,512]{1,0:T(8,128)S(1)}, u32[]{:S(2)}, u32[]{:S(2)}) collective-permute-start(f32[272,512]{1,0:T(8,128)} %get-tuple-element.29), channel_id=1, source_target_pairs={{0,124},{1,125},{2,126},{3,127},{4,0},{5,1},{6,2},{7,3},{8,4},{9,5... | collective-permute-start | bytes 1671176 | tf_op jit(solution)/shard_map/ppermute | solution.py:36
  24.8 13.8 %all_to_all.6 = f32[32,1,192]{2,1,0:T(1,128)S(1)} all-to-all(f32[32,1,192]{2,1,0:T(1,128)S(1)} %broadcast_in_dim.8), channel_id=1, replica_groups=mesh['az'=32,'ax'=4] {'az'}, dimensions={0} | all-to-all | bytes 49152 | tf_op jit(solution)/shard_map/all_to_all | solution.py:350
  38.8 5.3 %shard_map.88 = (f32[16,3,2,8,512]{4,3,2,1,0:T(8,128)S(1)}, f32[272,512]{1,0:T(8,128)S(1)}, f32[256,512]{1,0:T(8,128)S(1)}, f32[80,512]{1,0:T(8,128)S(1)}, f32[6...) custom-call(f32[16,3,2,8,512]{4,3,2,1,0:T(8,128)S(1)} %copy-done.1, ...), custom_call_target="tpu_custom_call" | custom-call | tf_op jit(solution)/shard_map/pallas_call | solution.py:371
  44.1 5.3 %collective-permute-start.4 = (f32[272,512]{1,0:T(8,128)S(1)}, f32[272,512]{1,0:T(8,128)S(1)}, u32[]{:S(2)}, u32[]{:S(2)}) collective-permute-start(f32[272,512]{1,0:T(8,128)S(1)} %get-tuple-element.32), channel_id=1, source_target_pairs={{0,124},{1,125},{2,126},{3,127},{4,0},{5,1},{6,2},{7,3},{8,4},{9,5... | collective-permute-start | bytes 1671176 | tf_op jit(solution)/shard_map/ppermute | solution.py:36
  49.4 1.3 %collective-permute-start.6 = (f32[80,512]{1,0:T(8,128)S(1)}, f32[80,512]{1,0:T(8,128)S(1)}, u32[]{:S(2)}, u32[]{:S(2)}) collective-permute-start(f32[80,512]{1,0:T(8,128)S(1)} %get-tuple-element.34.refs_8_), channel_id=1, source_target_pairs={{1,0},{2,1},{3,2},{5,4},{6,5},{7,6},{9,8},{10,9},{11,10},{13,12},{... | collective-permute-start | bytes 491528 | tf_op jit(solution)/shard_map/ppermute | solution.py:36
  50.7 4.7 %collective-permute-start.7 = (f32[64,512]{1,0:T(8,128)S(1)}, f32[64,512]{1,0:T(8,128)S(1)}, u32[]{:S(2)}, u32[]{:S(2)}) collective-permute-start(f32[64,512]{1,0:T(8,128)S(1)} %get-tuple-element.35), channel_id=1, source_target_pairs={{0,1},{1,2},{2,3},{4,5},{5,6},{6,7},{8,9},{9,10},{10,11},{12,13},{... | collective-permute-start | bytes 393224 | tf_op jit(solution)/shard_map/ppermute | solution.py:36
  55.4 1.0 collective-permute-done.7.refs_7_
  56.4 12.4 %collective-permute-done.5.refs_5_ = f32[256,512]{1,0:T(8,128)S(1)} collective-permute-done((f32[256,512]{1,0:T(8,128)S(1)}, f32[256,512]{1,0:T(8,128)S(1)}, u32[]{:S(2)}, u32[]{:S(2)}) %collective-permute-start.5) | collective-permute-done | bytes 524320 | tf_op jit(solution)/shard_map/ppermute | solution.py:36
  68.8 5.1 %shard_map.89 = (f32[16,3,2,8,512]{4,3,2,1,0:T(8,128)}, f32[272,512]{1,0:T(8,128)S(1)}, f32[256,512]{1,0:T(8,128)S(1)}, f32[80,512]{1,0:T(8,128)S(1)}, f32[64,512]{1,0:T(8,128)S(1)}, /*index=5*/f32[64,512]{1,0:T(8,128)S(1)}) custom-call(f32[16,3,2,8,512]{4,3,2,1,0:T(8,128)S(1)} %get-tuple-element.31.refs_0_, f32[3,2,8,512]{3,2,1,0:T(8,128)S(1)} %copy-done.3, ...), custom_call_target="tpu_custom_call" | custom-call | tf_op jit(solution)/shard_map/pallas_call | solution.py:371
  74.3 1.6 %collective-permute-start.9 = (f32[256,512]{1,0:T(8,128)S(1)}, f32[256,512]{1,0:T(8,128)S(1)}, u32[]{:S(2)}, u32[]{:S(2)}) collective-permute-start(f32[256,512]{1,0:T(8,128)S(1)} %get-tuple-element.42), channel_id=1, source_target_pairs={{0,4},{1,5},{2,6},{3,7},{4,8},{5,9},{6,10},{7,11},{8,12},{9,13},{1... | collective-permute-start | bytes 1572872 | tf_op jit(solution)/shard_map/ppermute | solution.py:36
  75.9 1.3 %collective-permute-start.10 = (f32[80,512]{1,0:T(8,128)S(1)}, f32[80,512]{1,0:T(8,128)S(1)}, u32[]{:S(2)}, u32[]{:S(2)}) collective-permute-start(f32[80,512]{1,0:T(8,128)S(1)} %get-tuple-element.43.refs_8_), channel_id=1, source_target_pairs={{1,0},{2,1},{3,2},{5,4},{6,5},{7,6},{9,8},{10,9},{11,10},{13,12},{... | collective-permute-start | bytes 491528 | tf_op jit(solution)/shard_map/ppermute | solution.py:36
  77.2 3.0 %collective-permute-start.11 = (f32[64,512]{1,0:T(8,128)S(1)}, f32[64,512]{1,0:T(8,128)S(1)}, u32[]{:S(2)}, u32[]{:S(2)}) collective-permute-start(f32[64,512]{1,0:T(8,128)S(1)} %get-tuple-element.44), channel_id=1, source_target_pairs={{0,1},{1,2},{2,3},{4,5},{5,6},{6,7},{8,9},{9,10},{10,11},{12,13},{... | collective-permute-start | bytes 393224 | tf_op jit(solution)/shard_map/ppermute | solution.py:36
  80.2 1.0 collective-permute-done.11.refs_7_
  81.2 13.0 %collective-permute-done.9.refs_5_ = f32[256,512]{1,0:T(8,128)S(1)} collective-permute-done((f32[256,512]{1,0:T(8,128)S(1)}, f32[256,512]{1,0:T(8,128)S(1)}, u32[]{:S(2)}, u32[]{:S(2)}) %collective-permute-start.9) | collective-permute-done | bytes 524320 | tf_op jit(solution)/shard_map/ppermute | solution.py:36
  94.2 1.4 %copy-done.4 = f32[16,3,2,8,512]{4,3,2,1,0:T(8,128)S(1)} copy-done((f32[16,3,2,8,512]{4,3,2,1,0:T(8,128)S(1)}, f32[16,3,2,8,512]{4,3,2,1,0:T(8,128)}, u32[]{:S(2)}) %copy-start.4) | copy-done | bytes 1572888
  95.6 3.9 %shard_map.90 = f32[16,3,2,8,512]{4,3,2,1,0:T(8,128)} custom-call(f32[16,3,2,8,512]{4,3,2,1,0:T(8,128)S(1)} %copy-done.4, f32[3,2,8,512]{3,2,1,0:T(8,128)S(1)} %copy-done.3, f32[296,512]{1,0:T(8,128)S(1)} %collective-permute-done.2.refs_2_.refs_5_, f32[88,512]{1,0:T(8,128)S(1)} %collective-permute-done.1.ax_behind.refs_3_.refs_7_, ...), custom_call_target="tpu_custom_call" | custom-call | tf_op jit(solution)/shard_map/pallas_call | solution.py:371
  (31 shorter events, 1.6 us)
Async XLA Ops:
  0.6 23.9 %copy-start.9 = (f32[3,16,4]{1,2,0:T(4,128)S(1)}, f32[3,16,4]{1,2,0:T(4,128)}, u32[]{:S(2)}) copy-start(f32[3,16,4]{1,2,0:T(4,128)} %param.12) | copy-start | bytes 2308
  4.1 6.6 %collective-permute-start.1 = (f32[88,512]{1,0:T(8,128)}, f32[88,512]{1,0:T(8,128)S(1)}, u32[]{:S(2)}, u32[]{:S(2)}) collective-permute-start(f32[88,512]{1,0:T(8,128)} %get-tuple-element.27), channel_id=1, source_target_pairs={{0,1},{1,2},{2,3},{4,5},{5,6},{6,7},{8,9},{9,10},{10,11},{12,13},{... | collective-permute-start | bytes 540680 | tf_op jit(solution)/shard_map/ppermute | solution.py:36
  5.4 5.3 %collective-permute-start = (f32[64,512]{1,0:T(8,128)}, f32[64,512]{1,0:T(8,128)S(1)}, u32[]{:S(2)}, u32[]{:S(2)}) collective-permute-start(f32[64,512]{1,0:T(8,128)} %get-tuple-element.26.refs_8_), channel_id=1, source_target_pairs={{1,0},{2,1},{3,2},{5,4},{6,5},{7,6},{9,8},{10,9},{11,10},{13,12},{... | collective-permute-start | bytes 393224 | tf_op jit(solution)/shard_map/ppermute | solution.py:36
  10.7 1.4 %copy-start = (f32[16,3,2,8,512]{4,3,2,1,0:T(8,128)S(1)}, f32[16,3,2,8,512]{4,3,2,1,0:T(8,128)}, u32[]{:S(2)}) copy-start(f32[16,3,2,8,512]{4,3,2,1,0:T(8,128)} %refs_13_.1) | copy-start | bytes 4718596
  12.1 0.9 copy-start.2
  13.0 0.8 copy-start.5
  13.7 25.0 %copy-start.1 = (f32[16,3,2,8,512]{4,3,2,1,0:T(8,128)S(1)}, f32[16,3,2,8,512]{4,3,2,1,0:T(8,128)}, u32[]{:S(2)}) copy-start(f32[16,3,2,8,512]{4,3,2,1,0:T(8,128)} %refs_13_.1) | copy-start | bytes 4718596
  13.7 25.0 %copy-start.3 = (f32[3,2,8,512]{3,2,1,0:T(8,128)S(1)}, f32[3,2,8,512]{3,2,1,0:T(8,128)}, u32[]{:S(2)}) copy-start(f32[3,2,8,512]{3,2,1,0:T(8,128)} %get-tuple-element.24.nu_ref.refs_1_) | copy-start | bytes 294916
  13.7 25.0 %copy-start.6 = (f32[2,8,512]{2,1,0:T(8,128)S(1)}, f32[2,8,512]{2,1,0:T(8,128)}, u32[]{:S(2)}) copy-start(f32[2,8,512]{2,1,0:T(8,128)} %get-tuple-element.25.code_ref.refs_9_) | copy-start | bytes 98308
  13.7 25.0 %copy-start.7 = (f32[64,512]{1,0:T(8,128)S(1)}, f32[64,512]{1,0:T(8,128)}, u32[]{:S(2)}) copy-start(f32[64,512]{1,0:T(8,128)} %get-tuple-element.26.refs_8_) | copy-start | bytes 393220
  13.7 25.0 %copy-start.8 = (s32[16,128]{1,0:T(8,128)S(1)}, s32[16,128]{1,0:T(8,128)}, u32[]{:S(2)}) copy-start(s32[16,128]{1,0:T(8,128)} %get-tuple-element.30.refs_10_) | copy-start | bytes 24580
  15.9 22.8 %collective-permute-start.2 = (f32[296,512]{1,0:T(8,128)}, f32[296,512]{1,0:T(8,128)S(1)}, u32[]{:S(2)}, u32[]{:S(2)}) collective-permute-start(f32[296,512]{1,0:T(8,128)} %get-tuple-element.28), channel_id=1, source_target_pairs={{0,4},{1,5},{2,6},{3,7},{4,8},{5,9},{6,10},{7,11},{8,12},{9,13},{1... | collective-permute-start | bytes 1818632 | tf_op jit(solution)/shard_map/ppermute | solution.py:36
  17.8 20.9 %collective-permute-start.3 = (f32[272,512]{1,0:T(8,128)}, f32[272,512]{1,0:T(8,128)S(1)}, u32[]{:S(2)}, u32[]{:S(2)}) collective-permute-start(f32[272,512]{1,0:T(8,128)} %get-tuple-element.29), channel_id=1, source_target_pairs={{0,124},{1,125},{2,126},{3,127},{4,0},{5,1},{6,2},{7,3},{8,4},{9,5... | collective-permute-start | bytes 1671176 | tf_op jit(solution)/shard_map/ppermute | solution.py:36
  44.1 24.7 %collective-permute-start.4 = (f32[272,512]{1,0:T(8,128)S(1)}, f32[272,512]{1,0:T(8,128)S(1)}, u32[]{:S(2)}, u32[]{:S(2)}) collective-permute-start(f32[272,512]{1,0:T(8,128)S(1)} %get-tuple-element.32), channel_id=1, source_target_pairs={{0,124},{1,125},{2,126},{3,127},{4,0},{5,1},{6,2},{7,3},{8,4},{9,5... | collective-permute-start | bytes 1671176 | tf_op jit(solution)/shard_map/ppermute | solution.py:36
  49.4 19.3 %collective-permute-start.5 = (f32[256,512]{1,0:T(8,128)S(1)}, f32[256,512]{1,0:T(8,128)S(1)}, u32[]{:S(2)}, u32[]{:S(2)}) collective-permute-start(f32[256,512]{1,0:T(8,128)S(1)} %get-tuple-element.33), channel_id=1, source_target_pairs={{0,4},{1,5},{2,6},{3,7},{4,8},{5,9},{6,10},{7,11},{8,12},{9,13},{1... | collective-permute-start | bytes 1572872 | tf_op jit(solution)/shard_map/ppermute | solution.py:36
  49.4 6.9 %collective-permute-start.6 = (f32[80,512]{1,0:T(8,128)S(1)}, f32[80,512]{1,0:T(8,128)S(1)}, u32[]{:S(2)}, u32[]{:S(2)}) collective-permute-start(f32[80,512]{1,0:T(8,128)S(1)} %get-tuple-element.34.refs_8_), channel_id=1, source_target_pairs={{1,0},{2,1},{3,2},{5,4},{6,5},{7,6},{9,8},{10,9},{11,10},{13,12},{... | collective-permute-start | bytes 491528 | tf_op jit(solution)/shard_map/ppermute | solution.py:36
  50.7 5.6 %collective-permute-start.7 = (f32[64,512]{1,0:T(8,128)S(1)}, f32[64,512]{1,0:T(8,128)S(1)}, u32[]{:S(2)}, u32[]{:S(2)}) collective-permute-start(f32[64,512]{1,0:T(8,128)S(1)} %get-tuple-element.35), channel_id=1, source_target_pairs={{0,1},{1,2},{2,3},{4,5},{5,6},{6,7},{8,9},{9,10},{10,11},{12,13},{... | collective-permute-start | bytes 393224 | tf_op jit(solution)/shard_map/ppermute | solution.py:36
  73.9 20.3 %collective-permute-start.8 = (f32[272,512]{1,0:T(8,128)S(1)}, f32[272,512]{1,0:T(8,128)S(1)}, u32[]{:S(2)}, u32[]{:S(2)}) collective-permute-start(f32[272,512]{1,0:T(8,128)S(1)} %get-tuple-element.41), channel_id=1, source_target_pairs={{0,124},{1,125},{2,126},{3,127},{4,0},{5,1},{6,2},{7,3},{8,4},{9,5... | collective-permute-start | bytes 1671176 | tf_op jit(solution)/shard_map/ppermute | solution.py:36
  74.3 19.9 %collective-permute-start.9 = (f32[256,512]{1,0:T(8,128)S(1)}, f32[256,512]{1,0:T(8,128)S(1)}, u32[]{:S(2)}, u32[]{:S(2)}) collective-permute-start(f32[256,512]{1,0:T(8,128)S(1)} %get-tuple-element.42), channel_id=1, source_target_pairs={{0,4},{1,5},{2,6},{3,7},{4,8},{5,9},{6,10},{7,11},{8,12},{9,13},{1... | collective-permute-start | bytes 1572872 | tf_op jit(solution)/shard_map/ppermute | solution.py:36
  75.9 5.3 %collective-permute-start.10 = (f32[80,512]{1,0:T(8,128)S(1)}, f32[80,512]{1,0:T(8,128)S(1)}, u32[]{:S(2)}, u32[]{:S(2)}) collective-permute-start(f32[80,512]{1,0:T(8,128)S(1)} %get-tuple-element.43.refs_8_), channel_id=1, source_target_pairs={{1,0},{2,1},{3,2},{5,4},{6,5},{7,6},{9,8},{10,9},{11,10},{13,12},{... | collective-permute-start | bytes 491528 | tf_op jit(solution)/shard_map/ppermute | solution.py:36
  77.2 4.0 %collective-permute-start.11 = (f32[64,512]{1,0:T(8,128)S(1)}, f32[64,512]{1,0:T(8,128)S(1)}, u32[]{:S(2)}, u32[]{:S(2)}) collective-permute-start(f32[64,512]{1,0:T(8,128)S(1)} %get-tuple-element.44), channel_id=1, source_target_pairs={{0,1},{1,2},{2,3},{4,5},{5,6},{6,7},{8,9},{9,10},{10,11},{12,13},{... | collective-permute-start | bytes 393224 | tf_op jit(solution)/shard_map/ppermute | solution.py:36
  94.2 1.4 %copy-start.4 = (f32[16,3,2,8,512]{4,3,2,1,0:T(8,128)S(1)}, f32[16,3,2,8,512]{4,3,2,1,0:T(8,128)}, u32[]{:S(2)}) copy-start(f32[16,3,2,8,512]{4,3,2,1,0:T(8,128)} %get-tuple-element.22.refs_0_) | copy-start | bytes 4718596

commit v3 on v2

--- a/solution.py
+++ b/solution.py
@@ -20,8 +20,10 @@
 VMEM = pl.BlockSpec(memory_space=pltpu.VMEM)
 SMEM = pl.BlockSpec(memory_space=pltpu.SMEM)
 HBM = pl.BlockSpec(memory_space=pltpu.HBM)
+ANY = pl.BlockSpec(memory_space=pl.ANY)
 MIB = 1024 * 1024
 LIMIT = 16 * MIB
+UNROLL = 4
 LIMIT_FIRST = 63 * MIB
 
 
@@ -138,26 +140,36 @@
     for part in range(parts):
         copies[5 + part].wait()
 
-        @pl.loop(part * some, (part + 1) * some)
+        @pl.loop(part * some, (part + 1) * some, unroll=UNROLL)
         def _(d):
             a = [[a_ref[d, c, i] for i in range(2)] for c in range(3)]
             pack_ax(d, devs, a, ax_minus, ax_plus)
             ax_plus[pl.ds(4 * devs + d, 1)] = a[1][0][top:]
 
 
-def plane_kernel(a_ref, nu_ref, code_ref, ax_ahead, ax_behind, minus, plus):
+def plane_kernel(a_ref, nu_ref, code_ref, minus, plus):
     devs, height = a_ref.shape[0], a_ref.shape[3]
-    end = 2 * devs * height
-    minus[pl.ds(end, devs)] = ax_behind[pl.ds(4 * devs, devs)]
-    plus[pl.ds(end, devs)] = ax_ahead[pl.ds(devs, devs)]
-    plus[pl.ds(end + devs, height)] = nu_ref[1, 1]
-    plus[pl.ds(end + devs + height, height)] = nu_ref[2, 1]
-    plus[pl.ds(end + devs + 2 * height, height)] = code_ref[1]
-
-    @pl.loop(0, devs)
+    end = 2 * devs * height + devs
+    plus[pl.ds(end, height)] = nu_ref[1, 1]
+    plus[pl.ds(end + height, height)] = nu_ref[2, 1]
+    plus[pl.ds(end + 2 * height, height)] = code_ref[1]
+
+    @pl.loop(0, devs, unroll=UNROLL)
     def _(d):
         a = [[a_ref[d, c, i] for i in range(2)] for c in range(3)]
         pack_az(d, height, a, minus, plus)
+
+
+def corner_kernel(devs, ax_ahead, ax_behind, minus_in, plus_in, minus, plus, sems):
+    at = pl.ds(2 * devs * (minus.shape[0] // (2 * devs + 2)), devs)
+    copies = [
+        pltpu.make_async_copy(ax_behind.at[pl.ds(4 * devs, devs)], minus.at[at], sems.at[0]),
+        pltpu.make_async_copy(ax_ahead.at[pl.ds(devs, devs)], plus.at[at], sems.at[1]),
+    ]
+    for copy in copies:
+        copy.start()
+    for copy in copies:
+        copy.wait()
 
 
 def picked(code, values):
@@ -195,7 +207,12 @@
         minus, plus, ax_minus, ax_plus, next_track = [next(it) for _ in range(5)]
     if stage == 0:
         src_ref, src_az_ref, src_ax_ref = next(it), next(it), next(it)
+    if stage == 2:
+        final_hbm = next(it)
     edge, corner = next(it), next(it)
+    if stage == 2:
+        leave = pltpu.make_async_copy(a_ref, final_hbm, next(it))
+        leave.start()
     devs, height = a_ref.shape[0], a_ref.shape[3]
     top = height - 1
     end = 2 * devs * height
@@ -222,7 +239,7 @@
 
     if stage == 0:
 
-        @pl.loop(0, devs)
+        @pl.loop(0, devs, unroll=UNROLL)
         def _(d):
             for c in (0, 2):
                 own = values(d, c, per)
@@ -243,7 +260,7 @@
         next_track[pl.ds(0, 2 * devs)] = corner[...]
         next_track[pl.ds(3 * devs, devs)] = edge[pl.ds(3 * devs, devs)]
 
-    @pl.loop(0, devs)
+    @pl.loop(0, devs, unroll=UNROLL)
     def _(d):
         a = [[a_ref[d, c, i] for i in range(2)] for c in range(3)]
         up = [None, ahead[block(2 * d, height)], ahead[block(2 * d + 1, height)]]
@@ -307,6 +324,9 @@
             pack_az(d, height, new, minus, plus)
             pack_ax(d, devs, new, ax_minus, ax_plus)
 
+    if stage == 2:
+        leave.wait()
+
 
 def f32(*shape):
     return jax.ShapeDtypeStruct(shape, jnp.float32)
@@ -338,13 +358,23 @@
     )(start_field, reluctivity, lamination, magnets, region_ids, slot_map)
     ax_ahead, ax_behind = moved(ax_minus, 0, -1), moved(ax_plus, 0, 1)
     planes = [f32(whole + devs, radial), f32(whole + devs + 3 * cells_ax, radial)]
-    minus, plus = pl.pallas_call(
+    packed = pl.pallas_call(
         plane_kernel,
         out_shape=planes,
-        in_specs=[VMEM] * 5,
+        in_specs=[VMEM] * 3,
         out_specs=[VMEM] * 2,
         compiler_params=pltpu.CompilerParams(vmem_limit_bytes=LIMIT),
-    )(start_field, nu, code, ax_ahead, ax_behind)
+        cost_estimate=pl.CostEstimate(flops=10**7, bytes_accessed=3 * MIB, transcendentals=0),
+    )(start_field, nu, code)
+    minus, plus = pl.pallas_call(
+        functools.partial(corner_kernel, devs),
+        out_shape=planes,
+        in_specs=[VMEM, VMEM, ANY, ANY],
+        out_specs=[ANY] * 2,
+        scratch_shapes=[pltpu.SemaphoreType.DMA((2,))],
+        input_output_aliases={2: 0, 3: 1},
+        compiler_params=pltpu.CompilerParams(vmem_limit_bytes=LIMIT),
+    )(ax_ahead, ax_behind, *packed)
     halos = (moved(minus, -1, 0), moved(plus, 1, 0), ax_ahead, ax_behind, ax_minus)
     flat = pieces.reshape(1, comps * devs * per)
     table = lax.all_to_all(
@@ -366,17 +396,20 @@
                 f32(4 * devs, radial),
                 f32(4 * devs, radial),
             ]
+        else:
+            outs += [field_like]
         if stage == 0:
             outs += [field_like, f32(2 * devs, cells_ax, radial), f32(4 * devs, radial)]
         return pl.pallas_call(
             functools.partial(step_kernel, stage, per),
             out_shape=outs,
             in_specs=[VMEM] * 9 + more_specs,
-            out_specs=[VMEM] * len(outs),
+            out_specs=[VMEM] * len(outs) if stage < 2 else [VMEM, HBM],
             scratch_shapes=[
                 pltpu.VMEM((4 * devs, radial), jnp.float32),
                 pltpu.VMEM((2 * devs, radial), jnp.float32),
-            ],
+            ]
+            + [pltpu.SemaphoreType.DMA] * (stage // 2),
             compiler_params=pltpu.CompilerParams(vmem_limit_bytes=LIMIT),
         )(field, nu, nu_az, nu_ax, *halos, *more)
 
@@ -384,8 +417,8 @@
     packed, track0, src = rest[:4], rest[4], rest[5:]
     final, *rest = step(1, middle, exchange(*packed), [*src, track0, start_field], [VMEM] * 5)
     packed, track1 = rest[:4], rest[4]
-    (residual,) = step(2, final, exchange(*packed), [*src, track0, track1], [VMEM] * 5)
-    return final, residual
+    residual, out = step(2, final, exchange(*packed), [*src, track0, track1], [VMEM] * 5)
+    return out, residual
 
 
 def solution(mesh):

time: 101 us -> 90.6 us (0.90)
  Pallas kernels: 19.9 us -> 11.7 us
  local copies, waits for them, and re-layouts: 4.79 us -> 3.37 us
  waiting for transfers between devices: 31.3 us -> 30 us
    pallas_call x3, Pallas kernels: 14.3 us -> 7.46 us  [step(): pl.pallas_call(functools.partial(step_kernel, stage, per), out_shape=outs...]
    unnamed x21 -> x19, local copies, waits for them, and re-layouts: 4.58 us -> 3.17 us
    ppermute x12, waiting for transfers between devices: 31.3 us -> 30 us  [moved(): return lax.ppermute(value, ('az', 'ax'), pairs)]
    all_to_all x1, blocking collectives: 13.8 us -> 14.8 us  [shards(): lax.all_to_all(jnp.broadcast_to(flat, (count_az, comps * devs * per)), 'a...]
    pallas_call x1 -> x2, Pallas kernels: 2.16 us -> 1.73 us  [the longest x1 1.09 us: shards(): pl.pallas_call(plane_kernel, out_shape=planes, in_specs=[VMEM] * 3, out_s...]
  transfers between devices with their start and end apart: 12 -> 12, of which waited for: 5 -> 4; matrix products, arithmetic and copies ran while one was open for 0% -> 0% of each run, Pallas kernels for 0% -> 1%
where the time goes in v3:
time: 90.6 us; the launch traced here: 89.8 us
  waiting for transfers between devices  30 us (33%)
  starting transfers between devices  29.1 us (32%)
  blocking collectives  14.8 us (16%)
  Pallas kernels  11.7 us (13%)
  local copies, waits for them, and re-layouts  3.37 us (4%)
    ppermute x12, waiting for transfers between devices, moved(): return lax.ppermute(value, ('az', 'ax'), pairs)  30 us
    ppermute x12, starting transfers between devices, moved(): return lax.ppermute(value, ('az', 'ax'), pairs)  29.1 us
    all_to_all x1, blocking collectives, shards(): lax.all_to_all(jnp.broadcast_to(flat, (count_az, comps * devs * per)), 'a...  14.8 us
    pallas_call x3, Pallas kernels, step(): pl.pallas_call(functools.partial(step_kernel, stage, per), out_shape=outs...  7.46 us
    unnamed x19, local copies, waits for them, and re-layouts  3.17 us
    pallas_call x1, Pallas kernels, shards(): pl.pallas_call(functools.partial(edge_kernel, per), out_shape=edges, in_s...  2.53 us
  transfers between devices with their start and end apart: 12, of which 4 were waited for; matrix products, arithmetic and copies ran while one was open for 0% of the time, Pallas kernels for 1%

profile of v3, /device:TPU:0, one launch (start us, length us, event | category | flops | bytes accessed | tf_op | source)
XLA Modules:
  0.0 89.8 jit_solution(9812578583027204406)
XLA Ops:
  0.6 2.5 %shard_map.86 = (f32[64,512]{1,0:T(8,128)}, f32[88,512]{1,0:T(8,128)}, f32[3,2,8,512]{3,2,1,0:T(8,128)}, f32[2,8,512]{2,1,0:T(8,128)}, s32[16,128]{1,0:T(8,128)}) custom-call(f32[16,3,2,8,512]{4,3,2,1,0:T(8,128)} %refs_13_.1, f32[3,2,8,512]{3,2,1,0:T(8,128)} %reluct_hbm.1, s32[2,8,512]{2,1,0:T(8,128)} %lam_hbm.1, s32[2,8,512]{2,1,0:T(8,128)} %mag_hbm.1, ...), custom_call_target="tpu_custom_call" | custom-call | tf_op jit(solution)/shard_map/pallas_call | solution.py:349
  3.2 1.3 %collective-permute-start.1 = (f32[88,512]{1,0:T(8,128)}, f32[88,512]{1,0:T(8,128)S(1)}, u32[]{:S(2)}, u32[]{:S(2)}) collective-permute-start(f32[88,512]{1,0:T(8,128)} %get-tuple-element.30), channel_id=1, source_target_pairs={{0,1},{1,2},{2,3},{4,5},{5,6},{6,7},{8,9},{9,10},{10,11},{12,13},{... | collective-permute-start | bytes 540680 | tf_op jit(solution)/shard_map/ppermute | solution.py:38
  4.5 1.3 %collective-permute-start = (f32[64,512]{1,0:T(8,128)}, f32[64,512]{1,0:T(8,128)S(1)}, u32[]{:S(2)}, u32[]{:S(2)}) collective-permute-start(f32[64,512]{1,0:T(8,128)} %get-tuple-element.29.refs_8_), channel_id=1, source_target_pairs={{1,0},{2,1},{3,2},{5,4},{6,5},{7,6},{9,8},{10,9},{11,10},{13,12},{... | collective-permute-start | bytes 393224 | tf_op jit(solution)/shard_map/ppermute | solution.py:38
  5.8 1.4 %copy-done = f32[16,3,2,8,512]{4,3,2,1,0:T(8,128)S(1)} copy-done((f32[16,3,2,8,512]{4,3,2,1,0:T(8,128)S(1)}, f32[16,3,2,8,512]{4,3,2,1,0:T(8,128)}, u32[]{:S(2)}) %copy-start) | copy-done | bytes 1572888
  7.2 0.9 copy-done.2
  8.1 0.8 copy-done.5
  8.9 1.1 %shard_map.87 = (f32[272,512]{1,0:T(8,128)}, f32[296,512]{1,0:T(8,128)S(1)}) custom-call(f32[16,3,2,8,512]{4,3,2,1,0:T(8,128)S(1)} %copy-done, f32[3,2,8,512]{3,2,1,0:T(8,128)S(1)} %copy-done.2, f32[2,8,512]{2,1,0:T(8,128)S(1)} %copy-done.5), custom_call_target="tpu_custom_call" | custom-call | flops 10000000 | bytes 3145728 | tf_op jit(solution)/shard_map/pallas_call | solution.py:361
  10.0 0.6 shard_map.88
  10.6 2.5 %collective-permute-start.2 = (f32[296,512]{1,0:T(8,128)S(1)}, f32[296,512]{1,0:T(8,128)S(1)}, u32[]{:S(2)}, u32[]{:S(2)}) collective-permute-start(f32[296,512]{1,0:T(8,128)S(1)} %get-tuple-element.34), channel_id=1, source_target_pairs={{0,4},{1,5},{2,6},{3,7},{4,8},{5,9},{6,10},{7,11},{8,12},{9,13},{1... | collective-permute-start | bytes 1818632 | tf_op jit(solution)/shard_map/ppermute | solution.py:38
  13.1 7.1 %collective-permute-start.3 = (f32[272,512]{1,0:T(8,128)}, f32[272,512]{1,0:T(8,128)}, u32[]{:S(2)}, u32[]{:S(2)}) collective-permute-start(f32[272,512]{1,0:T(8,128)} %get-tuple-element.35), channel_id=1, source_target_pairs={{0,124},{1,125},{2,126},{3,127},{4,0},{5,1},{6,2},{7,3},{8,4},{9,5... | collective-permute-start | bytes 1671176 | tf_op jit(solution)/shard_map/ppermute | solution.py:38
  20.5 14.8 %all_to_all.6 = f32[32,1,192]{2,1,0:T(1,128)S(1)} all-to-all(f32[32,1,192]{2,1,0:T(1,128)S(1)} %broadcast_in_dim.8), channel_id=1, replica_groups=mesh['az'=32,'ax'=4] {'az'}, dimensions={0} | all-to-all | bytes 49152 | tf_op jit(solution)/shard_map/all_to_all | solution.py:380
  35.5 3.4 %shard_map.89 = (f32[16,3,2,8,512]{4,3,2,1,0:T(8,128)S(1)}, f32[272,512]{1,0:T(8,128)S(1)}, f32[256,512]{1,0:T(8,128)S(1)}, f32[80,512]{1,0:T(8,128)S(1)}, f32[6...) custom-call(f32[16,3,2,8,512]{4,3,2,1,0:T(8,128)S(1)} %copy-done.1, ...), custom_call_target="tpu_custom_call" | custom-call | tf_op jit(solution)/shard_map/pallas_call | solution.py:403
  38.9 5.4 %collective-permute-start.4 = (f32[272,512]{1,0:T(8,128)S(1)}, f32[272,512]{1,0:T(8,128)S(1)}, u32[]{:S(2)}, u32[]{:S(2)}) collective-permute-start(f32[272,512]{1,0:T(8,128)S(1)} %get-tuple-element.38), channel_id=1, source_target_pairs={{0,124},{1,125},{2,126},{3,127},{4,0},{5,1},{6,2},{7,3},{8,4},{9,5... | collective-permute-start | bytes 1671176 | tf_op jit(solution)/shard_map/ppermute | solution.py:38
  44.3 1.3 %collective-permute-start.6 = (f32[80,512]{1,0:T(8,128)S(1)}, f32[80,512]{1,0:T(8,128)S(1)}, u32[]{:S(2)}, u32[]{:S(2)}) collective-permute-start(f32[80,512]{1,0:T(8,128)S(1)} %get-tuple-element.40.refs_8_), channel_id=1, source_target_pairs={{1,0},{2,1},{3,2},{5,4},{6,5},{7,6},{9,8},{10,9},{11,10},{13,12},{... | collective-permute-start | bytes 491528 | tf_op jit(solution)/shard_map/ppermute | solution.py:38
  45.6 3.7 %collective-permute-start.7 = (f32[64,512]{1,0:T(8,128)S(1)}, f32[64,512]{1,0:T(8,128)S(1)}, u32[]{:S(2)}, u32[]{:S(2)}) collective-permute-start(f32[64,512]{1,0:T(8,128)S(1)} %get-tuple-element.41), channel_id=1, source_target_pairs={{0,1},{1,2},{2,3},{4,5},{5,6},{6,7},{8,9},{9,10},{10,11},{12,13},{... | collective-permute-start | bytes 393224 | tf_op jit(solution)/shard_map/ppermute | solution.py:38
  49.3 1.0 %collective-permute-done.7.refs_7_ = f32[64,512]{1,0:T(8,128)S(1)} collective-permute-done((f32[64,512]{1,0:T(8,128)S(1)}, f32[64,512]{1,0:T(8,128)S(1)}, u32[]{:S(2)}, u32[]{:S(2)}) %collective-permute-start.7) | collective-permute-done | bytes 131104 | tf_op jit(solution)/shard_map/ppermute | solution.py:38
  50.3 14.3 %collective-permute-done.5.refs_5_ = f32[256,512]{1,0:T(8,128)S(1)} collective-permute-done((f32[256,512]{1,0:T(8,128)S(1)}, f32[256,512]{1,0:T(8,128)S(1)}, u32[]{:S(2)}, u32[]{:S(2)}) %collective-permute-start.5) | collective-permute-done | bytes 524320 | tf_op jit(solution)/shard_map/ppermute | solution.py:38
  64.6 1.7 %shard_map.90 = (f32[16,3,2,8,512]{4,3,2,1,0:T(8,128)S(1)}, f32[272,512]{1,0:T(8,128)S(1)}, f32[256,512]{1,0:T(8,128)S(1)}, f32[80,512]{1,0:T(8,128)S(1)}, f32[64,512]{1,0:T(8,128)S(1)}, /*index=5*/f32[64,512]{1,0:T(8,128)S(1)}) custom-call(f32[16,3,2,8,512]{4,3,2,1,0:T(8,128)S(1)} %get-tuple-element.37.refs_0_, f32[3,2,8,512]{3,2,1,0:T(8,128)S(1)} %copy-done.3, ...), custom_call_target="tpu_custom_call" | custom-call | tf_op jit(solution)/shard_map/pallas_call | solution.py:403
  66.9 1.5 %collective-permute-start.9 = (f32[256,512]{1,0:T(8,128)S(1)}, f32[256,512]{1,0:T(8,128)S(1)}, u32[]{:S(2)}, u32[]{:S(2)}) collective-permute-start(f32[256,512]{1,0:T(8,128)S(1)} %get-tuple-element.48), channel_id=1, source_target_pairs={{0,4},{1,5},{2,6},{3,7},{4,8},{5,9},{6,10},{7,11},{8,12},{9,13},{1... | collective-permute-start | bytes 1572872 | tf_op jit(solution)/shard_map/ppermute | solution.py:38
  68.5 1.3 %collective-permute-start.10 = (f32[80,512]{1,0:T(8,128)S(1)}, f32[80,512]{1,0:T(8,128)S(1)}, u32[]{:S(2)}, u32[]{:S(2)}) collective-permute-start(f32[80,512]{1,0:T(8,128)S(1)} %get-tuple-element.49.refs_8_), channel_id=1, source_target_pairs={{1,0},{2,1},{3,2},{5,4},{6,5},{7,6},{9,8},{10,9},{11,10},{13,12},{... | collective-permute-start | bytes 491528 | tf_op jit(solution)/shard_map/ppermute | solution.py:38
  69.8 3.0 %collective-permute-start.11 = (f32[64,512]{1,0:T(8,128)S(1)}, f32[64,512]{1,0:T(8,128)S(1)}, u32[]{:S(2)}, u32[]{:S(2)}) collective-permute-start(f32[64,512]{1,0:T(8,128)S(1)} %get-tuple-element.50), channel_id=1, source_target_pairs={{0,1},{1,2},{2,3},{4,5},{5,6},{6,7},{8,9},{9,10},{10,11},{12,13},{... | collective-permute-start | bytes 393224 | tf_op jit(solution)/shard_map/ppermute | solution.py:38
  72.8 1.0 %collective-permute-done.11.refs_7_ = f32[64,512]{1,0:T(8,128)S(1)} collective-permute-done((f32[64,512]{1,0:T(8,128)S(1)}, f32[64,512]{1,0:T(8,128)S(1)}, u32[]{:S(2)}, u32[]{:S(2)}) %collective-permute-start.11) | collective-permute-done | bytes 131104 | tf_op jit(solution)/shard_map/ppermute | solution.py:38
  73.8 13.7 %collective-permute-done.9.refs_5_ = f32[256,512]{1,0:T(8,128)S(1)} collective-permute-done((f32[256,512]{1,0:T(8,128)S(1)}, f32[256,512]{1,0:T(8,128)S(1)}, u32[]{:S(2)}, u32[]{:S(2)}) %collective-permute-start.9) | collective-permute-done | bytes 524320 | tf_op jit(solution)/shard_map/ppermute | solution.py:38
  87.5 2.3 %shard_map.91 = (f32[16,3,2,8,512]{4,3,2,1,0:T(8,128)}, f32[16,3,2,8,512]{4,3,2,1,0:T(8,128)}) custom-call(f32[16,3,2,8,512]{4,3,2,1,0:T(8,128)S(1)} %get-tuple-element.46.refs_0_, f32[3,2,8,512]{3,2,1,0:T(8,128)S(1)} %copy-done.3, f32[296,512]{1,0:T(8,128)S(1)} %collective-permute-done.2.refs_2_.refs_5_, ...), custom_call_target="tpu_custom_call" | custom-call | tf_op jit(solution)/shard_map/pallas_call | solution.py:403
  (30 shorter events, 1.0 us)
Async XLA Ops:
  3.2 6.8 %collective-permute-start.1 = (f32[88,512]{1,0:T(8,128)}, f32[88,512]{1,0:T(8,128)S(1)}, u32[]{:S(2)}, u32[]{:S(2)}) collective-permute-start(f32[88,512]{1,0:T(8,128)} %get-tuple-element.30), channel_id=1, source_target_pairs={{0,1},{1,2},{2,3},{4,5},{5,6},{6,7},{8,9},{9,10},{10,11},{12,13},{... | collective-permute-start | bytes 540680 | tf_op jit(solution)/shard_map/ppermute | solution.py:38
  4.5 5.5 %collective-permute-start = (f32[64,512]{1,0:T(8,128)}, f32[64,512]{1,0:T(8,128)S(1)}, u32[]{:S(2)}, u32[]{:S(2)}) collective-permute-start(f32[64,512]{1,0:T(8,128)} %get-tuple-element.29.refs_8_), channel_id=1, source_target_pairs={{1,0},{2,1},{3,2},{5,4},{6,5},{7,6},{9,8},{10,9},{11,10},{13,12},{... | collective-permute-start | bytes 393224 | tf_op jit(solution)/shard_map/ppermute | solution.py:38
  5.8 1.4 %copy-start = (f32[16,3,2,8,512]{4,3,2,1,0:T(8,128)S(1)}, f32[16,3,2,8,512]{4,3,2,1,0:T(8,128)}, u32[]{:S(2)}) copy-start(f32[16,3,2,8,512]{4,3,2,1,0:T(8,128)} %refs_13_.1) | copy-start | bytes 4718596
  7.2 0.9 copy-start.2
  8.1 0.8 copy-start.5
  8.8 11.4 %copy-start.8 = (f32[3,16,4]{1,2,0:T(4,128)S(1)}, f32[3,16,4]{1,2,0:T(4,128)}, u32[]{:S(2)}) copy-start(f32[3,16,4]{1,2,0:T(4,128)} %param.12) | copy-start | bytes 2308
  8.8 26.6 %copy-start.1 = (f32[16,3,2,8,512]{4,3,2,1,0:T(8,128)S(1)}, f32[16,3,2,8,512]{4,3,2,1,0:T(8,128)}, u32[]{:S(2)}) copy-start(f32[16,3,2,8,512]{4,3,2,1,0:T(8,128)} %refs_13_.1) | copy-start | bytes 4718596
  8.8 26.6 %copy-start.3 = (f32[3,2,8,512]{3,2,1,0:T(8,128)S(1)}, f32[3,2,8,512]{3,2,1,0:T(8,128)}, u32[]{:S(2)}) copy-start(f32[3,2,8,512]{3,2,1,0:T(8,128)} %get-tuple-element.28.nu_ref.refs_1_) | copy-start | bytes 294916
  8.8 26.6 %copy-start.4 = (f32[64,512]{1,0:T(8,128)S(1)}, f32[64,512]{1,0:T(8,128)}, u32[]{:S(2)}) copy-start(f32[64,512]{1,0:T(8,128)} %get-tuple-element.29.refs_8_) | copy-start | bytes 393220
  8.9 26.6 %copy-start.6 = (f32[2,8,512]{2,1,0:T(8,128)S(1)}, f32[2,8,512]{2,1,0:T(8,128)}, u32[]{:S(2)}) copy-start(f32[2,8,512]{2,1,0:T(8,128)} %get-tuple-element.31.code_ref.refs_9_) | copy-start | bytes 98308
  8.9 26.6 %copy-start.7 = (s32[16,128]{1,0:T(8,128)S(1)}, s32[16,128]{1,0:T(8,128)}, u32[]{:S(2)}) copy-start(s32[16,128]{1,0:T(8,128)} %get-tuple-element.36.refs_10_) | copy-start | bytes 24580
  10.6 24.8 %collective-permute-start.2 = (f32[296,512]{1,0:T(8,128)S(1)}, f32[296,512]{1,0:T(8,128)S(1)}, u32[]{:S(2)}, u32[]{:S(2)}) collective-permute-start(f32[296,512]{1,0:T(8,128)S(1)} %get-tuple-element.34), channel_id=1, source_target_pairs={{0,4},{1,5},{2,6},{3,7},{4,8},{5,9},{6,10},{7,11},{8,12},{9,13},{1... | collective-permute-start | bytes 1818632 | tf_op jit(solution)/shard_map/ppermute | solution.py:38
  13.1 22.3 %collective-permute-start.3 = (f32[272,512]{1,0:T(8,128)}, f32[272,512]{1,0:T(8,128)}, u32[]{:S(2)}, u32[]{:S(2)}) collective-permute-start(f32[272,512]{1,0:T(8,128)} %get-tuple-element.35), channel_id=1, source_target_pairs={{0,124},{1,125},{2,126},{3,127},{4,0},{5,1},{6,2},{7,3},{8,4},{9,5... | collective-permute-start | bytes 1671176 | tf_op jit(solution)/shard_map/ppermute | solution.py:38
  38.9 25.8 %collective-permute-start.4 = (f32[272,512]{1,0:T(8,128)S(1)}, f32[272,512]{1,0:T(8,128)S(1)}, u32[]{:S(2)}, u32[]{:S(2)}) collective-permute-start(f32[272,512]{1,0:T(8,128)S(1)} %get-tuple-element.38), channel_id=1, source_target_pairs={{0,124},{1,125},{2,126},{3,127},{4,0},{5,1},{6,2},{7,3},{8,4},{9,5... | collective-permute-start | bytes 1671176 | tf_op jit(solution)/shard_map/ppermute | solution.py:38
  44.3 20.3 %collective-permute-start.5 = (f32[256,512]{1,0:T(8,128)S(1)}, f32[256,512]{1,0:T(8,128)S(1)}, u32[]{:S(2)}, u32[]{:S(2)}) collective-permute-start(f32[256,512]{1,0:T(8,128)S(1)} %get-tuple-element.39), channel_id=1, source_target_pairs={{0,4},{1,5},{2,6},{3,7},{4,8},{5,9},{6,10},{7,11},{8,12},{9,13},{1... | collective-permute-start | bytes 1572872 | tf_op jit(solution)/shard_map/ppermute | solution.py:38
  44.3 6.0 %collective-permute-start.6 = (f32[80,512]{1,0:T(8,128)S(1)}, f32[80,512]{1,0:T(8,128)S(1)}, u32[]{:S(2)}, u32[]{:S(2)}) collective-permute-start(f32[80,512]{1,0:T(8,128)S(1)} %get-tuple-element.40.refs_8_), channel_id=1, source_target_pairs={{1,0},{2,1},{3,2},{5,4},{6,5},{7,6},{9,8},{10,9},{11,10},{13,12},{... | collective-permute-start | bytes 491528 | tf_op jit(solution)/shard_map/ppermute | solution.py:38
  45.6 4.7 %collective-permute-start.7 = (f32[64,512]{1,0:T(8,128)S(1)}, f32[64,512]{1,0:T(8,128)S(1)}, u32[]{:S(2)}, u32[]{:S(2)}) collective-permute-start(f32[64,512]{1,0:T(8,128)S(1)} %get-tuple-element.41), channel_id=1, source_target_pairs={{0,1},{1,2},{2,3},{4,5},{5,6},{6,7},{8,9},{9,10},{10,11},{12,13},{... | collective-permute-start | bytes 393224 | tf_op jit(solution)/shard_map/ppermute | solution.py:38
  66.4 21.1 %collective-permute-start.8 = (f32[272,512]{1,0:T(8,128)S(1)}, f32[272,512]{1,0:T(8,128)S(1)}, u32[]{:S(2)}, u32[]{:S(2)}) collective-permute-start(f32[272,512]{1,0:T(8,128)S(1)} %get-tuple-element.47), channel_id=1, source_target_pairs={{0,124},{1,125},{2,126},{3,127},{4,0},{5,1},{6,2},{7,3},{8,4},{9,5... | collective-permute-start | bytes 1671176 | tf_op jit(solution)/shard_map/ppermute | solution.py:38
  66.9 20.5 %collective-permute-start.9 = (f32[256,512]{1,0:T(8,128)S(1)}, f32[256,512]{1,0:T(8,128)S(1)}, u32[]{:S(2)}, u32[]{:S(2)}) collective-permute-start(f32[256,512]{1,0:T(8,128)S(1)} %get-tuple-element.48), channel_id=1, source_target_pairs={{0,4},{1,5},{2,6},{3,7},{4,8},{5,9},{6,10},{7,11},{8,12},{9,13},{1... | collective-permute-start | bytes 1572872 | tf_op jit(solution)/shard_map/ppermute | solution.py:38
  68.5 5.3 %collective-permute-start.10 = (f32[80,512]{1,0:T(8,128)S(1)}, f32[80,512]{1,0:T(8,128)S(1)}, u32[]{:S(2)}, u32[]{:S(2)}) collective-permute-start(f32[80,512]{1,0:T(8,128)S(1)} %get-tuple-element.49.refs_8_), channel_id=1, source_target_pairs={{1,0},{2,1},{3,2},{5,4},{6,5},{7,6},{9,8},{10,9},{11,10},{13,12},{... | collective-permute-start | bytes 491528 | tf_op jit(solution)/shard_map/ppermute | solution.py:38
  69.8 4.0 %collective-permute-start.11 = (f32[64,512]{1,0:T(8,128)S(1)}, f32[64,512]{1,0:T(8,128)S(1)}, u32[]{:S(2)}, u32[]{:S(2)}) collective-permute-start(f32[64,512]{1,0:T(8,128)S(1)} %get-tuple-element.50), channel_id=1, source_target_pairs={{0,1},{1,2},{2,3},{4,5},{5,6},{6,7},{8,9},{9,10},{10,11},{12,13},{... | collective-permute-start | bytes 393224 | tf_op jit(solution)/shard_map/ppermute | solution.py:38

commit v4 on v3

--- a/solution.py
+++ b/solution.py
@@ -36,6 +36,28 @@
         if 0 <= q + shift_ax < count_ax
     ]
     return lax.ppermute(value, ("az", "ax"), pairs)
+
+
+def swapped(value, odd):
+    count_az, count_ax = lax.axis_size("az"), lax.axis_size("ax")
+    pairs = [
+        (a * count_ax + q, (a + (1 if a % 2 == odd else -1)) % count_az * count_ax + q)
+        for a in range(count_az)
+        for q in range(count_ax)
+    ]
+    return lax.ppermute(value, ("az", "ax"), pairs)
+
+
+def by_parity(body, far, near):
+    parity = lax.rem(lax.axis_index("az"), 2)
+
+    @pl.when(parity == 0)
+    def _():
+        body(near, far)
+
+    @pl.when(parity == 1)
+    def _():
+        body(far, near)
 
 
 def lanes(shape):
@@ -147,29 +169,37 @@
             ax_plus[pl.ds(4 * devs + d, 1)] = a[1][0][top:]
 
 
-def plane_kernel(a_ref, nu_ref, code_ref, minus, plus):
+def plane_kernel(a_ref, nu_ref, code_ref, far, near):
     devs, height = a_ref.shape[0], a_ref.shape[3]
     end = 2 * devs * height + devs
-    plus[pl.ds(end, height)] = nu_ref[1, 1]
-    plus[pl.ds(end + height, height)] = nu_ref[2, 1]
-    plus[pl.ds(end + 2 * height, height)] = code_ref[1]
-
-    @pl.loop(0, devs, unroll=UNROLL)
-    def _(d):
-        a = [[a_ref[d, c, i] for i in range(2)] for c in range(3)]
-        pack_az(d, height, a, minus, plus)
-
-
-def corner_kernel(devs, ax_ahead, ax_behind, minus_in, plus_in, minus, plus, sems):
-    at = pl.ds(2 * devs * (minus.shape[0] // (2 * devs + 2)), devs)
-    copies = [
-        pltpu.make_async_copy(ax_behind.at[pl.ds(4 * devs, devs)], minus.at[at], sems.at[0]),
-        pltpu.make_async_copy(ax_ahead.at[pl.ds(devs, devs)], plus.at[at], sems.at[1]),
-    ]
-    for copy in copies:
-        copy.start()
-    for copy in copies:
-        copy.wait()
+
+    def body(plus, minus):
+        plus[pl.ds(end, height)] = nu_ref[1, 1]
+        plus[pl.ds(end + height, height)] = nu_ref[2, 1]
+        plus[pl.ds(end + 2 * height, height)] = code_ref[1]
+
+        @pl.loop(0, devs, unroll=UNROLL)
+        def _(d):
+            a = [[a_ref[d, c, i] for i in range(2)] for c in range(3)]
+            pack_az(d, height, a, minus, plus)
+
+    by_parity(body, far, near)
+
+
+def corner_kernel(end, devs, ax_ahead, ax_behind, far_in, near_in, far, near, sems):
+    at = pl.ds(end, devs)
+
+    def body(plus, minus):
+        copies = [
+            pltpu.make_async_copy(ax_behind.at[pl.ds(4 * devs, devs)], minus.at[at], sems.at[0]),
+            pltpu.make_async_copy(ax_ahead.at[pl.ds(devs, devs)], plus.at[at], sems.at[1]),
+        ]
+        for copy in copies:
+            copy.start()
+        for copy in copies:
+            copy.wait()
+
+    by_parity(body, far, near)
 
 
 def picked(code, values):
@@ -190,9 +220,26 @@
 
 
 def step_kernel(stage, per, *refs):
+    refs = list(refs)
+    halo = [refs.pop(4), refs.pop(4)]
+    statics = refs.pop(2), refs.pop(2)
+    sent = [None, None]
+    if stage < 2:
+        first = (10, 12)[stage]
+        sent = [refs.pop(first), refs.pop(first)]
+
+    def body(plus, minus):
+        step_body(stage, per, refs, plus, minus)
+
+    by_parity(body, (halo[0], statics[0], sent[0]), (halo[1], statics[1], sent[1]))
+
+
+def step_body(stage, per, refs, beyond_refs, behind_refs):
     it = iter(refs)
-    a_ref, nu_ref, nu_az_ref, nu_ax_ref = next(it), next(it), next(it), next(it)
-    ahead, behind, ax_ahead, ax_behind, mine = [next(it) for _ in range(5)]
+    ahead, _, plus = beyond_refs
+    behind, nu_az_ref, minus = behind_refs
+    a_ref, nu_ref, nu_ax_ref = next(it), next(it), next(it)
+    ax_ahead, ax_behind, mine = [next(it) for _ in range(3)]
     if stage == 0:
         code_ref, offset_ref, table_ref = next(it), next(it), next(it)
     else:
@@ -204,7 +251,7 @@
         track = next(it)
     out_ref = next(it)
     if stage < 2:
-        minus, plus, ax_minus, ax_plus, next_track = [next(it) for _ in range(5)]
+        ax_minus, ax_plus, next_track = [next(it) for _ in range(3)]
     if stage == 0:
         src_ref, src_az_ref, src_ax_ref = next(it), next(it), next(it)
     if stage == 2:
@@ -357,7 +404,7 @@
         compiler_params=pltpu.CompilerParams(vmem_limit_bytes=LIMIT_FIRST),
     )(start_field, reluctivity, lamination, magnets, region_ids, slot_map)
     ax_ahead, ax_behind = moved(ax_minus, 0, -1), moved(ax_plus, 0, 1)
-    planes = [f32(whole + devs, radial), f32(whole + devs + 3 * cells_ax, radial)]
+    planes = [f32(whole + devs + 3 * cells_ax, radial)] * 2
     packed = pl.pallas_call(
         plane_kernel,
         out_shape=planes,
@@ -366,8 +413,8 @@
         compiler_params=pltpu.CompilerParams(vmem_limit_bytes=LIMIT),
         cost_estimate=pl.CostEstimate(flops=10**7, bytes_accessed=3 * MIB, transcendentals=0),
     )(start_field, nu, code)
-    minus, plus = pl.pallas_call(
-        functools.partial(corner_kernel, devs),
+    far, near = pl.pallas_call(
+        functools.partial(corner_kernel, whole, devs),
         out_shape=planes,
         in_specs=[VMEM, VMEM, ANY, ANY],
         out_specs=[ANY] * 2,
@@ -375,23 +422,23 @@
         input_output_aliases={2: 0, 3: 1},
         compiler_params=pltpu.CompilerParams(vmem_limit_bytes=LIMIT),
     )(ax_ahead, ax_behind, *packed)
-    halos = (moved(minus, -1, 0), moved(plus, 1, 0), ax_ahead, ax_behind, ax_minus)
+    far_halo, near_halo = swapped(far, 1), swapped(near, 0)
+    halos = (far_halo, near_halo, ax_ahead, ax_behind, ax_minus)
     flat = pieces.reshape(1, comps * devs * per)
     table = lax.all_to_all(
         jnp.broadcast_to(flat, (count_az, comps * devs * per)), "az", 0, 0, tiled=True
     ).reshape(-1)
-    nu_az, nu_ax = halos[1], halos[3]
-
-    def exchange(minus, plus, ax_minus, ax_plus):
-        ahead, behind = moved(minus, -1, 0), moved(plus, 1, 0)
-        return ahead, behind, moved(ax_minus, 0, -1), moved(ax_plus, 0, 1), ax_minus
+
+    def exchange(far, near, ax_minus, ax_plus):
+        from_far, from_near = swapped(far, 1), swapped(near, 0)
+        return from_far, from_near, moved(ax_minus, 0, -1), moved(ax_plus, 0, 1), ax_minus
 
     def step(stage, field, halos, more, more_specs):
         outs = [field_like]
         if stage < 2:
             outs += [
                 f32(whole + devs, radial),
-                f32(whole, radial),
+                f32(whole + devs, radial),
                 f32(5 * devs, radial),
                 f32(4 * devs, radial),
                 f32(4 * devs, radial),
@@ -403,7 +450,7 @@
         return pl.pallas_call(
             functools.partial(step_kernel, stage, per),
             out_shape=outs,
-            in_specs=[VMEM] * 9 + more_specs,
+            in_specs=[VMEM] * 10 + more_specs,
             out_specs=[VMEM] * len(outs) if stage < 2 else [VMEM, HBM],
             scratch_shapes=[
                 pltpu.VMEM((4 * devs, radial), jnp.float32),
@@ -411,7 +458,7 @@
             ]
             + [pltpu.SemaphoreType.DMA] * (stage // 2),
             compiler_params=pltpu.CompilerParams(vmem_limit_bytes=LIMIT),
-        )(field, nu, nu_az, nu_ax, *halos, *more)
+        )(field, nu, far_halo, near_halo, *halos[:2], ax_behind, *halos[2:], *more)
 
     middle, *rest = step(0, start_field, halos, [code, offset, table], [VMEM, SMEM, SMEM])
     packed, track0, src = rest[:4], rest[4], rest[5:]

time: 90.6 us -> 87.6 us (0.967)
  waiting for transfers between devices: 30 us -> 22.5 us
  starting transfers between devices: 29.1 us -> 32.2 us
  blocking collectives: 14.8 us -> 16 us
    ppermute x12 -> x6, waiting for transfers between devices: 30 us -> 1.93 us  [moved(): return lax.ppermute(value, ('az', 'ax'), pairs)]
    ppermute x0 -> x6, starting transfers between devices: none -> 20.7 us  [swapped(): return lax.ppermute(value, ('az', 'ax'), pairs)]
    ppermute x0 -> x6, waiting for transfers between devices: none -> 20.6 us  [swapped(): return lax.ppermute(value, ('az', 'ax'), pairs)]
    ppermute x12 -> x6, starting transfers between devices: 29.1 us -> 11.5 us  [moved(): return lax.ppermute(value, ('az', 'ax'), pairs)]
    all_to_all x1, blocking collectives: 14.8 us -> 16 us  [shards(): lax.all_to_all(jnp.broadcast_to(flat, (count_az, comps * devs * per)), 'a...]
  transfers between devices with their start and end apart: 12 -> 12, of which waited for: 4 -> 4; matrix products, arithmetic and copies ran while one was open for 0% -> 0% of each run, Pallas kernels for 1% -> 2%
where the time goes in v4:
time: 87.6 us; the launch traced here: 87.2 us
  starting transfers between devices  32.2 us (37%)
  waiting for transfers between devices  22.5 us (26%)
  blocking collectives  16 us (18%)
  Pallas kernels  12.1 us (14%)
  local copies, waits for them, and re-layouts  3.37 us (4%)
    ppermute x6, starting transfers between devices, swapped(): return lax.ppermute(value, ('az', 'ax'), pairs)  20.7 us
    ppermute x6, waiting for transfers between devices, swapped(): return lax.ppermute(value, ('az', 'ax'), pairs)  20.6 us
    all_to_all x1, blocking collectives, shards(): lax.all_to_all(jnp.broadcast_to(flat, (count_az, comps * devs * per)), 'a...  16 us
    ppermute x6, starting transfers between devices, moved(): return lax.ppermute(value, ('az', 'ax'), pairs)  11.5 us
    pallas_call x3, Pallas kernels, step(): pl.pallas_call(functools.partial(step_kernel, stage, per), out_shape=outs...  7.55 us
    unnamed x19, local copies, waits for them, and re-layouts  3.17 us
    pallas_call x1, Pallas kernels, shards(): pl.pallas_call(functools.partial(edge_kernel, per), out_shape=edges, in_s...  2.55 us
    ppermute x6, waiting for transfers between devices, moved(): return lax.ppermute(value, ('az', 'ax'), pairs)  1.93 us
  transfers between devices with their start and end apart: 12, of which 4 were waited for; matrix products, arithmetic and copies ran while one was open for 0% of the time, Pallas kernels for 2%

profile of v4, /device:TPU:0, one launch (start us, length us, event | category | flops | bytes accessed | tf_op | source)
XLA Modules:
  0.0 87.2 jit_solution(11116202531256286979)
XLA Ops:
  0.6 2.5 %shard_map.86 = (f32[64,512]{1,0:T(8,128)}, f32[88,512]{1,0:T(8,128)}, f32[3,2,8,512]{3,2,1,0:T(8,128)}, f32[2,8,512]{2,1,0:T(8,128)}, s32[16,128]{1,0:T(8,128)}) custom-call(f32[16,3,2,8,512]{4,3,2,1,0:T(8,128)} %refs_14_.1, f32[3,2,8,512]{3,2,1,0:T(8,128)} %reluct_hbm.1, s32[2,8,512]{2,1,0:T(8,128)} %lam_hbm.1, s32[2,8,512]{2,1,0:T(8,128)} %mag_hbm.1, ...), custom_call_target="tpu_custom_call" | custom-call | tf_op jit(solution)/shard_map/pallas_call | solution.py:396
  3.2 1.3 %collective-permute-start.1 = (f32[88,512]{1,0:T(8,128)}, f32[88,512]{1,0:T(8,128)S(1)}, u32[]{:S(2)}, u32[]{:S(2)}) collective-permute-start(f32[88,512]{1,0:T(8,128)} %get-tuple-element.30), channel_id=1, source_target_pairs={{0,1},{1,2},{2,3},{4,5},{5,6},{6,7},{8,9},{9,10},{10,11},{12,13},{... | collective-permute-start | bytes 540680 | tf_op jit(solution)/shard_map/ppermute | solution.py:38
  4.5 1.3 %collective-permute-start = (f32[64,512]{1,0:T(8,128)}, f32[64,512]{1,0:T(8,128)S(1)}, u32[]{:S(2)}, u32[]{:S(2)}) collective-permute-start(f32[64,512]{1,0:T(8,128)} %get-tuple-element.29.refs_9_), channel_id=1, source_target_pairs={{1,0},{2,1},{3,2},{5,4},{6,5},{7,6},{9,8},{10,9},{11,10},{13,12},{... | collective-permute-start | bytes 393224 | tf_op jit(solution)/shard_map/ppermute | solution.py:38
  5.8 1.4 %copy-done = f32[16,3,2,8,512]{4,3,2,1,0:T(8,128)S(1)} copy-done((f32[16,3,2,8,512]{4,3,2,1,0:T(8,128)S(1)}, f32[16,3,2,8,512]{4,3,2,1,0:T(8,128)}, u32[]{:S(2)}) %copy-start) | copy-done | bytes 1572888
  7.2 0.9 %copy-done.2 = f32[3,2,8,512]{3,2,1,0:T(8,128)S(1)} copy-done((f32[3,2,8,512]{3,2,1,0:T(8,128)S(1)}, f32[3,2,8,512]{3,2,1,0:T(8,128)}, u32[]{:S(2)}) %copy-start.2) | copy-done | bytes 98328
  8.1 0.8 copy-done.5
  8.9 1.4 %shard_map.87 = (f32[296,512]{1,0:T(8,128)}, f32[296,512]{1,0:T(8,128)}) custom-call(f32[16,3,2,8,512]{4,3,2,1,0:T(8,128)S(1)} %copy-done, f32[3,2,8,512]{3,2,1,0:T(8,128)S(1)} %copy-done.2, f32[2,8,512]{2,1,0:T(8,128)S(1)} %copy-done.5), custom_call_target="tpu_custom_call" | custom-call | flops 10000000 | bytes 3145728 | tf_op jit(solution)/shard_map/pallas_call | solution.py:408
  10.3 0.6 shard_map.88
  10.9 9.6 %collective-permute-start.2 = (f32[296,512]{1,0:T(8,128)}, f32[296,512]{1,0:T(8,128)S(1)}, u32[]{:S(2)}, u32[]{:S(2)}) collective-permute-start(f32[296,512]{1,0:T(8,128)} %get-tuple-element.34), channel_id=1, source_target_pairs={{0,124},{1,125},{2,126},{3,127},{4,8},{5,9},{6,10},{7,11},{8,4},{9... | collective-permute-start | bytes 1818632 | tf_op jit(solution)/shard_map/ppermute | solution.py:48
  20.6 0.1 broadcast_in_dim.7
  20.7 16.0 %all_to_all.6 = f32[32,1,192]{2,1,0:T(1,128)S(1)} all-to-all(f32[32,1,192]{2,1,0:T(1,128)S(1)} %broadcast_in_dim.8), channel_id=1, replica_groups=mesh['az'=32,'ax'=4] {'az'}, dimensions={0} | all-to-all | bytes 49152 | tf_op jit(solution)/shard_map/all_to_all | solution.py:428
  37.0 3.4 %shard_map.89 = (f32[16,3,2,8,512]{4,3,2,1,0:T(8,128)S(1)}, f32[272,512]{1,0:T(8,128)S(1)}, f32[272,512]{1,0:T(8,128)S(1)}, f32[80,512]{1,0:T(8,128)S(1)}, f32[6...) custom-call(f32[16,3,2,8,512]{4,3,2,1,0:T(8,128)S(1)} %copy-done.1, ...), custom_call_target="tpu_custom_call" | custom-call | tf_op jit(solution)/shard_map/pallas_call | solution.py:450
  40.4 5.6 %collective-permute-start.4 = (f32[272,512]{1,0:T(8,128)S(1)}, f32[272,512]{1,0:T(8,128)S(1)}, u32[]{:S(2)}, u32[]{:S(2)}) collective-permute-start(f32[272,512]{1,0:T(8,128)S(1)} %get-tuple-element.38), channel_id=1, source_target_pairs={{0,124},{1,125},{2,126},{3,127},{4,8},{5,9},{6,10},{7,11},{8,4},{9... | collective-permute-start | bytes 1671176 | tf_op jit(solution)/shard_map/ppermute | solution.py:48
  46.0 1.3 %collective-permute-start.6 = (f32[80,512]{1,0:T(8,128)S(1)}, f32[80,512]{1,0:T(8,128)S(1)}, u32[]{:S(2)}, u32[]{:S(2)}) collective-permute-start(f32[80,512]{1,0:T(8,128)S(1)} %get-tuple-element.40.refs_9_), channel_id=1, source_target_pairs={{1,0},{2,1},{3,2},{5,4},{6,5},{7,6},{9,8},{10,9},{11,10},{13,12},{... | collective-permute-start | bytes 491528 | tf_op jit(solution)/shard_map/ppermute | solution.py:38
  47.3 3.3 %collective-permute-start.7 = (f32[64,512]{1,0:T(8,128)S(1)}, f32[64,512]{1,0:T(8,128)S(1)}, u32[]{:S(2)}, u32[]{:S(2)}) collective-permute-start(f32[64,512]{1,0:T(8,128)S(1)} %get-tuple-element.41), channel_id=1, source_target_pairs={{0,1},{1,2},{2,3},{4,5},{5,6},{6,7},{8,9},{9,10},{10,11},{12,13},{... | collective-permute-start | bytes 393224 | tf_op jit(solution)/shard_map/ppermute | solution.py:38
  50.6 1.0 %collective-permute-done.7.refs_8_ = f32[64,512]{1,0:T(8,128)S(1)} collective-permute-done((f32[64,512]{1,0:T(8,128)S(1)}, f32[64,512]{1,0:T(8,128)S(1)}, u32[]{:S(2)}, u32[]{:S(2)}) %collective-permute-start.7) | collective-permute-done | bytes 131104 | tf_op jit(solution)/shard_map/ppermute | solution.py:38
  51.6 10.1 %collective-permute-done.4.refs_4_ = f32[272,512]{1,0:T(8,128)S(1)} collective-permute-done((f32[272,512]{1,0:T(8,128)S(1)}, f32[272,512]{1,0:T(8,128)S(1)}, u32[]{:S(2)}, u32[]{:S(2)}) %collective-permute-start.4) | collective-permute-done | bytes 557088 | tf_op jit(solution)/shard_map/ppermute | solution.py:48
  61.7 1.7 %shard_map.90 = (f32[16,3,2,8,512]{4,3,2,1,0:T(8,128)S(1)}, f32[272,512]{1,0:T(8,128)S(1)}, f32[272,512]{1,0:T(8,128)S(1)}, f32[80,512]{1,0:T(8,128)S(1)}, f32[64,512]{1,0:T(8,128)S(1)}, /*index=5*/f32[64,512]{1,0:T(8,128)S(1)}) custom-call(f32[16,3,2,8,512]{4,3,2,1,0:T(8,128)S(1)} %get-tuple-element.37.refs_0_, f32[3,2,8,512]{3,2,1,0:T(8,128)S(1)} %copy-done.3, ...), custom_call_target="tpu_custom_call" | custom-call | tf_op jit(solution)/shard_map/pallas_call | solution.py:450
  63.4 5.5 %collective-permute-start.8 = (f32[272,512]{1,0:T(8,128)S(1)}, f32[272,512]{1,0:T(8,128)S(1)}, u32[]{:S(2)}, u32[]{:S(2)}) collective-permute-start(f32[272,512]{1,0:T(8,128)S(1)} %get-tuple-element.47), channel_id=1, source_target_pairs={{0,124},{1,125},{2,126},{3,127},{4,8},{5,9},{6,10},{7,11},{8,4},{9... | collective-permute-start | bytes 1671176 | tf_op jit(solution)/shard_map/ppermute | solution.py:48
  69.0 1.3 %collective-permute-start.10 = (f32[80,512]{1,0:T(8,128)S(1)}, f32[80,512]{1,0:T(8,128)S(1)}, u32[]{:S(2)}, u32[]{:S(2)}) collective-permute-start(f32[80,512]{1,0:T(8,128)S(1)} %get-tuple-element.49.refs_9_), channel_id=1, source_target_pairs={{1,0},{2,1},{3,2},{5,4},{6,5},{7,6},{9,8},{10,9},{11,10},{13,12},{... | collective-permute-start | bytes 491528 | tf_op jit(solution)/shard_map/ppermute | solution.py:38
  70.3 3.0 %collective-permute-start.11 = (f32[64,512]{1,0:T(8,128)S(1)}, f32[64,512]{1,0:T(8,128)S(1)}, u32[]{:S(2)}, u32[]{:S(2)}) collective-permute-start(f32[64,512]{1,0:T(8,128)S(1)} %get-tuple-element.50), channel_id=1, source_target_pairs={{0,1},{1,2},{2,3},{4,5},{5,6},{6,7},{8,9},{9,10},{10,11},{12,13},{... | collective-permute-start | bytes 393224 | tf_op jit(solution)/shard_map/ppermute | solution.py:38
  73.3 1.0 %collective-permute-done.11.refs_8_ = f32[64,512]{1,0:T(8,128)S(1)} collective-permute-done((f32[64,512]{1,0:T(8,128)S(1)}, f32[64,512]{1,0:T(8,128)S(1)}, u32[]{:S(2)}, u32[]{:S(2)}) %collective-permute-start.11) | collective-permute-done | bytes 131104 | tf_op jit(solution)/shard_map/ppermute | solution.py:38
  74.3 10.5 %collective-permute-done.8.refs_4_ = f32[272,512]{1,0:T(8,128)S(1)} collective-permute-done((f32[272,512]{1,0:T(8,128)S(1)}, f32[272,512]{1,0:T(8,128)S(1)}, u32[]{:S(2)}, u32[]{:S(2)}) %collective-permute-start.8) | collective-permute-done | bytes 557088 | tf_op jit(solution)/shard_map/ppermute | solution.py:48
  84.8 2.4 %shard_map.91 = (f32[16,3,2,8,512]{4,3,2,1,0:T(8,128)}, f32[16,3,2,8,512]{4,3,2,1,0:T(8,128)}) custom-call(f32[16,3,2,8,512]{4,3,2,1,0:T(8,128)S(1)} %get-tuple-element.46.refs_0_, f32[3,2,8,512]{3,2,1,0:T(8,128)S(1)} %copy-done.3, f32[296,512]{1,0:T(8,128)S(1)} %collective-permute-done.2.refs_2_.refs_4_, ...), custom_call_target="tpu_custom_call" | custom-call | tf_op jit(solution)/shard_map/pallas_call | solution.py:450
  (30 shorter events, 0.3 us)
Async XLA Ops:
  3.2 7.1 %collective-permute-start.1 = (f32[88,512]{1,0:T(8,128)}, f32[88,512]{1,0:T(8,128)S(1)}, u32[]{:S(2)}, u32[]{:S(2)}) collective-permute-start(f32[88,512]{1,0:T(8,128)} %get-tuple-element.30), channel_id=1, source_target_pairs={{0,1},{1,2},{2,3},{4,5},{5,6},{6,7},{8,9},{9,10},{10,11},{12,13},{... | collective-permute-start | bytes 540680 | tf_op jit(solution)/shard_map/ppermute | solution.py:38
  4.5 5.8 %collective-permute-start = (f32[64,512]{1,0:T(8,128)}, f32[64,512]{1,0:T(8,128)S(1)}, u32[]{:S(2)}, u32[]{:S(2)}) collective-permute-start(f32[64,512]{1,0:T(8,128)} %get-tuple-element.29.refs_9_), channel_id=1, source_target_pairs={{1,0},{2,1},{3,2},{5,4},{6,5},{7,6},{9,8},{10,9},{11,10},{13,12},{... | collective-permute-start | bytes 393224 | tf_op jit(solution)/shard_map/ppermute | solution.py:38
  5.8 1.4 %copy-start = (f32[16,3,2,8,512]{4,3,2,1,0:T(8,128)S(1)}, f32[16,3,2,8,512]{4,3,2,1,0:T(8,128)}, u32[]{:S(2)}) copy-start(f32[16,3,2,8,512]{4,3,2,1,0:T(8,128)} %refs_14_.1) | copy-start | bytes 4718596
  7.2 0.9 %copy-start.2 = (f32[3,2,8,512]{3,2,1,0:T(8,128)S(1)}, f32[3,2,8,512]{3,2,1,0:T(8,128)}, u32[]{:S(2)}) copy-start(f32[3,2,8,512]{3,2,1,0:T(8,128)} %get-tuple-element.28.nu_ref.refs_1_) | copy-start | bytes 294916
  8.1 0.8 copy-start.5
  8.9 11.7 %copy-start.8 = (f32[3,16,4]{1,2,0:T(4,128)S(1)}, f32[3,16,4]{1,2,0:T(4,128)}, u32[]{:S(2)}) copy-start(f32[3,16,4]{1,2,0:T(4,128)} %param.12) | copy-start | bytes 2308
  8.9 28.1 %copy-start.1 = (f32[16,3,2,8,512]{4,3,2,1,0:T(8,128)S(1)}, f32[16,3,2,8,512]{4,3,2,1,0:T(8,128)}, u32[]{:S(2)}) copy-start(f32[16,3,2,8,512]{4,3,2,1,0:T(8,128)} %refs_14_.1) | copy-start | bytes 4718596
  8.9 28.1 %copy-start.3 = (f32[3,2,8,512]{3,2,1,0:T(8,128)S(1)}, f32[3,2,8,512]{3,2,1,0:T(8,128)}, u32[]{:S(2)}) copy-start(f32[3,2,8,512]{3,2,1,0:T(8,128)} %get-tuple-element.28.nu_ref.refs_1_) | copy-start | bytes 294916
  8.9 28.1 %copy-start.4 = (f32[64,512]{1,0:T(8,128)S(1)}, f32[64,512]{1,0:T(8,128)}, u32[]{:S(2)}) copy-start(f32[64,512]{1,0:T(8,128)} %get-tuple-element.29.refs_9_) | copy-start | bytes 393220
  8.9 28.1 %copy-start.6 = (f32[2,8,512]{2,1,0:T(8,128)S(1)}, f32[2,8,512]{2,1,0:T(8,128)}, u32[]{:S(2)}) copy-start(f32[2,8,512]{2,1,0:T(8,128)} %get-tuple-element.31.code_ref.refs_10_) | copy-start | bytes 98308
  8.9 28.1 %copy-start.7 = (s32[16,128]{1,0:T(8,128)S(1)}, s32[16,128]{1,0:T(8,128)}, u32[]{:S(2)}) copy-start(s32[16,128]{1,0:T(8,128)} %get-tuple-element.36.refs_11_) | copy-start | bytes 24580
  10.9 26.0 %collective-permute-start.2 = (f32[296,512]{1,0:T(8,128)}, f32[296,512]{1,0:T(8,128)S(1)}, u32[]{:S(2)}, u32[]{:S(2)}) collective-permute-start(f32[296,512]{1,0:T(8,128)} %get-tuple-element.34), channel_id=1, source_target_pairs={{0,124},{1,125},{2,126},{3,127},{4,8},{5,9},{6,10},{7,11},{8,4},{9... | collective-permute-start | bytes 1818632 | tf_op jit(solution)/shard_map/ppermute | solution.py:48
  20.5 16.4 %collective-permute-start.3 = (f32[296,512]{1,0:T(8,128)}, f32[296,512]{1,0:T(8,128)S(1)}, u32[]{:S(2)}, u32[]{:S(2)}) collective-permute-start(f32[296,512]{1,0:T(8,128)} %get-tuple-element.35), channel_id=1, source_target_pairs={{0,4},{1,5},{2,6},{3,7},{4,0},{5,1},{6,2},{7,3},{8,12},{9,13},{10,... | collective-permute-start | bytes 1818632 | tf_op jit(solution)/shard_map/ppermute | solution.py:48
  40.4 21.3 %collective-permute-start.4 = (f32[272,512]{1,0:T(8,128)S(1)}, f32[272,512]{1,0:T(8,128)S(1)}, u32[]{:S(2)}, u32[]{:S(2)}) collective-permute-start(f32[272,512]{1,0:T(8,128)S(1)} %get-tuple-element.38), channel_id=1, source_target_pairs={{0,124},{1,125},{2,126},{3,127},{4,8},{5,9},{6,10},{7,11},{8,4},{9... | collective-permute-start | bytes 1671176 | tf_op jit(solution)/shard_map/ppermute | solution.py:48
  46.0 15.7 %collective-permute-start.5 = (f32[272,512]{1,0:T(8,128)S(1)}, f32[272,512]{1,0:T(8,128)S(1)}, u32[]{:S(2)}, u32[]{:S(2)}) collective-permute-start(f32[272,512]{1,0:T(8,128)S(1)} %get-tuple-element.39), channel_id=1, source_target_pairs={{0,4},{1,5},{2,6},{3,7},{4,0},{5,1},{6,2},{7,3},{8,12},{9,13},{10,... | collective-permute-start | bytes 1671176 | tf_op jit(solution)/shard_map/ppermute | solution.py:48
  46.0 5.6 %collective-permute-start.6 = (f32[80,512]{1,0:T(8,128)S(1)}, f32[80,512]{1,0:T(8,128)S(1)}, u32[]{:S(2)}, u32[]{:S(2)}) collective-permute-start(f32[80,512]{1,0:T(8,128)S(1)} %get-tuple-element.40.refs_9_), channel_id=1, source_target_pairs={{1,0},{2,1},{3,2},{5,4},{6,5},{7,6},{9,8},{10,9},{11,10},{13,12},{... | collective-permute-start | bytes 491528 | tf_op jit(solution)/shard_map/ppermute | solution.py:38
  47.3 4.3 %collective-permute-start.7 = (f32[64,512]{1,0:T(8,128)S(1)}, f32[64,512]{1,0:T(8,128)S(1)}, u32[]{:S(2)}, u32[]{:S(2)}) collective-permute-start(f32[64,512]{1,0:T(8,128)S(1)} %get-tuple-element.41), channel_id=1, source_target_pairs={{0,1},{1,2},{2,3},{4,5},{5,6},{6,7},{8,9},{9,10},{10,11},{12,13},{... | collective-permute-start | bytes 393224 | tf_op jit(solution)/shard_map/ppermute | solution.py:38
  63.4 21.3 %collective-permute-start.8 = (f32[272,512]{1,0:T(8,128)S(1)}, f32[272,512]{1,0:T(8,128)S(1)}, u32[]{:S(2)}, u32[]{:S(2)}) collective-permute-start(f32[272,512]{1,0:T(8,128)S(1)} %get-tuple-element.47), channel_id=1, source_target_pairs={{0,124},{1,125},{2,126},{3,127},{4,8},{5,9},{6,10},{7,11},{8,4},{9... | collective-permute-start | bytes 1671176 | tf_op jit(solution)/shard_map/ppermute | solution.py:48
  69.0 15.8 %collective-permute-start.9 = (f32[272,512]{1,0:T(8,128)S(1)}, f32[272,512]{1,0:T(8,128)S(1)}, u32[]{:S(2)}, u32[]{:S(2)}) collective-permute-start(f32[272,512]{1,0:T(8,128)S(1)} %get-tuple-element.48), channel_id=1, source_target_pairs={{0,4},{1,5},{2,6},{3,7},{4,0},{5,1},{6,2},{7,3},{8,12},{9,13},{10,... | collective-permute-start | bytes 1671176 | tf_op jit(solution)/shard_map/ppermute | solution.py:48
  69.0 5.3 %collective-permute-start.10 = (f32[80,512]{1,0:T(8,128)S(1)}, f32[80,512]{1,0:T(8,128)S(1)}, u32[]{:S(2)}, u32[]{:S(2)}) collective-permute-start(f32[80,512]{1,0:T(8,128)S(1)} %get-tuple-element.49.refs_9_), channel_id=1, source_target_pairs={{1,0},{2,1},{3,2},{5,4},{6,5},{7,6},{9,8},{10,9},{11,10},{13,12},{... | collective-permute-start | bytes 491528 | tf_op jit(solution)/shard_map/ppermute | solution.py:38
  70.3 4.0 %collective-permute-start.11 = (f32[64,512]{1,0:T(8,128)S(1)}, f32[64,512]{1,0:T(8,128)S(1)}, u32[]{:S(2)}, u32[]{:S(2)}) collective-permute-start(f32[64,512]{1,0:T(8,128)S(1)} %get-tuple-element.50), channel_id=1, source_target_pairs={{0,1},{1,2},{2,3},{4,5},{5,6},{6,7},{8,9},{9,10},{10,11},{12,13},{... | collective-permute-start | bytes 393224 | tf_op jit(solution)/shard_map/ppermute | solution.py:38

commit v5 on v4

--- a/solution.py
+++ b/solution.py
@@ -48,8 +48,14 @@
     return lax.ppermute(value, ("az", "ax"), pairs)
 
 
-def by_parity(body, far, near):
-    parity = lax.rem(lax.axis_index("az"), 2)
+def swapped_ax(value, odd):
+    count = lax.axis_size("ax")
+    pairs = [(q, q + (1 if q % 2 == odd else -1)) for q in range(count)]
+    return lax.ppermute(value, "ax", [(q, to) for q, to in pairs if 0 <= to < count])
+
+
+def by_parity(axis, body, far, near):
+    parity = lax.rem(lax.axis_index(axis), 2)
 
     @pl.when(parity == 0)
     def _():
@@ -121,7 +127,7 @@
 
 def edge_kernel(
     per, a_hbm, reluct_hbm, lam_hbm, mag_hbm, reg_hbm, slots_hbm,
-    ax_minus, ax_plus, nu_ref, code_ref, offset_ref,
+    ax_far, ax_near, nu_ref, code_ref, offset_ref,
     a_ref, lam_ref, mag_ref, reg_ref, slots_ref, sems,
 ):
     devs = a_ref.shape[0]
@@ -151,62 +157,90 @@
     offset_ref[...] = row * (3 * devs * per) + (slots - row * per)
     for i in range(2):
         nu_ref[1, i] = nu_ref[1, i] * (1.0 + 3.0 * lam_ref[i].astype(jnp.float32))
-        code_ref[i] = jnp.where(mag_ref[i] == 1, reg_ref[i] - base + 1, 0).astype(jnp.float32)
-    for i in range(2):
-        at = 5 * devs + i
-        ax_plus[pl.ds(at, 1)] = nu_ref[0, i, top:]
-        ax_plus[pl.ds(at + 2, 1)] = nu_ref[2, i, top:]
-        ax_plus[pl.ds(at + 4, 1)] = code_ref[i, top:]
-        ax_plus[pl.ds(at + 6, 1)] = jnp.zeros_like(code_ref[i, top:])
-
+        code_ref[i] = jnp.where(mag_ref[i] == 1, reg_ref[i] - base, -1).astype(jnp.float32)
     for part in range(parts):
         copies[5 + part].wait()
 
-        @pl.loop(part * some, (part + 1) * some, unroll=UNROLL)
+    def body(ax_plus, ax_minus):
+        for i in range(2):
+            at = 5 * devs + i
+            ax_plus[pl.ds(at, 1)] = nu_ref[0, i, top:]
+            ax_plus[pl.ds(at + 2, 1)] = nu_ref[2, i, top:]
+            ax_plus[pl.ds(at + 4, 1)] = code_ref[i, top:]
+            ax_plus[pl.ds(at + 6, 1)] = jnp.zeros_like(code_ref[i, top:])
+
+        @pl.loop(0, devs, unroll=UNROLL)
         def _(d):
             a = [[a_ref[d, c, i] for i in range(2)] for c in range(3)]
             pack_ax(d, devs, a, ax_minus, ax_plus)
             ax_plus[pl.ds(4 * devs + d, 1)] = a[1][0][top:]
 
-
-def plane_kernel(a_ref, nu_ref, code_ref, far, near):
+    by_parity("ax", body, ax_far, ax_near)
+
+
+def plane_kernel(a_ref, far, near):
     devs, height = a_ref.shape[0], a_ref.shape[3]
-    end = 2 * devs * height + devs
 
     def body(plus, minus):
-        plus[pl.ds(end, height)] = nu_ref[1, 1]
-        plus[pl.ds(end + height, height)] = nu_ref[2, 1]
-        plus[pl.ds(end + 2 * height, height)] = code_ref[1]
-
         @pl.loop(0, devs, unroll=UNROLL)
         def _(d):
             a = [[a_ref[d, c, i] for i in range(2)] for c in range(3)]
             pack_az(d, height, a, minus, plus)
 
-    by_parity(body, far, near)
-
-
-def corner_kernel(end, devs, ax_ahead, ax_behind, far_in, near_in, far, near, sems):
+    by_parity("az", body, far, near)
+
+
+def corner_kernel(end, devs, ax_far, ax_near, nu, code, far_in, near_in, far, near, sems):
     at = pl.ds(end, devs)
-
-    def body(plus, minus):
-        copies = [
-            pltpu.make_async_copy(ax_behind.at[pl.ds(4 * devs, devs)], minus.at[at], sems.at[0]),
-            pltpu.make_async_copy(ax_ahead.at[pl.ds(devs, devs)], plus.at[at], sems.at[1]),
-        ]
-        for copy in copies:
-            copy.start()
-        for copy in copies:
-            copy.wait()
-
-    by_parity(body, far, near)
-
-
-def picked(code, values):
-    out = jnp.zeros_like(code)
-    for k, value in enumerate(values):
-        out = jnp.where(code == k + 1.0, value, out)
-    return out
+    height = nu.shape[2]
+
+    def body_ax(ax_ahead, ax_behind):
+        def body(plus, minus):
+            copies = [
+                (ax_behind.at[pl.ds(4 * devs, devs)], minus.at[at]),
+                (ax_ahead.at[pl.ds(devs, devs)], plus.at[at]),
+            ]
+            for k, source in enumerate((nu.at[1, 1], nu.at[2, 1], code.at[1])):
+                copies.append((source, plus.at[pl.ds(end + devs + k * height, height)]))
+            copies = [
+                pltpu.make_async_copy(source, to, sems.at[k]) for k, (source, to) in enumerate(copies)
+            ]
+            for copy in copies:
+                copy.start()
+            for copy in copies:
+                copy.wait()
+
+        by_parity("az", body, far, near)
+
+    by_parity("ax", body_ax, ax_far, ax_near)
+
+
+def settle_kernel(halo_far, halo_near, a_ref, ahead, behind, minus):
+    devs = a_ref.shape[0]
+
+    def body(ahead_ref, behind_ref):
+        ahead[...] = ahead_ref[pl.ds(0, ahead.shape[0])]
+        behind[...] = behind_ref[...]
+
+    by_parity("ax", body, halo_far, halo_near)
+    for d in range(devs):
+        for i in range(2):
+            minus[i * devs + d : i * devs + d + 1] = a_ref[d, 0, i, 0:1]
+            minus[(2 + i) * devs + d : (2 + i) * devs + d + 1] = a_ref[d, 2, i, 0:1]
+
+
+def picked(nu, code, values):
+    rest, weight = code, 1
+    while weight < len(values):
+        weight *= 2
+    values = list(values) + [values[-1]] * (weight - len(values))
+    while len(values) > 1:
+        weight //= 2
+        high = rest > weight - 0.5
+        rest = jnp.where(high, rest - weight, rest)
+        half = len(values) // 2
+        values = [jnp.where(high, b, a) for a, b in zip(values[:half], values[half:])]
+    return jnp.where(code > -0.5, nu * values[0], 0.0)
 
 
 def advanced(stage, value, start, curl):
@@ -231,7 +265,7 @@
     def body(plus, minus):
         step_body(stage, per, refs, plus, minus)
 
-    by_parity(body, (halo[0], statics[0], sent[0]), (halo[1], statics[1], sent[1]))
+    by_parity("az", body, (halo[0], statics[0], sent[0]), (halo[1], statics[1], sent[1]))
 
 
 def step_body(stage, per, refs, beyond_refs, behind_refs):
@@ -258,7 +292,8 @@
         final_hbm = next(it)
     edge, corner = next(it), next(it)
     if stage == 2:
-        leave = pltpu.make_async_copy(a_ref, final_hbm, next(it))
+        res_hbm, out_ref, sems = out_ref, next(it), next(it)
+        leave = pltpu.make_async_copy(a_ref, final_hbm, sems.at[0])
         leave.start()
     devs, height = a_ref.shape[0], a_ref.shape[3]
     top = height - 1
@@ -291,8 +326,8 @@
             for c in (0, 2):
                 own = values(d, c, per)
                 for i in range(2):
-                    src_ax_ref[pl.ds((c + i) * devs + d, 1)] = nu_ax_ref[pl.ds(nu_ax + c + i, 1)] * picked(
-                        nu_ax_ref[pl.ds(nu_ax + 4 + i, 1)], own
+                    src_ax_ref[pl.ds((c + i) * devs + d, 1)] = picked(
+                        nu_ax_ref[pl.ds(nu_ax + c + i, 1)], nu_ax_ref[pl.ds(nu_ax + 4 + i, 1)], own
                     )
 
     for at, own, sign in ((0, 2, 1.0), (1, 3, 1.0), (2, 0, -1.0), (3, 1, -1.0)):
@@ -325,7 +360,7 @@
             )
             for c in range(3):
                 if stage == 0:
-                    src = nu_ref[c, i] * picked(code_ref[i], own[c])
+                    src = picked(nu_ref[c, i], code_ref[i], own[c])
                     src_ref[d, c, i] = src
                 else:
                     src = src_ref[d, c, i]
@@ -333,8 +368,10 @@
         back_src = [None, None]
         for c in range(1, 3):
             if stage == 0:
-                src = nu_az_ref[block(2 * devs + 1 + c, height)] * picked(
-                    nu_az_ref[pl.ds(nu_az + 2 * height, height)], values(d, c, 0)
+                src = picked(
+                    nu_az_ref[pl.ds(nu_az + (c - 1) * height, height)],
+                    nu_az_ref[pl.ds(nu_az + 2 * height, height)],
+                    values(d, c, 0),
                 )
                 src_az_ref[2 * d + c - 1] = src
             else:
@@ -364,6 +401,8 @@
                 value = advanced(stage, a[c][i], start, curl[c])
                 out_ref[d, c, i] = value
                 new[c][i] = value
+        if stage == 2:
+            pltpu.make_async_copy(out_ref.at[d], res_hbm.at[d], sems.at[1]).start()
         if stage < 2:
             first1, first2 = back1[0:1], back2[0:1]
             ax_minus[pl.ds(4 * devs + d, 1)] = first2 - (first1 - radial_prev(first1))
@@ -373,6 +412,7 @@
 
     if stage == 2:
         leave.wait()
+        pltpu.make_async_copy(out_ref, res_hbm, sems.at[1]).wait()
 
 
 def f32(*shape):
@@ -387,13 +427,13 @@
 
     field_like = f32(*start_field.shape)
     edges = [
-        f32(4 * devs, radial),
+        f32(5 * devs + 8, radial),
         f32(5 * devs + 8, radial),
         f32(*reluctivity.shape),
         f32(*lamination.shape),
         jax.ShapeDtypeStruct(slot_map.shape, jnp.int32),
     ]
-    ax_minus, ax_plus, nu, code, offset = pl.pallas_call(
+    ax_far, ax_near, nu, code, offset = pl.pallas_call(
         functools.partial(edge_kernel, per),
         out_shape=edges,
         in_specs=[HBM] * 6,
@@ -403,25 +443,32 @@
         + [pltpu.VMEM(slot_map.shape, jnp.int32), pltpu.SemaphoreType.DMA((7,))],
         compiler_params=pltpu.CompilerParams(vmem_limit_bytes=LIMIT_FIRST),
     )(start_field, reluctivity, lamination, magnets, region_ids, slot_map)
-    ax_ahead, ax_behind = moved(ax_minus, 0, -1), moved(ax_plus, 0, 1)
+    ax_halos = swapped_ax(ax_far, 1), swapped_ax(ax_near, 0)
     planes = [f32(whole + devs + 3 * cells_ax, radial)] * 2
     packed = pl.pallas_call(
         plane_kernel,
         out_shape=planes,
-        in_specs=[VMEM] * 3,
+        in_specs=[VMEM],
         out_specs=[VMEM] * 2,
         compiler_params=pltpu.CompilerParams(vmem_limit_bytes=LIMIT),
         cost_estimate=pl.CostEstimate(flops=10**7, bytes_accessed=3 * MIB, transcendentals=0),
-    )(start_field, nu, code)
+    )(start_field)
     far, near = pl.pallas_call(
         functools.partial(corner_kernel, whole, devs),
         out_shape=planes,
-        in_specs=[VMEM, VMEM, ANY, ANY],
+        in_specs=[VMEM, VMEM, ANY, ANY, ANY, ANY],
         out_specs=[ANY] * 2,
-        scratch_shapes=[pltpu.SemaphoreType.DMA((2,))],
-        input_output_aliases={2: 0, 3: 1},
+        scratch_shapes=[pltpu.SemaphoreType.DMA((5,))],
+        input_output_aliases={4: 0, 5: 1},
         compiler_params=pltpu.CompilerParams(vmem_limit_bytes=LIMIT),
-    )(ax_ahead, ax_behind, *packed)
+    )(*ax_halos, nu, code, *packed)
+    ax_ahead, ax_behind, ax_minus = pl.pallas_call(
+        settle_kernel,
+        out_shape=[f32(4 * devs, radial), f32(5 * devs + 8, radial), f32(4 * devs, radial)],
+        in_specs=[VMEM] * 3,
+        out_specs=[VMEM] * 3,
+        compiler_params=pltpu.CompilerParams(vmem_limit_bytes=LIMIT),
+    )(*ax_halos, start_field)
     far_halo, near_halo = swapped(far, 1), swapped(near, 0)
     halos = (far_halo, near_halo, ax_ahead, ax_behind, ax_minus)
     flat = pieces.reshape(1, comps * devs * per)
@@ -451,12 +498,12 @@
             functools.partial(step_kernel, stage, per),
             out_shape=outs,
             in_specs=[VMEM] * 10 + more_specs,
-            out_specs=[VMEM] * len(outs) if stage < 2 else [VMEM, HBM],
+            out_specs=[VMEM if stage < 2 else HBM] * len(outs),
             scratch_shapes=[
                 pltpu.VMEM((4 * devs, radial), jnp.float32),
                 pltpu.VMEM((2 * devs, radial), jnp.float32),
             ]
-            + [pltpu.SemaphoreType.DMA] * (stage // 2),
+            + [pltpu.VMEM(start_field.shape, jnp.float32), pltpu.SemaphoreType.DMA((2,))] * (stage // 2),
             compiler_params=pltpu.CompilerParams(vmem_limit_bytes=LIMIT),
         )(field, nu, far_halo, near_halo, *halos[:2], ax_behind, *halos[2:], *more)
 

time: 87.6 us -> 86.8 us (level)
  waiting for transfers between devices: 22.5 us -> 20.2 us
  starting transfers between devices: 32.2 us -> 33.6 us
    ppermute x0 -> x2, starting transfers between devices: none -> 3.68 us  [swapped_ax(): lax.ppermute(value, 'ax', [(q, to) for q, to in pairs if 0 <= to < count])]
    ppermute x6 -> x4, starting transfers between devices: 11.5 us -> 8.64 us  [moved(): return lax.ppermute(value, ('az', 'ax'), pairs)]
    ppermute x6, waiting for transfers between devices: 20.6 us -> 18.3 us  [swapped(): return lax.ppermute(value, ('az', 'ax'), pairs)]
    ppermute x6 -> x4, waiting for transfers between devices: 1.93 us -> 1.93 us  [moved(): return lax.ppermute(value, ('az', 'ax'), pairs)]
    unnamed x19 -> x17, local copies, waits for them, and re-layouts: 3.17 us -> 3.17 us
where the time goes in v5:
time: 86.8 us; the launch traced here: 86.4 us
  starting transfers between devices  33.6 us (39%)
  waiting for transfers between devices  20.2 us (23%)
  blocking collectives  16.4 us (19%)
  Pallas kernels  11.9 us (14%)
  local copies, waits for them, and re-layouts  3.37 us (4%)
    ppermute x6, starting transfers between devices, swapped(): return lax.ppermute(value, ('az', 'ax'), pairs)  21.3 us
    ppermute x6, waiting for transfers between devices, swapped(): return lax.ppermute(value, ('az', 'ax'), pairs)  18.3 us
    all_to_all x1, blocking collectives, shards(): lax.all_to_all(jnp.broadcast_to(flat, (count_az, comps * devs * per)), 'a...  16.4 us
    ppermute x4, starting transfers between devices, moved(): return lax.ppermute(value, ('az', 'ax'), pairs)  8.64 us
    pallas_call x3, Pallas kernels, step(): pl.pallas_call(functools.partial(step_kernel, stage, per), out_shape=outs...  6.98 us
    ppermute x2, starting transfers between devices, swapped_ax(): lax.ppermute(value, 'ax', [(q, to) for q, to in pairs if 0 <= to < count])  3.68 us
    unnamed x17, local copies, waits for them, and re-layouts  3.17 us
    pallas_call x1, Pallas kernels, shards(): pl.pallas_call(functools.partial(edge_kernel, per), out_shape=edges, in_s...  2.83 us
  transfers between devices with their start and end apart: 12, of which 4 were waited for; matrix products, arithmetic and copies ran while one was open for 0% of the time, Pallas kernels for 2%

profile of v5, /device:TPU:0, one launch (start us, length us, event | category | flops | bytes accessed | tf_op | source)
XLA Modules:
  0.0 86.4 jit_solution(418324463764034408)
XLA Ops:
  0.6 2.8 %shard_map.86 = (f32[88,512]{1,0:T(8,128)}, f32[88,512]{1,0:T(8,128)}, f32[3,2,8,512]{3,2,1,0:T(8,128)}, f32[2,8,512]{2,1,0:T(8,128)}, s32[16,128]{1,0:T(8,128)}) custom-call(f32[16,3,2,8,512]{4,3,2,1,0:T(8,128)} %refs_14_.1, f32[3,2,8,512]{3,2,1,0:T(8,128)} %reluct_hbm.1, s32[2,8,512]{2,1,0:T(8,128)} %lam_hbm.1, s32[2,8,512]{2,1,0:T(8,128)} %mag_hbm.1, ...), custom_call_target="tpu_custom_call" | custom-call | tf_op jit(solution)/shard_map/pallas_call | solution.py:436
  3.5 0.7 collective-permute-start
  4.2 3.0 %collective-permute-start.1 = (f32[88,512]{1,0:T(8,128)}, f32[88,512]{1,0:T(8,128)S(1)}, u32[]{:S(2)}, u32[]{:S(2)}) collective-permute-start(f32[88,512]{1,0:T(8,128)} %get-tuple-element.33), channel_id=1, source_target_pairs={{0,1},{1,0},{2,3},{3,2},{4,5},{5,4},{6,7},{7,6},{8,9},{9,8},{10,11... | collective-permute-start | bytes 540680 | tf_op jit(solution)/shard_map/ppermute | solution.py:54
  7.2 1.4 %copy-done = f32[16,3,2,8,512]{4,3,2,1,0:T(8,128)S(1)} copy-done((f32[16,3,2,8,512]{4,3,2,1,0:T(8,128)S(1)}, f32[16,3,2,8,512]{4,3,2,1,0:T(8,128)}, u32[]{:S(2)}) %copy-start) | copy-done | bytes 1572888
  8.6 1.4 %shard_map.87 = (f32[296,512]{1,0:T(8,128)}, f32[296,512]{1,0:T(8,128)}) custom-call(f32[16,3,2,8,512]{4,3,2,1,0:T(8,128)S(1)} %copy-done), custom_call_target="tpu_custom_call" | custom-call | flops 10000000 | bytes 3145728 | tf_op jit(solution)/shard_map/pallas_call | solution.py:448
  10.0 0.9 %copy-done.2 = f32[3,2,8,512]{3,2,1,0:T(8,128)S(1)} copy-done((f32[3,2,8,512]{3,2,1,0:T(8,128)S(1)}, f32[3,2,8,512]{3,2,1,0:T(8,128)}, u32[]{:S(2)}) %copy-start.2) | copy-done | bytes 98328
  10.9 0.8 copy-done.4
  11.6 0.7 shard_map.88
  12.3 8.7 %collective-permute-start.2 = (f32[296,512]{1,0:T(8,128)}, f32[296,512]{1,0:T(8,128)S(1)}, u32[]{:S(2)}, u32[]{:S(2)}) collective-permute-start(f32[296,512]{1,0:T(8,128)} %get-tuple-element.37), channel_id=1, source_target_pairs={{0,124},{1,125},{2,126},{3,127},{4,8},{5,9},{6,10},{7,11},{8,4},{9... | collective-permute-start | bytes 1818632 | tf_op jit(solution)/shard_map/ppermute | solution.py:48
  21.1 0.1 broadcast_in_dim.7
  21.3 16.4 %all_to_all.6 = f32[32,1,192]{2,1,0:T(1,128)S(1)} all-to-all(f32[32,1,192]{2,1,0:T(1,128)S(1)} %broadcast_in_dim.8), channel_id=1, replica_groups=mesh['az'=32,'ax'=4] {'az'}, dimensions={0} | all-to-all | bytes 49152 | tf_op jit(solution)/shard_map/all_to_all | solution.py:475
  38.0 3.4 %shard_map.90 = (f32[16,3,2,8,512]{4,3,2,1,0:T(8,128)S(1)}, f32[272,512]{1,0:T(8,128)S(1)}, f32[272,512]{1,0:T(8,128)S(1)}, f32[80,512]{1,0:T(8,128)S(1)}, f32[6...) custom-call(f32[16,3,2,8,512]{4,3,2,1,0:T(8,128)S(1)} %copy-done.1, ...), custom_call_target="tpu_custom_call" | custom-call | tf_op jit(solution)/shard_map/pallas_call | solution.py:497
  41.4 6.3 %collective-permute-start.4 = (f32[272,512]{1,0:T(8,128)S(1)}, f32[272,512]{1,0:T(8,128)S(1)}, u32[]{:S(2)}, u32[]{:S(2)}) collective-permute-start(f32[272,512]{1,0:T(8,128)S(1)} %get-tuple-element.44), channel_id=1, source_target_pairs={{0,124},{1,125},{2,126},{3,127},{4,8},{5,9},{6,10},{7,11},{8,4},{9... | collective-permute-start | bytes 1671176 | tf_op jit(solution)/shard_map/ppermute | solution.py:48
  47.7 1.3 %collective-permute-start.6 = (f32[80,512]{1,0:T(8,128)S(1)}, f32[80,512]{1,0:T(8,128)S(1)}, u32[]{:S(2)}, u32[]{:S(2)}) collective-permute-start(f32[80,512]{1,0:T(8,128)S(1)} %get-tuple-element.46.refs_9_), channel_id=1, source_target_pairs={{1,0},{2,1},{3,2},{5,4},{6,5},{7,6},{9,8},{10,9},{11,10},{13,12},{... | collective-permute-start | bytes 491528 | tf_op jit(solution)/shard_map/ppermute | solution.py:38
  49.0 3.0 %collective-permute-start.7 = (f32[64,512]{1,0:T(8,128)S(1)}, f32[64,512]{1,0:T(8,128)S(1)}, u32[]{:S(2)}, u32[]{:S(2)}) collective-permute-start(f32[64,512]{1,0:T(8,128)S(1)} %get-tuple-element.47), channel_id=1, source_target_pairs={{0,1},{1,2},{2,3},{4,5},{5,6},{6,7},{8,9},{9,10},{10,11},{12,13},{... | collective-permute-start | bytes 393224 | tf_op jit(solution)/shard_map/ppermute | solution.py:38
  52.0 1.0 %collective-permute-done.7.refs_8_ = f32[64,512]{1,0:T(8,128)S(1)} collective-permute-done((f32[64,512]{1,0:T(8,128)S(1)}, f32[64,512]{1,0:T(8,128)S(1)}, u32[]{:S(2)}, u32[]{:S(2)}) %collective-permute-start.7) | collective-permute-done | bytes 131104 | tf_op jit(solution)/shard_map/ppermute | solution.py:38
  53.0 9.8 %collective-permute-done.4.refs_4_ = f32[272,512]{1,0:T(8,128)S(1)} collective-permute-done((f32[272,512]{1,0:T(8,128)S(1)}, f32[272,512]{1,0:T(8,128)S(1)}, u32[]{:S(2)}, u32[]{:S(2)}) %collective-permute-start.4) | collective-permute-done | bytes 557088 | tf_op jit(solution)/shard_map/ppermute | solution.py:48
  62.8 1.7 %shard_map.91 = (f32[16,3,2,8,512]{4,3,2,1,0:T(8,128)S(1)}, f32[272,512]{1,0:T(8,128)S(1)}, f32[272,512]{1,0:T(8,128)S(1)}, f32[80,512]{1,0:T(8,128)S(1)}, f32[64,512]{1,0:T(8,128)S(1)}, /*index=5*/f32[64,512]{1,0:T(8,128)S(1)}) custom-call(f32[16,3,2,8,512]{4,3,2,1,0:T(8,128)S(1)} %get-tuple-element.43.refs_0_, f32[3,2,8,512]{3,2,1,0:T(8,128)S(1)} %copy-done.3, ...), custom_call_target="tpu_custom_call" | custom-call | tf_op jit(solution)/shard_map/pallas_call | solution.py:497
  64.5 6.3 %collective-permute-start.8 = (f32[272,512]{1,0:T(8,128)S(1)}, f32[272,512]{1,0:T(8,128)S(1)}, u32[]{:S(2)}, u32[]{:S(2)}) collective-permute-start(f32[272,512]{1,0:T(8,128)S(1)} %get-tuple-element.53), channel_id=1, source_target_pairs={{0,124},{1,125},{2,126},{3,127},{4,8},{5,9},{6,10},{7,11},{8,4},{9... | collective-permute-start | bytes 1671176 | tf_op jit(solution)/shard_map/ppermute | solution.py:48
  70.7 1.3 %collective-permute-start.10 = (f32[80,512]{1,0:T(8,128)S(1)}, f32[80,512]{1,0:T(8,128)S(1)}, u32[]{:S(2)}, u32[]{:S(2)}) collective-permute-start(f32[80,512]{1,0:T(8,128)S(1)} %get-tuple-element.55.refs_9_), channel_id=1, source_target_pairs={{1,0},{2,1},{3,2},{5,4},{6,5},{7,6},{9,8},{10,9},{11,10},{13,12},{... | collective-permute-start | bytes 491528 | tf_op jit(solution)/shard_map/ppermute | solution.py:38
  72.0 3.0 %collective-permute-start.11 = (f32[64,512]{1,0:T(8,128)S(1)}, f32[64,512]{1,0:T(8,128)S(1)}, u32[]{:S(2)}, u32[]{:S(2)}) collective-permute-start(f32[64,512]{1,0:T(8,128)S(1)} %get-tuple-element.56), channel_id=1, source_target_pairs={{0,1},{1,2},{2,3},{4,5},{5,6},{6,7},{8,9},{9,10},{10,11},{12,13},{... | collective-permute-start | bytes 393224 | tf_op jit(solution)/shard_map/ppermute | solution.py:38
  75.1 1.0 %collective-permute-done.11.refs_8_ = f32[64,512]{1,0:T(8,128)S(1)} collective-permute-done((f32[64,512]{1,0:T(8,128)S(1)}, f32[64,512]{1,0:T(8,128)S(1)}, u32[]{:S(2)}, u32[]{:S(2)}) %collective-permute-start.11) | collective-permute-done | bytes 131104 | tf_op jit(solution)/shard_map/ppermute | solution.py:38
  76.0 8.5 %collective-permute-done.8.refs_4_ = f32[272,512]{1,0:T(8,128)S(1)} collective-permute-done((f32[272,512]{1,0:T(8,128)S(1)}, f32[272,512]{1,0:T(8,128)S(1)}, u32[]{:S(2)}, u32[]{:S(2)}) %collective-permute-start.8) | collective-permute-done | bytes 557088 | tf_op jit(solution)/shard_map/ppermute | solution.py:48
  84.5 1.8 %shard_map.92 = (f32[16,3,2,8,512]{4,3,2,1,0:T(8,128)}, f32[16,3,2,8,512]{4,3,2,1,0:T(8,128)}) custom-call(f32[16,3,2,8,512]{4,3,2,1,0:T(8,128)S(1)} %get-tuple-element.52.refs_0_, f32[3,2,8,512]{3,2,1,0:T(8,128)S(1)} %copy-done.3, f32[296,512]{1,0:T(8,128)S(1)} %collective-permute-done.2.refs_2_.refs_4_, ...), custom_call_target="tpu_custom_call" | custom-call | tf_op jit(solution)/shard_map/pallas_call | solution.py:497
  (29 shorter events, 0.4 us)
Async XLA Ops:
  3.5 6.5 %collective-permute-start = (f32[88,512]{1,0:T(8,128)}, f32[88,512]{1,0:T(8,128)S(1)}, u32[]{:S(2)}, u32[]{:S(2)}) collective-permute-start(f32[88,512]{1,0:T(8,128)} %get-tuple-element.32), channel_id=1, source_target_pairs={{1,2},{2,1},{5,6},{6,5},{9,10},{10,9},{13,14},{14,13},{17,18},{18,... | collective-permute-start | bytes 540680 | tf_op jit(solution)/shard_map/ppermute | solution.py:54
  4.2 5.8 %collective-permute-start.1 = (f32[88,512]{1,0:T(8,128)}, f32[88,512]{1,0:T(8,128)S(1)}, u32[]{:S(2)}, u32[]{:S(2)}) collective-permute-start(f32[88,512]{1,0:T(8,128)} %get-tuple-element.33), channel_id=1, source_target_pairs={{0,1},{1,0},{2,3},{3,2},{4,5},{5,4},{6,7},{7,6},{8,9},{9,8},{10,11... | collective-permute-start | bytes 540680 | tf_op jit(solution)/shard_map/ppermute | solution.py:54
  7.2 1.4 %copy-start = (f32[16,3,2,8,512]{4,3,2,1,0:T(8,128)S(1)}, f32[16,3,2,8,512]{4,3,2,1,0:T(8,128)}, u32[]{:S(2)}) copy-start(f32[16,3,2,8,512]{4,3,2,1,0:T(8,128)} %refs_14_.1) | copy-start | bytes 4718596
  8.6 12.5 %copy-start.7 = (f32[3,16,4]{1,2,0:T(4,128)S(1)}, f32[3,16,4]{1,2,0:T(4,128)}, u32[]{:S(2)}) copy-start(f32[3,16,4]{1,2,0:T(4,128)} %param.12) | copy-start | bytes 2308
  8.6 29.3 %copy-start.1 = (f32[16,3,2,8,512]{4,3,2,1,0:T(8,128)S(1)}, f32[16,3,2,8,512]{4,3,2,1,0:T(8,128)}, u32[]{:S(2)}) copy-start(f32[16,3,2,8,512]{4,3,2,1,0:T(8,128)} %refs_14_.1) | copy-start | bytes 4718596
  10.0 0.9 %copy-start.2 = (f32[3,2,8,512]{3,2,1,0:T(8,128)S(1)}, f32[3,2,8,512]{3,2,1,0:T(8,128)}, u32[]{:S(2)}) copy-start(f32[3,2,8,512]{3,2,1,0:T(8,128)} %get-tuple-element.31.nu.refs_1_) | copy-start | bytes 294916
  10.8 0.8 copy-start.4
  11.6 26.4 %copy-start.3 = (f32[3,2,8,512]{3,2,1,0:T(8,128)S(1)}, f32[3,2,8,512]{3,2,1,0:T(8,128)}, u32[]{:S(2)}) copy-start(f32[3,2,8,512]{3,2,1,0:T(8,128)} %get-tuple-element.31.nu.refs_1_) | copy-start | bytes 294916
  11.6 26.4 %copy-start.5 = (f32[2,8,512]{2,1,0:T(8,128)S(1)}, f32[2,8,512]{2,1,0:T(8,128)}, u32[]{:S(2)}) copy-start(f32[2,8,512]{2,1,0:T(8,128)} %get-tuple-element.34.code.refs_10_) | copy-start | bytes 98308
  11.6 26.4 %copy-start.6 = (s32[16,128]{1,0:T(8,128)S(1)}, s32[16,128]{1,0:T(8,128)}, u32[]{:S(2)}) copy-start(s32[16,128]{1,0:T(8,128)} %get-tuple-element.42.refs_11_) | copy-start | bytes 24580
  12.3 25.6 %collective-permute-start.2 = (f32[296,512]{1,0:T(8,128)}, f32[296,512]{1,0:T(8,128)S(1)}, u32[]{:S(2)}, u32[]{:S(2)}) collective-permute-start(f32[296,512]{1,0:T(8,128)} %get-tuple-element.37), channel_id=1, source_target_pairs={{0,124},{1,125},{2,126},{3,127},{4,8},{5,9},{6,10},{7,11},{8,4},{9... | collective-permute-start | bytes 1818632 | tf_op jit(solution)/shard_map/ppermute | solution.py:48
  21.0 16.9 %collective-permute-start.3 = (f32[296,512]{1,0:T(8,128)}, f32[296,512]{1,0:T(8,128)S(1)}, u32[]{:S(2)}, u32[]{:S(2)}) collective-permute-start(f32[296,512]{1,0:T(8,128)} %get-tuple-element.38), channel_id=1, source_target_pairs={{0,4},{1,5},{2,6},{3,7},{4,0},{5,1},{6,2},{7,3},{8,12},{9,13},{10,... | collective-permute-start | bytes 1818632 | tf_op jit(solution)/shard_map/ppermute | solution.py:48
  41.4 21.3 %collective-permute-start.4 = (f32[272,512]{1,0:T(8,128)S(1)}, f32[272,512]{1,0:T(8,128)S(1)}, u32[]{:S(2)}, u32[]{:S(2)}) collective-permute-start(f32[272,512]{1,0:T(8,128)S(1)} %get-tuple-element.44), channel_id=1, source_target_pairs={{0,124},{1,125},{2,126},{3,127},{4,8},{5,9},{6,10},{7,11},{8,4},{9... | collective-permute-start | bytes 1671176 | tf_op jit(solution)/shard_map/ppermute | solution.py:48
  47.7 15.1 %collective-permute-start.5 = (f32[272,512]{1,0:T(8,128)S(1)}, f32[272,512]{1,0:T(8,128)S(1)}, u32[]{:S(2)}, u32[]{:S(2)}) collective-permute-start(f32[272,512]{1,0:T(8,128)S(1)} %get-tuple-element.45), channel_id=1, source_target_pairs={{0,4},{1,5},{2,6},{3,7},{4,0},{5,1},{6,2},{7,3},{8,12},{9,13},{10,... | collective-permute-start | bytes 1671176 | tf_op jit(solution)/shard_map/ppermute | solution.py:48
  47.7 5.3 %collective-permute-start.6 = (f32[80,512]{1,0:T(8,128)S(1)}, f32[80,512]{1,0:T(8,128)S(1)}, u32[]{:S(2)}, u32[]{:S(2)}) collective-permute-start(f32[80,512]{1,0:T(8,128)S(1)} %get-tuple-element.46.refs_9_), channel_id=1, source_target_pairs={{1,0},{2,1},{3,2},{5,4},{6,5},{7,6},{9,8},{10,9},{11,10},{13,12},{... | collective-permute-start | bytes 491528 | tf_op jit(solution)/shard_map/ppermute | solution.py:38
  49.0 4.0 %collective-permute-start.7 = (f32[64,512]{1,0:T(8,128)S(1)}, f32[64,512]{1,0:T(8,128)S(1)}, u32[]{:S(2)}, u32[]{:S(2)}) collective-permute-start(f32[64,512]{1,0:T(8,128)S(1)} %get-tuple-element.47), channel_id=1, source_target_pairs={{0,1},{1,2},{2,3},{4,5},{5,6},{6,7},{8,9},{9,10},{10,11},{12,13},{... | collective-permute-start | bytes 393224 | tf_op jit(solution)/shard_map/ppermute | solution.py:38
  64.5 20.0 %collective-permute-start.8 = (f32[272,512]{1,0:T(8,128)S(1)}, f32[272,512]{1,0:T(8,128)S(1)}, u32[]{:S(2)}, u32[]{:S(2)}) collective-permute-start(f32[272,512]{1,0:T(8,128)S(1)} %get-tuple-element.53), channel_id=1, source_target_pairs={{0,124},{1,125},{2,126},{3,127},{4,8},{5,9},{6,10},{7,11},{8,4},{9... | collective-permute-start | bytes 1671176 | tf_op jit(solution)/shard_map/ppermute | solution.py:48
  70.7 13.8 %collective-permute-start.9 = (f32[272,512]{1,0:T(8,128)S(1)}, f32[272,512]{1,0:T(8,128)S(1)}, u32[]{:S(2)}, u32[]{:S(2)}) collective-permute-start(f32[272,512]{1,0:T(8,128)S(1)} %get-tuple-element.54), channel_id=1, source_target_pairs={{0,4},{1,5},{2,6},{3,7},{4,0},{5,1},{6,2},{7,3},{8,12},{9,13},{10,... | collective-permute-start | bytes 1671176 | tf_op jit(solution)/shard_map/ppermute | solution.py:48
  70.7 5.3 %collective-permute-start.10 = (f32[80,512]{1,0:T(8,128)S(1)}, f32[80,512]{1,0:T(8,128)S(1)}, u32[]{:S(2)}, u32[]{:S(2)}) collective-permute-start(f32[80,512]{1,0:T(8,128)S(1)} %get-tuple-element.55.refs_9_), channel_id=1, source_target_pairs={{1,0},{2,1},{3,2},{5,4},{6,5},{7,6},{9,8},{10,9},{11,10},{13,12},{... | collective-permute-start | bytes 491528 | tf_op jit(solution)/shard_map/ppermute | solution.py:38
  72.0 4.0 %collective-permute-start.11 = (f32[64,512]{1,0:T(8,128)S(1)}, f32[64,512]{1,0:T(8,128)S(1)}, u32[]{:S(2)}, u32[]{:S(2)}) collective-permute-start(f32[64,512]{1,0:T(8,128)S(1)} %get-tuple-element.56), channel_id=1, source_target_pairs={{0,1},{1,2},{2,3},{4,5},{5,6},{6,7},{8,9},{9,10},{10,11},{12,13},{... | collective-permute-start | bytes 393224 | tf_op jit(solution)/shard_map/ppermute | solution.py:38

commit v6 on v5

--- a/solution.py
+++ b/solution.py
@@ -127,13 +127,11 @@
 
 def edge_kernel(
     per, a_hbm, reluct_hbm, lam_hbm, mag_hbm, reg_hbm, slots_hbm,
-    ax_far, ax_near, nu_ref, code_ref, offset_ref,
-    a_ref, lam_ref, mag_ref, reg_ref, slots_ref, sems,
+    ax_far, ax_near, nu_ref, code_ref, offset_ref, static_ref,
+    first_ref, last_ref, lam_ref, mag_ref, reg_ref, slots_ref, sems,
 ):
-    devs = a_ref.shape[0]
-    top = a_ref.shape[3] - 1
-    parts = 2
-    some = devs // parts
+    devs = a_hbm.shape[0]
+    top = nu_ref.shape[2] - 1
     copies = [
         pltpu.make_async_copy(reluct_hbm, nu_ref, sems.at[0]),
         pltpu.make_async_copy(lam_hbm, lam_ref, sems.at[1]),
@@ -141,9 +139,16 @@
         pltpu.make_async_copy(reg_hbm, reg_ref, sems.at[3]),
         pltpu.make_async_copy(slots_hbm, slots_ref, sems.at[4]),
     ]
-    for part in range(parts):
-        at = pl.ds(part * some, some)
-        copies.append(pltpu.make_async_copy(a_hbm.at[at], a_ref.at[at], sems.at[5 + part]))
+    row_copies = []
+    for c in range(3):
+        for i in range(2):
+            to = first_ref.at[pl.ds((2 * c + i) * devs, devs)]
+            if c != 1:
+                row_copies.append((a_hbm.at[:, c, i, 0], to))
+            to = last_ref.at[pl.ds((2 * c + i) * devs, devs)]
+            row_copies.append((a_hbm.at[:, c, i, top], to))
+    for k, (source, to) in enumerate(row_copies):
+        copies.append(pltpu.make_async_copy(source, to, sems.at[5 + k]))
     for copy in copies:
         copy.start()
     for copy in copies[:5]:
@@ -158,8 +163,12 @@
     for i in range(2):
         nu_ref[1, i] = nu_ref[1, i] * (1.0 + 3.0 * lam_ref[i].astype(jnp.float32))
         code_ref[i] = jnp.where(mag_ref[i] == 1, reg_ref[i] - base, -1).astype(jnp.float32)
-    for part in range(parts):
-        copies[5 + part].wait()
+    height = top + 1
+    static_ref[pl.ds(0, height)] = nu_ref[1, 1]
+    static_ref[pl.ds(height, height)] = nu_ref[2, 1]
+    static_ref[pl.ds(2 * height, height)] = code_ref[1]
+    for copy in copies[5:]:
+        copy.wait()
 
     def body(ax_plus, ax_minus):
         for i in range(2):
@@ -169,19 +178,25 @@
             ax_plus[pl.ds(at + 4, 1)] = code_ref[i, top:]
             ax_plus[pl.ds(at + 6, 1)] = jnp.zeros_like(code_ref[i, top:])
 
-        @pl.loop(0, devs, unroll=UNROLL)
-        def _(d):
-            a = [[a_ref[d, c, i] for i in range(2)] for c in range(3)]
-            pack_ax(d, devs, a, ax_minus, ax_plus)
-            ax_plus[pl.ds(4 * devs + d, 1)] = a[1][0][top:]
+        firsts = [first_ref[pl.ds(k * devs, devs)] for k in (0, 1, 4, 5)]
+        lasts = [[last_ref[pl.ds((2 * c + i) * devs, devs)] for i in range(2)] for c in range(3)]
+        for k, first in enumerate(firsts):
+            ax_minus[pl.ds(k * devs, devs)] = first
+        for i in range(2):
+            ax_plus[pl.ds(i * devs, devs)] = lasts[1][i] - radial_next(lasts[1][i]) - lasts[2][i]
+        ax_plus[pl.ds(2 * devs, devs)] = lasts[1][1] - lasts[1][0] + lasts[0][0]
+        ax_plus[pl.ds(3 * devs, devs)] = lasts[0][1] - lasts[1][1]
+        ax_plus[pl.ds(4 * devs, devs)] = lasts[1][0]
 
     by_parity("ax", body, ax_far, ax_near)
 
 
-def plane_kernel(a_ref, far, near):
+def plane_kernel(a_ref, static_ref, far, near):
     devs, height = a_ref.shape[0], a_ref.shape[3]
 
     def body(plus, minus):
+        plus[pl.ds(2 * devs * height + devs, 3 * height)] = static_ref[...]
+
         @pl.loop(0, devs, unroll=UNROLL)
         def _(d):
             a = [[a_ref[d, c, i] for i in range(2)] for c in range(3)]
@@ -190,9 +205,8 @@
     by_parity("az", body, far, near)
 
 
-def corner_kernel(end, devs, ax_far, ax_near, nu, code, far_in, near_in, far, near, sems):
+def corner_kernel(end, devs, ax_far, ax_near, far_in, near_in, far, near, sems):
     at = pl.ds(end, devs)
-    height = nu.shape[2]
 
     def body_ax(ax_ahead, ax_behind):
         def body(plus, minus):
@@ -200,8 +214,6 @@
                 (ax_behind.at[pl.ds(4 * devs, devs)], minus.at[at]),
                 (ax_ahead.at[pl.ds(devs, devs)], plus.at[at]),
             ]
-            for k, source in enumerate((nu.at[1, 1], nu.at[2, 1], code.at[1])):
-                copies.append((source, plus.at[pl.ds(end + devs + k * height, height)]))
             copies = [
                 pltpu.make_async_copy(source, to, sems.at[k]) for k, (source, to) in enumerate(copies)
             ]
@@ -432,15 +444,16 @@
         f32(*reluctivity.shape),
         f32(*lamination.shape),
         jax.ShapeDtypeStruct(slot_map.shape, jnp.int32),
+        f32(3 * cells_ax, radial),
     ]
-    ax_far, ax_near, nu, code, offset = pl.pallas_call(
+    ax_far, ax_near, nu, code, offset, static = pl.pallas_call(
         functools.partial(edge_kernel, per),
         out_shape=edges,
         in_specs=[HBM] * 6,
         out_specs=[VMEM] * len(edges),
-        scratch_shapes=[pltpu.VMEM(start_field.shape, jnp.float32)]
+        scratch_shapes=[pltpu.VMEM((6 * devs, radial), jnp.float32)] * 2
         + [pltpu.VMEM(lamination.shape, jnp.int32)] * 3
-        + [pltpu.VMEM(slot_map.shape, jnp.int32), pltpu.SemaphoreType.DMA((7,))],
+        + [pltpu.VMEM(slot_map.shape, jnp.int32), pltpu.SemaphoreType.DMA((15,))],
         compiler_params=pltpu.CompilerParams(vmem_limit_bytes=LIMIT_FIRST),
     )(start_field, reluctivity, lamination, magnets, region_ids, slot_map)
     ax_halos = swapped_ax(ax_far, 1), swapped_ax(ax_near, 0)
@@ -448,20 +461,20 @@
     packed = pl.pallas_call(
         plane_kernel,
         out_shape=planes,
-        in_specs=[VMEM],
+        in_specs=[VMEM] * 2,
         out_specs=[VMEM] * 2,
         compiler_params=pltpu.CompilerParams(vmem_limit_bytes=LIMIT),
         cost_estimate=pl.CostEstimate(flops=10**7, bytes_accessed=3 * MIB, transcendentals=0),
-    )(start_field)
+    )(start_field, static)
     far, near = pl.pallas_call(
         functools.partial(corner_kernel, whole, devs),
         out_shape=planes,
-        in_specs=[VMEM, VMEM, ANY, ANY, ANY, ANY],
+        in_specs=[VMEM, VMEM, ANY, ANY],
         out_specs=[ANY] * 2,
-        scratch_shapes=[pltpu.SemaphoreType.DMA((5,))],
-        input_output_aliases={4: 0, 5: 1},
+        scratch_shapes=[pltpu.SemaphoreType.DMA((2,))],
+        input_output_aliases={2: 0, 3: 1},
         compiler_params=pltpu.CompilerParams(vmem_limit_bytes=LIMIT),
-    )(*ax_halos, nu, code, *packed)
+    )(*ax_halos, *packed)
     ax_ahead, ax_behind, ax_minus = pl.pallas_call(
         settle_kernel,
         out_shape=[f32(4 * devs, radial), f32(5 * devs + 8, radial), f32(4 * devs, radial)],

time: 86.8 us -> 83.7 us (0.964)
  waiting for transfers between devices: 20.2 us -> 19.3 us
    ppermute x6, waiting for transfers between devices: 18.3 us -> 17.4 us  [swapped(): return lax.ppermute(value, ('az', 'ax'), pairs)]
    unnamed x17 -> x15, local copies, waits for them, and re-layouts: 3.17 us -> 2.32 us
where the time goes in v6:
time: 83.7 us; the launch traced here: 83.3 us
  starting transfers between devices  33.7 us (40%)
  waiting for transfers between devices  19.3 us (23%)
  blocking collectives  15.7 us (19%)
  Pallas kernels  11.2 us (13%)
  local copies, waits for them, and re-layouts  2.52 us (3%)
    ppermute x6, starting transfers between devices, swapped(): return lax.ppermute(value, ('az', 'ax'), pairs)  21.4 us
    ppermute x6, waiting for transfers between devices, swapped(): return lax.ppermute(value, ('az', 'ax'), pairs)  17.4 us
    all_to_all x1, blocking collectives, shards(): lax.all_to_all(jnp.broadcast_to(flat, (count_az, comps * devs * per)), 'a...  15.7 us
    ppermute x4, starting transfers between devices, moved(): return lax.ppermute(value, ('az', 'ax'), pairs)  8.64 us
    pallas_call x3, Pallas kernels, step(): pl.pallas_call(functools.partial(step_kernel, stage, per), out_shape=outs...  7.01 us
    ppermute x2, starting transfers between devices, swapped_ax(): lax.ppermute(value, 'ax', [(q, to) for q, to in pairs if 0 <= to < count])  3.68 us
    unnamed x15, local copies, waits for them, and re-layouts  2.32 us
    pallas_call x1, Pallas kernels, shards(): pl.pallas_call(functools.partial(edge_kernel, per), out_shape=edges, in_s...  2.08 us
  transfers between devices with their start and end apart: 12, of which 4 were waited for; matrix products, arithmetic and copies ran while one was open for 0% of the time, Pallas kernels for 2%

profile of v6, /device:TPU:0, one launch (start us, length us, event | category | flops | bytes accessed | tf_op | source)
XLA Modules:
  0.0 83.3 jit_solution(16061262960448426216)
XLA Ops:
  0.6 2.1 %shard_map.86 = (f32[88,512]{1,0:T(8,128)}, f32[88,512]{1,0:T(8,128)}, f32[3,2,8,512]{3,2,1,0:T(8,128)}, f32[2,8,512]{2,1,0:T(8,128)}, s32[16,128]{1,0:T(8,128)}, /*index=5*/f32[24,512]{1,0:T(8,128)}) custom-call(f32[16,3,2,8,512]{4,3,2,1,0:T(8,128)} %refs_14_.1, f32[3,2,8,512]{3,2,1,0:T(8,128)} %reluct_hbm.1, s32[2,8,512]{2,1,0:T(8,128)} %lam_hbm.1, ...), custom_call_target="tpu_custom_call" | custom-call | tf_op jit(solution)/shard_map/pallas_call | solution.py:449
  2.7 0.7 collective-permute-start
  3.4 3.0 %collective-permute-start.1 = (f32[88,512]{1,0:T(8,128)}, f32[88,512]{1,0:T(8,128)S(1)}, u32[]{:S(2)}, u32[]{:S(2)}) collective-permute-start(f32[88,512]{1,0:T(8,128)} %get-tuple-element.34), channel_id=1, source_target_pairs={{0,1},{1,0},{2,3},{3,2},{4,5},{5,4},{6,7},{7,6},{8,9},{9,8},{10,11... | collective-permute-start | bytes 540680 | tf_op jit(solution)/shard_map/ppermute | solution.py:54
  6.4 1.4 %copy-done = f32[16,3,2,8,512]{4,3,2,1,0:T(8,128)S(1)} copy-done((f32[16,3,2,8,512]{4,3,2,1,0:T(8,128)S(1)}, f32[16,3,2,8,512]{4,3,2,1,0:T(8,128)}, u32[]{:S(2)}) %copy-start) | copy-done | bytes 1572888
  7.8 0.8 copy-done.3
  8.6 1.4 %shard_map.87 = (f32[296,512]{1,0:T(8,128)}, f32[296,512]{1,0:T(8,128)}) custom-call(f32[16,3,2,8,512]{4,3,2,1,0:T(8,128)S(1)} %copy-done, f32[24,512]{1,0:T(8,128)S(1)} %copy-done.3), custom_call_target="tpu_custom_call" | custom-call | flops 10000000 | bytes 3145728 | tf_op jit(solution)/shard_map/pallas_call | solution.py:461
  10.0 0.7 shard_map.88
  10.7 8.7 %collective-permute-start.2 = (f32[296,512]{1,0:T(8,128)}, f32[296,512]{1,0:T(8,128)S(1)}, u32[]{:S(2)}, u32[]{:S(2)}) collective-permute-start(f32[296,512]{1,0:T(8,128)} %get-tuple-element.38), channel_id=1, source_target_pairs={{0,124},{1,125},{2,126},{3,127},{4,8},{5,9},{6,10},{7,11},{8,4},{9... | collective-permute-start | bytes 1818632 | tf_op jit(solution)/shard_map/ppermute | solution.py:48
  19.4 0.1 copy.11
  19.5 0.1 broadcast_in_dim.7
  19.7 15.7 %all_to_all.6 = f32[32,1,192]{2,1,0:T(1,128)S(1)} all-to-all(f32[32,1,192]{2,1,0:T(1,128)S(1)} %broadcast_in_dim.8), channel_id=1, replica_groups=mesh['az'=32,'ax'=4] {'az'}, dimensions={0} | all-to-all | bytes 49152 | tf_op jit(solution)/shard_map/all_to_all | solution.py:488
  35.7 3.5 %shard_map.90 = (f32[16,3,2,8,512]{4,3,2,1,0:T(8,128)S(1)}, f32[272,512]{1,0:T(8,128)S(1)}, f32[272,512]{1,0:T(8,128)S(1)}, f32[80,512]{1,0:T(8,128)S(1)}, f32[6...) custom-call(f32[16,3,2,8,512]{4,3,2,1,0:T(8,128)S(1)} %copy-done.1, ...), custom_call_target="tpu_custom_call" | custom-call | tf_op jit(solution)/shard_map/pallas_call | solution.py:510
  39.1 6.2 %collective-permute-start.4 = (f32[272,512]{1,0:T(8,128)S(1)}, f32[272,512]{1,0:T(8,128)S(1)}, u32[]{:S(2)}, u32[]{:S(2)}) collective-permute-start(f32[272,512]{1,0:T(8,128)S(1)} %get-tuple-element.46), channel_id=1, source_target_pairs={{0,124},{1,125},{2,126},{3,127},{4,8},{5,9},{6,10},{7,11},{8,4},{9... | collective-permute-start | bytes 1671176 | tf_op jit(solution)/shard_map/ppermute | solution.py:48
  45.3 1.3 %collective-permute-start.6 = (f32[80,512]{1,0:T(8,128)S(1)}, f32[80,512]{1,0:T(8,128)S(1)}, u32[]{:S(2)}, u32[]{:S(2)}) collective-permute-start(f32[80,512]{1,0:T(8,128)S(1)} %get-tuple-element.48.refs_9_), channel_id=1, source_target_pairs={{1,0},{2,1},{3,2},{5,4},{6,5},{7,6},{9,8},{10,9},{11,10},{13,12},{... | collective-permute-start | bytes 491528 | tf_op jit(solution)/shard_map/ppermute | solution.py:38
  46.6 3.0 %collective-permute-start.7 = (f32[64,512]{1,0:T(8,128)S(1)}, f32[64,512]{1,0:T(8,128)S(1)}, u32[]{:S(2)}, u32[]{:S(2)}) collective-permute-start(f32[64,512]{1,0:T(8,128)S(1)} %get-tuple-element.49), channel_id=1, source_target_pairs={{0,1},{1,2},{2,3},{4,5},{5,6},{6,7},{8,9},{9,10},{10,11},{12,13},{... | collective-permute-start | bytes 393224 | tf_op jit(solution)/shard_map/ppermute | solution.py:38
  49.7 1.0 %collective-permute-done.7.refs_8_ = f32[64,512]{1,0:T(8,128)S(1)} collective-permute-done((f32[64,512]{1,0:T(8,128)S(1)}, f32[64,512]{1,0:T(8,128)S(1)}, u32[]{:S(2)}, u32[]{:S(2)}) %collective-permute-start.7) | collective-permute-done | bytes 131104 | tf_op jit(solution)/shard_map/ppermute | solution.py:38
  50.6 9.0 %collective-permute-done.4.refs_4_ = f32[272,512]{1,0:T(8,128)S(1)} collective-permute-done((f32[272,512]{1,0:T(8,128)S(1)}, f32[272,512]{1,0:T(8,128)S(1)}, u32[]{:S(2)}, u32[]{:S(2)}) %collective-permute-start.4) | collective-permute-done | bytes 557088 | tf_op jit(solution)/shard_map/ppermute | solution.py:48
  59.7 1.7 %shard_map.91 = (f32[16,3,2,8,512]{4,3,2,1,0:T(8,128)S(1)}, f32[272,512]{1,0:T(8,128)S(1)}, f32[272,512]{1,0:T(8,128)S(1)}, f32[80,512]{1,0:T(8,128)S(1)}, f32[64,512]{1,0:T(8,128)S(1)}, /*index=5*/f32[64,512]{1,0:T(8,128)S(1)}) custom-call(f32[16,3,2,8,512]{4,3,2,1,0:T(8,128)S(1)} %get-tuple-element.45.refs_0_, f32[3,2,8,512]{3,2,1,0:T(8,128)S(1)} %copy-done.2, ...), custom_call_target="tpu_custom_call" | custom-call | tf_op jit(solution)/shard_map/pallas_call | solution.py:510
  61.4 6.4 %collective-permute-start.8 = (f32[272,512]{1,0:T(8,128)S(1)}, f32[272,512]{1,0:T(8,128)S(1)}, u32[]{:S(2)}, u32[]{:S(2)}) collective-permute-start(f32[272,512]{1,0:T(8,128)S(1)} %get-tuple-element.55), channel_id=1, source_target_pairs={{0,124},{1,125},{2,126},{3,127},{4,8},{5,9},{6,10},{7,11},{8,4},{9... | collective-permute-start | bytes 1671176 | tf_op jit(solution)/shard_map/ppermute | solution.py:48
  67.8 1.3 %collective-permute-start.10 = (f32[80,512]{1,0:T(8,128)S(1)}, f32[80,512]{1,0:T(8,128)S(1)}, u32[]{:S(2)}, u32[]{:S(2)}) collective-permute-start(f32[80,512]{1,0:T(8,128)S(1)} %get-tuple-element.57.refs_9_), channel_id=1, source_target_pairs={{1,0},{2,1},{3,2},{5,4},{6,5},{7,6},{9,8},{10,9},{11,10},{13,12},{... | collective-permute-start | bytes 491528 | tf_op jit(solution)/shard_map/ppermute | solution.py:38
  69.1 3.0 %collective-permute-start.11 = (f32[64,512]{1,0:T(8,128)S(1)}, f32[64,512]{1,0:T(8,128)S(1)}, u32[]{:S(2)}, u32[]{:S(2)}) collective-permute-start(f32[64,512]{1,0:T(8,128)S(1)} %get-tuple-element.58), channel_id=1, source_target_pairs={{0,1},{1,2},{2,3},{4,5},{5,6},{6,7},{8,9},{9,10},{10,11},{12,13},{... | collective-permute-start | bytes 393224 | tf_op jit(solution)/shard_map/ppermute | solution.py:38
  72.2 1.0 %collective-permute-done.11.refs_8_ = f32[64,512]{1,0:T(8,128)S(1)} collective-permute-done((f32[64,512]{1,0:T(8,128)S(1)}, f32[64,512]{1,0:T(8,128)S(1)}, u32[]{:S(2)}, u32[]{:S(2)}) %collective-permute-start.11) | collective-permute-done | bytes 131104 | tf_op jit(solution)/shard_map/ppermute | solution.py:38
  73.1 8.3 %collective-permute-done.8.refs_4_ = f32[272,512]{1,0:T(8,128)S(1)} collective-permute-done((f32[272,512]{1,0:T(8,128)S(1)}, f32[272,512]{1,0:T(8,128)S(1)}, u32[]{:S(2)}, u32[]{:S(2)}) %collective-permute-start.8) | collective-permute-done | bytes 557088 | tf_op jit(solution)/shard_map/ppermute | solution.py:48
  81.5 1.8 %shard_map.92 = (f32[16,3,2,8,512]{4,3,2,1,0:T(8,128)}, f32[16,3,2,8,512]{4,3,2,1,0:T(8,128)}) custom-call(f32[16,3,2,8,512]{4,3,2,1,0:T(8,128)S(1)} %get-tuple-element.54.refs_0_, f32[3,2,8,512]{3,2,1,0:T(8,128)S(1)} %copy-done.2, f32[296,512]{1,0:T(8,128)S(1)} %collective-permute-done.2.refs_2_.refs_4_, ...), custom_call_target="tpu_custom_call" | custom-call | tf_op jit(solution)/shard_map/pallas_call | solution.py:510
  (27 shorter events, 0.3 us)
Async XLA Ops:
  2.7 7.3 %collective-permute-start = (f32[88,512]{1,0:T(8,128)}, f32[88,512]{1,0:T(8,128)S(1)}, u32[]{:S(2)}, u32[]{:S(2)}) collective-permute-start(f32[88,512]{1,0:T(8,128)} %get-tuple-element.33), channel_id=1, source_target_pairs={{1,2},{2,1},{5,6},{6,5},{9,10},{10,9},{13,14},{14,13},{17,18},{18,... | collective-permute-start | bytes 540680 | tf_op jit(solution)/shard_map/ppermute | solution.py:54
  3.4 6.6 %collective-permute-start.1 = (f32[88,512]{1,0:T(8,128)}, f32[88,512]{1,0:T(8,128)S(1)}, u32[]{:S(2)}, u32[]{:S(2)}) collective-permute-start(f32[88,512]{1,0:T(8,128)} %get-tuple-element.34), channel_id=1, source_target_pairs={{0,1},{1,0},{2,3},{3,2},{4,5},{5,4},{6,7},{7,6},{8,9},{9,8},{10,11... | collective-permute-start | bytes 540680 | tf_op jit(solution)/shard_map/ppermute | solution.py:54
  6.4 1.4 %copy-start = (f32[16,3,2,8,512]{4,3,2,1,0:T(8,128)S(1)}, f32[16,3,2,8,512]{4,3,2,1,0:T(8,128)}, u32[]{:S(2)}) copy-start(f32[16,3,2,8,512]{4,3,2,1,0:T(8,128)} %refs_14_.1) | copy-start | bytes 4718596
  7.8 0.8 copy-start.3
  8.6 10.8 %copy-start.6 = (f32[3,16,4]{1,2,0:T(4,128)S(1)}, f32[3,16,4]{1,2,0:T(4,128)}, u32[]{:S(2)}) copy-start(f32[3,16,4]{1,2,0:T(4,128)} %param.12) | copy-start | bytes 2308
  8.6 26.9 %copy-start.1 = (f32[16,3,2,8,512]{4,3,2,1,0:T(8,128)S(1)}, f32[16,3,2,8,512]{4,3,2,1,0:T(8,128)}, u32[]{:S(2)}) copy-start(f32[16,3,2,8,512]{4,3,2,1,0:T(8,128)} %refs_14_.1) | copy-start | bytes 4718596
  10.0 25.6 %copy-start.2 = (f32[3,2,8,512]{3,2,1,0:T(8,128)S(1)}, f32[3,2,8,512]{3,2,1,0:T(8,128)}, u32[]{:S(2)}) copy-start(f32[3,2,8,512]{3,2,1,0:T(8,128)} %get-tuple-element.32.refs_1_) | copy-start | bytes 294916
  10.0 25.6 %copy-start.4 = (f32[2,8,512]{2,1,0:T(8,128)S(1)}, f32[2,8,512]{2,1,0:T(8,128)}, u32[]{:S(2)}) copy-start(f32[2,8,512]{2,1,0:T(8,128)} %get-tuple-element.43.refs_10_) | copy-start | bytes 98308
  10.0 25.6 %copy-start.5 = (s32[16,128]{1,0:T(8,128)S(1)}, s32[16,128]{1,0:T(8,128)}, u32[]{:S(2)}) copy-start(s32[16,128]{1,0:T(8,128)} %get-tuple-element.44.refs_11_) | copy-start | bytes 24580
  10.7 24.9 %collective-permute-start.2 = (f32[296,512]{1,0:T(8,128)}, f32[296,512]{1,0:T(8,128)S(1)}, u32[]{:S(2)}, u32[]{:S(2)}) collective-permute-start(f32[296,512]{1,0:T(8,128)} %get-tuple-element.38), channel_id=1, source_target_pairs={{0,124},{1,125},{2,126},{3,127},{4,8},{5,9},{6,10},{7,11},{8,4},{9... | collective-permute-start | bytes 1818632 | tf_op jit(solution)/shard_map/ppermute | solution.py:48
  19.4 16.2 %collective-permute-start.3 = (f32[296,512]{1,0:T(8,128)}, f32[296,512]{1,0:T(8,128)S(1)}, u32[]{:S(2)}, u32[]{:S(2)}) collective-permute-start(f32[296,512]{1,0:T(8,128)} %get-tuple-element.39), channel_id=1, source_target_pairs={{0,4},{1,5},{2,6},{3,7},{4,0},{5,1},{6,2},{7,3},{8,12},{9,13},{10,... | collective-permute-start | bytes 1818632 | tf_op jit(solution)/shard_map/ppermute | solution.py:48
  39.1 20.6 %collective-permute-start.4 = (f32[272,512]{1,0:T(8,128)S(1)}, f32[272,512]{1,0:T(8,128)S(1)}, u32[]{:S(2)}, u32[]{:S(2)}) collective-permute-start(f32[272,512]{1,0:T(8,128)S(1)} %get-tuple-element.46), channel_id=1, source_target_pairs={{0,124},{1,125},{2,126},{3,127},{4,8},{5,9},{6,10},{7,11},{8,4},{9... | collective-permute-start | bytes 1671176 | tf_op jit(solution)/shard_map/ppermute | solution.py:48
  45.3 14.4 %collective-permute-start.5 = (f32[272,512]{1,0:T(8,128)S(1)}, f32[272,512]{1,0:T(8,128)S(1)}, u32[]{:S(2)}, u32[]{:S(2)}) collective-permute-start(f32[272,512]{1,0:T(8,128)S(1)} %get-tuple-element.47), channel_id=1, source_target_pairs={{0,4},{1,5},{2,6},{3,7},{4,0},{5,1},{6,2},{7,3},{8,12},{9,13},{10,... | collective-permute-start | bytes 1671176 | tf_op jit(solution)/shard_map/ppermute | solution.py:48
  45.3 5.3 %collective-permute-start.6 = (f32[80,512]{1,0:T(8,128)S(1)}, f32[80,512]{1,0:T(8,128)S(1)}, u32[]{:S(2)}, u32[]{:S(2)}) collective-permute-start(f32[80,512]{1,0:T(8,128)S(1)} %get-tuple-element.48.refs_9_), channel_id=1, source_target_pairs={{1,0},{2,1},{3,2},{5,4},{6,5},{7,6},{9,8},{10,9},{11,10},{13,12},{... | collective-permute-start | bytes 491528 | tf_op jit(solution)/shard_map/ppermute | solution.py:38
  46.6 4.0 %collective-permute-start.7 = (f32[64,512]{1,0:T(8,128)S(1)}, f32[64,512]{1,0:T(8,128)S(1)}, u32[]{:S(2)}, u32[]{:S(2)}) collective-permute-start(f32[64,512]{1,0:T(8,128)S(1)} %get-tuple-element.49), channel_id=1, source_target_pairs={{0,1},{1,2},{2,3},{4,5},{5,6},{6,7},{8,9},{9,10},{10,11},{12,13},{... | collective-permute-start | bytes 393224 | tf_op jit(solution)/shard_map/ppermute | solution.py:38
  61.4 20.1 %collective-permute-start.8 = (f32[272,512]{1,0:T(8,128)S(1)}, f32[272,512]{1,0:T(8,128)S(1)}, u32[]{:S(2)}, u32[]{:S(2)}) collective-permute-start(f32[272,512]{1,0:T(8,128)S(1)} %get-tuple-element.55), channel_id=1, source_target_pairs={{0,124},{1,125},{2,126},{3,127},{4,8},{5,9},{6,10},{7,11},{8,4},{9... | collective-permute-start | bytes 1671176 | tf_op jit(solution)/shard_map/ppermute | solution.py:48
  67.8 13.6 %collective-permute-start.9 = (f32[272,512]{1,0:T(8,128)S(1)}, f32[272,512]{1,0:T(8,128)S(1)}, u32[]{:S(2)}, u32[]{:S(2)}) collective-permute-start(f32[272,512]{1,0:T(8,128)S(1)} %get-tuple-element.56), channel_id=1, source_target_pairs={{0,4},{1,5},{2,6},{3,7},{4,0},{5,1},{6,2},{7,3},{8,12},{9,13},{10,... | collective-permute-start | bytes 1671176 | tf_op jit(solution)/shard_map/ppermute | solution.py:48
  67.8 5.3 %collective-permute-start.10 = (f32[80,512]{1,0:T(8,128)S(1)}, f32[80,512]{1,0:T(8,128)S(1)}, u32[]{:S(2)}, u32[]{:S(2)}) collective-permute-start(f32[80,512]{1,0:T(8,128)S(1)} %get-tuple-element.57.refs_9_), channel_id=1, source_target_pairs={{1,0},{2,1},{3,2},{5,4},{6,5},{7,6},{9,8},{10,9},{11,10},{13,12},{... | collective-permute-start | bytes 491528 | tf_op jit(solution)/shard_map/ppermute | solution.py:38
  69.1 4.0 %collective-permute-start.11 = (f32[64,512]{1,0:T(8,128)S(1)}, f32[64,512]{1,0:T(8,128)S(1)}, u32[]{:S(2)}, u32[]{:S(2)}) collective-permute-start(f32[64,512]{1,0:T(8,128)S(1)} %get-tuple-element.58), channel_id=1, source_target_pairs={{0,1},{1,2},{2,3},{4,5},{5,6},{6,7},{8,9},{9,10},{10,11},{12,13},{... | collective-permute-start | bytes 393224 | tf_op jit(solution)/shard_map/ppermute | solution.py:38

commit v7 on v6

--- a/solution.py
+++ b/solution.py
@@ -263,6 +263,31 @@
             value * (1.0 + mix_second - mass_term * step_second) - start * mix_second - curl * step_second
         )
     return -curl - mass_term * value
+
+
+def flux_of(d, devs, a, up1, up2, ax_ahead):
+    flux = [[None, None], [None, None], [None, None]]
+    for i in range(2):
+        next1 = a[1][1] if i == 0 else up1
+        next2 = a[2][1] if i == 0 else up2
+        row0 = ax_ahead[pl.ds(i * devs + d, 1)]
+        row2 = ax_ahead[pl.ds((2 + i) * devs + d, 1)]
+        flux[0][i] = (axial_next(a[2][i], row2) - a[2][i]) - (radial_next(a[1][i]) - a[1][i])
+        flux[1][i] = (radial_next(a[0][i]) - a[0][i]) - (next2 - a[2][i])
+        flux[2][i] = (next1 - a[1][i]) - (axial_next(a[0][i], row0) - a[0][i])
+    return flux
+
+
+def flux_kernel(a_ref, nu_ref, src_ref, ax_ahead, out_ref):
+    devs = a_ref.shape[0]
+
+    @pl.loop(0, devs, unroll=UNROLL)
+    def _(d):
+        a = [[a_ref[d, c, i] for i in range(2)] for c in range(3)]
+        flux = flux_of(d, devs, a, 0.0, 0.0, ax_ahead)
+        for c in range(3):
+            for i in range(2):
+                out_ref[d, c, i] = nu_ref[c, i] * flux[c][i] - src_ref[d, c, i]
 
 
 def step_kernel(stage, per, *refs):
@@ -360,23 +385,19 @@
         up = [None, ahead[block(2 * d, height)], ahead[block(2 * d + 1, height)]]
         inten = [[None, None], [None, None], [None, None]]
         own = [values(d, c, per) for c in range(3)] if stage == 0 else None
+        if stage == 0:
+            fluxes = flux_of(d, devs, a, up[1], up[2], ax_ahead)
         for i in range(2):
-            next1 = a[1][1] if i == 0 else up[1]
-            next2 = a[2][1] if i == 0 else up[2]
-            row0 = ax_ahead[pl.ds(i * devs + d, 1)]
-            row2 = ax_ahead[pl.ds((2 + i) * devs + d, 1)]
-            flux = (
-                (axial_next(a[2][i], row2) - a[2][i]) - (radial_next(a[1][i]) - a[1][i]),
-                (radial_next(a[0][i]) - a[0][i]) - (next2 - a[2][i]),
-                (next1 - a[1][i]) - (axial_next(a[0][i], row0) - a[0][i]),
-            )
             for c in range(3):
                 if stage == 0:
                     src = picked(nu_ref[c, i], code_ref[i], own[c])
                     src_ref[d, c, i] = src
+                    inten[c][i] = nu_ref[c, i] * fluxes[c][i] - src
                 else:
-                    src = src_ref[d, c, i]
-                inten[c][i] = nu_ref[c, i] * flux[c] - src
+                    inten[c][i] = src_ref[d, c, i]
+        if stage > 0:
+            inten[1][1] = inten[1][1] - nu_ref[1, 1] * up[2]
+            inten[2][1] = inten[2][1] + nu_ref[2, 1] * up[1]
         back_src = [None, None]
         for c in range(1, 3):
             if stage == 0:
@@ -520,11 +541,25 @@
             compiler_params=pltpu.CompilerParams(vmem_limit_bytes=LIMIT),
         )(field, nu, far_halo, near_halo, *halos[:2], ax_behind, *halos[2:], *more)
 
+    def known(field, halos):
+        return pl.pallas_call(
+            flux_kernel,
+            out_shape=field_like,
+            in_specs=[VMEM] * 4,
+            out_specs=VMEM,
+            compiler_params=pltpu.CompilerParams(vmem_limit_bytes=LIMIT),
+            cost_estimate=pl.CostEstimate(flops=10**7, bytes_accessed=5 * MIB, transcendentals=0),
+        )(field, nu, src[0], halos[2])
+
     middle, *rest = step(0, start_field, halos, [code, offset, table], [VMEM, SMEM, SMEM])
     packed, track0, src = rest[:4], rest[4], rest[5:]
-    final, *rest = step(1, middle, exchange(*packed), [*src, track0, start_field], [VMEM] * 5)
+    halos = exchange(*packed)
+    more = [known(middle, halos), *src[1:], track0, start_field]
+    final, *rest = step(1, middle, halos, more, [VMEM] * 5)
     packed, track1 = rest[:4], rest[4]
-    residual, out = step(2, final, exchange(*packed), [*src, track0, track1], [VMEM] * 5)
+    halos = exchange(*packed)
+    more = [known(final, halos), *src[1:], track0, track1]
+    residual, out = step(2, final, halos, more, [VMEM] * 5)
     return out, residual
 
 

time: 83.7 us -> 83.7 us (level)
    ppermute x4, waiting for transfers between devices: 1.93 us -> 0.77 us  [moved(): return lax.ppermute(value, ('az', 'ax'), pairs)]
    pallas_call x0 -> x2, Pallas kernels: none -> 1.12 us  [known(): pl.pallas_call(flux_kernel, out_shape=field_like, in_specs=[VMEM] * 4, ou...]
  transfers between devices with their start and end apart: 12 -> 12, of which waited for: 4 -> 4; matrix products, arithmetic and copies ran while one was open for 0% -> 0% of each run, Pallas kernels for 2% -> 3%
where the time goes in v7:
time: 83.7 us; the launch traced here: 83.3 us
  starting transfers between devices  33.7 us (40%)
  waiting for transfers between devices  18.8 us (22%)
  blocking collectives  15.7 us (19%)
  Pallas kernels  11.7 us (14%)
  local copies, waits for them, and re-layouts  2.52 us (3%)
    ppermute x6, starting transfers between devices, swapped(): return lax.ppermute(value, ('az', 'ax'), pairs)  21.4 us
    ppermute x6, waiting for transfers between devices, swapped(): return lax.ppermute(value, ('az', 'ax'), pairs)  18 us
    all_to_all x1, blocking collectives, shards(): lax.all_to_all(jnp.broadcast_to(flat, (count_az, comps * devs * per)), 'a...  15.7 us
    ppermute x4, starting transfers between devices, moved(): return lax.ppermute(value, ('az', 'ax'), pairs)  8.64 us
    pallas_call x3, Pallas kernels, step(): pl.pallas_call(functools.partial(step_kernel, stage, per), out_shape=outs...  6.4 us
    ppermute x2, starting transfers between devices, swapped_ax(): lax.ppermute(value, 'ax', [(q, to) for q, to in pairs if 0 <= to < count])  3.68 us
    unnamed x15, local copies, waits for them, and re-layouts  2.32 us
    pallas_call x1, Pallas kernels, shards(): pl.pallas_call(functools.partial(edge_kernel, per), out_shape=edges, in_s...  2.08 us
  transfers between devices with their start and end apart: 12, of which 4 were waited for; matrix products, arithmetic and copies ran while one was open for 0% of the time, Pallas kernels for 3%

profile of v7, /device:TPU:0, one launch (start us, length us, event | category | flops | bytes accessed | tf_op | source)
XLA Modules:
  0.0 83.3 jit_solution(8405672409626322058)
XLA Ops:
  0.6 2.1 %shard_map.86 = (f32[88,512]{1,0:T(8,128)}, f32[88,512]{1,0:T(8,128)}, f32[3,2,8,512]{3,2,1,0:T(8,128)}, f32[2,8,512]{2,1,0:T(8,128)}, s32[16,128]{1,0:T(8,128)}, /*index=5*/f32[24,512]{1,0:T(8,128)}) custom-call(f32[16,3,2,8,512]{4,3,2,1,0:T(8,128)} %refs_14_.1, f32[3,2,8,512]{3,2,1,0:T(8,128)} %reluct_hbm.1, s32[2,8,512]{2,1,0:T(8,128)} %lam_hbm.1, ...), custom_call_target="tpu_custom_call" | custom-call | tf_op jit(solution)/shard_map/pallas_call | solution.py:470
  2.7 0.7 collective-permute-start
  3.4 3.0 %collective-permute-start.1 = (f32[88,512]{1,0:T(8,128)}, f32[88,512]{1,0:T(8,128)S(1)}, u32[]{:S(2)}, u32[]{:S(2)}) collective-permute-start(f32[88,512]{1,0:T(8,128)} %get-tuple-element.34), channel_id=1, source_target_pairs={{0,1},{1,0},{2,3},{3,2},{4,5},{5,4},{6,7},{7,6},{8,9},{9,8},{10,11... | collective-permute-start | bytes 540680 | tf_op jit(solution)/shard_map/ppermute | solution.py:54
  6.4 1.4 %copy-done = f32[16,3,2,8,512]{4,3,2,1,0:T(8,128)S(1)} copy-done((f32[16,3,2,8,512]{4,3,2,1,0:T(8,128)S(1)}, f32[16,3,2,8,512]{4,3,2,1,0:T(8,128)}, u32[]{:S(2)}) %copy-start) | copy-done | bytes 1572888
  7.8 0.8 copy-done.3
  8.6 1.4 %shard_map.87 = (f32[296,512]{1,0:T(8,128)}, f32[296,512]{1,0:T(8,128)}) custom-call(f32[16,3,2,8,512]{4,3,2,1,0:T(8,128)S(1)} %copy-done, f32[24,512]{1,0:T(8,128)S(1)} %copy-done.3), custom_call_target="tpu_custom_call" | custom-call | flops 10000000 | bytes 3145728 | tf_op jit(solution)/shard_map/pallas_call | solution.py:482
  10.0 0.7 shard_map.88
  10.7 8.7 %collective-permute-start.2 = (f32[296,512]{1,0:T(8,128)}, f32[296,512]{1,0:T(8,128)S(1)}, u32[]{:S(2)}, u32[]{:S(2)}) collective-permute-start(f32[296,512]{1,0:T(8,128)} %get-tuple-element.38), channel_id=1, source_target_pairs={{0,124},{1,125},{2,126},{3,127},{4,8},{5,9},{6,10},{7,11},{8,4},{9... | collective-permute-start | bytes 1818632 | tf_op jit(solution)/shard_map/ppermute | solution.py:48
  19.7 15.7 %all_to_all.6 = f32[32,1,192]{2,1,0:T(1,128)S(1)} all-to-all(f32[32,1,192]{2,1,0:T(1,128)S(1)} %broadcast_in_dim.8), channel_id=1, replica_groups=mesh['az'=32,'ax'=4] {'az'}, dimensions={0} | all-to-all | bytes 49152 | tf_op jit(solution)/shard_map/all_to_all | solution.py:509
  35.7 3.5 %shard_map.90 = (f32[16,3,2,8,512]{4,3,2,1,0:T(8,128)S(1)}, f32[272,512]{1,0:T(8,128)S(1)}, f32[272,512]{1,0:T(8,128)S(1)}, f32[80,512]{1,0:T(8,128)S(1)}, f32[6...) custom-call(f32[16,3,2,8,512]{4,3,2,1,0:T(8,128)S(1)} %copy-done.1, ...), custom_call_target="tpu_custom_call" | custom-call | tf_op jit(solution)/shard_map/pallas_call | solution.py:531
  39.1 6.2 %collective-permute-start.4 = (f32[272,512]{1,0:T(8,128)S(1)}, f32[272,512]{1,0:T(8,128)S(1)}, u32[]{:S(2)}, u32[]{:S(2)}) collective-permute-start(f32[272,512]{1,0:T(8,128)S(1)} %get-tuple-element.46), channel_id=1, source_target_pairs={{0,124},{1,125},{2,126},{3,127},{4,8},{5,9},{6,10},{7,11},{8,4},{9... | collective-permute-start | bytes 1671176 | tf_op jit(solution)/shard_map/ppermute | solution.py:48
  45.3 1.3 %collective-permute-start.6 = (f32[80,512]{1,0:T(8,128)S(1)}, f32[80,512]{1,0:T(8,128)S(1)}, u32[]{:S(2)}, u32[]{:S(2)}) collective-permute-start(f32[80,512]{1,0:T(8,128)S(1)} %get-tuple-element.48.refs_9_), channel_id=1, source_target_pairs={{1,0},{2,1},{3,2},{5,4},{6,5},{7,6},{9,8},{10,9},{11,10},{13,12},{... | collective-permute-start | bytes 491528 | tf_op jit(solution)/shard_map/ppermute | solution.py:38
  46.6 3.0 %collective-permute-start.7 = (f32[64,512]{1,0:T(8,128)S(1)}, f32[64,512]{1,0:T(8,128)S(1)}, u32[]{:S(2)}, u32[]{:S(2)}) collective-permute-start(f32[64,512]{1,0:T(8,128)S(1)} %get-tuple-element.49), channel_id=1, source_target_pairs={{0,1},{1,2},{2,3},{4,5},{5,6},{6,7},{8,9},{9,10},{10,11},{12,13},{... | collective-permute-start | bytes 393224 | tf_op jit(solution)/shard_map/ppermute | solution.py:38
  49.7 0.6 shard_map.91.refs_10_
  50.3 0.4 collective-permute-done.7.refs_8_
  50.6 9.1 %collective-permute-done.4.refs_4_ = f32[272,512]{1,0:T(8,128)S(1)} collective-permute-done((f32[272,512]{1,0:T(8,128)S(1)}, f32[272,512]{1,0:T(8,128)S(1)}, u32[]{:S(2)}, u32[]{:S(2)}) %collective-permute-start.4) | collective-permute-done | bytes 557088 | tf_op jit(solution)/shard_map/ppermute | solution.py:48
  59.7 1.3 %shard_map.92 = (f32[16,3,2,8,512]{4,3,2,1,0:T(8,128)S(1)}, f32[272,512]{1,0:T(8,128)S(1)}, f32[272,512]{1,0:T(8,128)S(1)}, f32[80,512]{1,0:T(8,128)S(1)}, f32[64,512]{1,0:T(8,128)S(1)}, /*index=5*/f32[64,512]{1,0:T(8,128)S(1)}) custom-call(f32[16,3,2,8,512]{4,3,2,1,0:T(8,128)S(1)} %get-tuple-element.45.a_ref.refs_0_, f32[3,2,8,512]{3,2,1,0:T(8,128)S(1)} %copy-done.2, ...), custom_call_target="tpu_custom_call" | custom-call | tf_op jit(solution)/shard_map/pallas_call | solution.py:531
  61.0 6.4 %collective-permute-start.8 = (f32[272,512]{1,0:T(8,128)S(1)}, f32[272,512]{1,0:T(8,128)S(1)}, u32[]{:S(2)}, u32[]{:S(2)}) collective-permute-start(f32[272,512]{1,0:T(8,128)S(1)} %get-tuple-element.55), channel_id=1, source_target_pairs={{0,124},{1,125},{2,126},{3,127},{4,8},{5,9},{6,10},{7,11},{8,4},{9... | collective-permute-start | bytes 1671176 | tf_op jit(solution)/shard_map/ppermute | solution.py:48
  67.4 1.3 %collective-permute-start.10 = (f32[80,512]{1,0:T(8,128)S(1)}, f32[80,512]{1,0:T(8,128)S(1)}, u32[]{:S(2)}, u32[]{:S(2)}) collective-permute-start(f32[80,512]{1,0:T(8,128)S(1)} %get-tuple-element.57.refs_9_), channel_id=1, source_target_pairs={{1,0},{2,1},{3,2},{5,4},{6,5},{7,6},{9,8},{10,9},{11,10},{13,12},{... | collective-permute-start | bytes 491528 | tf_op jit(solution)/shard_map/ppermute | solution.py:38
  68.7 3.0 %collective-permute-start.11 = (f32[64,512]{1,0:T(8,128)S(1)}, f32[64,512]{1,0:T(8,128)S(1)}, u32[]{:S(2)}, u32[]{:S(2)}) collective-permute-start(f32[64,512]{1,0:T(8,128)S(1)} %get-tuple-element.58), channel_id=1, source_target_pairs={{0,1},{1,2},{2,3},{4,5},{5,6},{6,7},{8,9},{9,10},{10,11},{12,13},{... | collective-permute-start | bytes 393224 | tf_op jit(solution)/shard_map/ppermute | solution.py:38
  71.7 0.6 shard_map.93.refs_10_
  72.3 0.4 collective-permute-done.11.refs_8_
  72.7 8.9 %collective-permute-done.8.refs_4_ = f32[272,512]{1,0:T(8,128)S(1)} collective-permute-done((f32[272,512]{1,0:T(8,128)S(1)}, f32[272,512]{1,0:T(8,128)S(1)}, u32[]{:S(2)}, u32[]{:S(2)}) %collective-permute-start.8) | collective-permute-done | bytes 557088 | tf_op jit(solution)/shard_map/ppermute | solution.py:48
  81.7 1.7 %shard_map.94 = (f32[16,3,2,8,512]{4,3,2,1,0:T(8,128)}, f32[16,3,2,8,512]{4,3,2,1,0:T(8,128)}) custom-call(f32[16,3,2,8,512]{4,3,2,1,0:T(8,128)S(1)} %get-tuple-element.54.a_ref.refs_0_, f32[3,2,8,512]{3,2,1,0:T(8,128)S(1)} %copy-done.2, f32[296,512]{1,0:T(8,128)S(1)} %collective-permute-done.2.refs_2_.refs_4_, ...), custom_call_target="tpu_custom_call" | custom-call | tf_op jit(solution)/shard_map/pallas_call | solution.py:531
  (29 shorter events, 0.5 us)
Async XLA Ops:
  2.7 7.3 %collective-permute-start = (f32[88,512]{1,0:T(8,128)}, f32[88,512]{1,0:T(8,128)S(1)}, u32[]{:S(2)}, u32[]{:S(2)}) collective-permute-start(f32[88,512]{1,0:T(8,128)} %get-tuple-element.33), channel_id=1, source_target_pairs={{1,2},{2,1},{5,6},{6,5},{9,10},{10,9},{13,14},{14,13},{17,18},{18,... | collective-permute-start | bytes 540680 | tf_op jit(solution)/shard_map/ppermute | solution.py:54
  3.4 6.6 %collective-permute-start.1 = (f32[88,512]{1,0:T(8,128)}, f32[88,512]{1,0:T(8,128)S(1)}, u32[]{:S(2)}, u32[]{:S(2)}) collective-permute-start(f32[88,512]{1,0:T(8,128)} %get-tuple-element.34), channel_id=1, source_target_pairs={{0,1},{1,0},{2,3},{3,2},{4,5},{5,4},{6,7},{7,6},{8,9},{9,8},{10,11... | collective-permute-start | bytes 540680 | tf_op jit(solution)/shard_map/ppermute | solution.py:54
  6.4 1.4 %copy-start = (f32[16,3,2,8,512]{4,3,2,1,0:T(8,128)S(1)}, f32[16,3,2,8,512]{4,3,2,1,0:T(8,128)}, u32[]{:S(2)}) copy-start(f32[16,3,2,8,512]{4,3,2,1,0:T(8,128)} %refs_14_.1) | copy-start | bytes 4718596
  7.8 0.8 copy-start.3
  8.6 10.8 %copy-start.6 = (f32[3,16,4]{1,2,0:T(4,128)S(1)}, f32[3,16,4]{1,2,0:T(4,128)}, u32[]{:S(2)}) copy-start(f32[3,16,4]{1,2,0:T(4,128)} %param.12) | copy-start | bytes 2308
  8.6 26.9 %copy-start.1 = (f32[16,3,2,8,512]{4,3,2,1,0:T(8,128)S(1)}, f32[16,3,2,8,512]{4,3,2,1,0:T(8,128)}, u32[]{:S(2)}) copy-start(f32[16,3,2,8,512]{4,3,2,1,0:T(8,128)} %refs_14_.1) | copy-start | bytes 4718596
  10.0 25.6 %copy-start.2 = (f32[3,2,8,512]{3,2,1,0:T(8,128)S(1)}, f32[3,2,8,512]{3,2,1,0:T(8,128)}, u32[]{:S(2)}) copy-start(f32[3,2,8,512]{3,2,1,0:T(8,128)} %get-tuple-element.32.refs_1_.nu_ref) | copy-start | bytes 294916
  10.0 25.6 %copy-start.4 = (f32[2,8,512]{2,1,0:T(8,128)S(1)}, f32[2,8,512]{2,1,0:T(8,128)}, u32[]{:S(2)}) copy-start(f32[2,8,512]{2,1,0:T(8,128)} %get-tuple-element.43.refs_10_) | copy-start | bytes 98308
  10.0 25.6 %copy-start.5 = (s32[16,128]{1,0:T(8,128)S(1)}, s32[16,128]{1,0:T(8,128)}, u32[]{:S(2)}) copy-start(s32[16,128]{1,0:T(8,128)} %get-tuple-element.44.refs_11_) | copy-start | bytes 24580
  10.7 24.9 %collective-permute-start.2 = (f32[296,512]{1,0:T(8,128)}, f32[296,512]{1,0:T(8,128)S(1)}, u32[]{:S(2)}, u32[]{:S(2)}) collective-permute-start(f32[296,512]{1,0:T(8,128)} %get-tuple-element.38), channel_id=1, source_target_pairs={{0,124},{1,125},{2,126},{3,127},{4,8},{5,9},{6,10},{7,11},{8,4},{9... | collective-permute-start | bytes 1818632 | tf_op jit(solution)/shard_map/ppermute | solution.py:48
  19.4 16.2 %collective-permute-start.3 = (f32[296,512]{1,0:T(8,128)}, f32[296,512]{1,0:T(8,128)S(1)}, u32[]{:S(2)}, u32[]{:S(2)}) collective-permute-start(f32[296,512]{1,0:T(8,128)} %get-tuple-element.39), channel_id=1, source_target_pairs={{0,4},{1,5},{2,6},{3,7},{4,0},{5,1},{6,2},{7,3},{8,12},{9,13},{10,... | collective-permute-start | bytes 1818632 | tf_op jit(solution)/shard_map/ppermute | solution.py:48
  39.1 20.6 %collective-permute-start.4 = (f32[272,512]{1,0:T(8,128)S(1)}, f32[272,512]{1,0:T(8,128)S(1)}, u32[]{:S(2)}, u32[]{:S(2)}) collective-permute-start(f32[272,512]{1,0:T(8,128)S(1)} %get-tuple-element.46), channel_id=1, source_target_pairs={{0,124},{1,125},{2,126},{3,127},{4,8},{5,9},{6,10},{7,11},{8,4},{9... | collective-permute-start | bytes 1671176 | tf_op jit(solution)/shard_map/ppermute | solution.py:48
  45.3 14.4 %collective-permute-start.5 = (f32[272,512]{1,0:T(8,128)S(1)}, f32[272,512]{1,0:T(8,128)S(1)}, u32[]{:S(2)}, u32[]{:S(2)}) collective-permute-start(f32[272,512]{1,0:T(8,128)S(1)} %get-tuple-element.47), channel_id=1, source_target_pairs={{0,4},{1,5},{2,6},{3,7},{4,0},{5,1},{6,2},{7,3},{8,12},{9,13},{10,... | collective-permute-start | bytes 1671176 | tf_op jit(solution)/shard_map/ppermute | solution.py:48
  45.3 4.3 %collective-permute-start.6 = (f32[80,512]{1,0:T(8,128)S(1)}, f32[80,512]{1,0:T(8,128)S(1)}, u32[]{:S(2)}, u32[]{:S(2)}) collective-permute-start(f32[80,512]{1,0:T(8,128)S(1)} %get-tuple-element.48.refs_9_), channel_id=1, source_target_pairs={{1,0},{2,1},{3,2},{5,4},{6,5},{7,6},{9,8},{10,9},{11,10},{13,12},{... | collective-permute-start | bytes 491528 | tf_op jit(solution)/shard_map/ppermute | solution.py:38
  46.6 4.0 %collective-permute-start.7 = (f32[64,512]{1,0:T(8,128)S(1)}, f32[64,512]{1,0:T(8,128)S(1)}, u32[]{:S(2)}, u32[]{:S(2)}) collective-permute-start(f32[64,512]{1,0:T(8,128)S(1)} %get-tuple-element.49), channel_id=1, source_target_pairs={{0,1},{1,2},{2,3},{4,5},{5,6},{6,7},{8,9},{9,10},{10,11},{12,13},{... | collective-permute-start | bytes 393224 | tf_op jit(solution)/shard_map/ppermute | solution.py:38
  61.0 20.7 %collective-permute-start.8 = (f32[272,512]{1,0:T(8,128)S(1)}, f32[272,512]{1,0:T(8,128)S(1)}, u32[]{:S(2)}, u32[]{:S(2)}) collective-permute-start(f32[272,512]{1,0:T(8,128)S(1)} %get-tuple-element.55), channel_id=1, source_target_pairs={{0,124},{1,125},{2,126},{3,127},{4,8},{5,9},{6,10},{7,11},{8,4},{9... | collective-permute-start | bytes 1671176 | tf_op jit(solution)/shard_map/ppermute | solution.py:48
  67.4 14.3 %collective-permute-start.9 = (f32[272,512]{1,0:T(8,128)S(1)}, f32[272,512]{1,0:T(8,128)S(1)}, u32[]{:S(2)}, u32[]{:S(2)}) collective-permute-start(f32[272,512]{1,0:T(8,128)S(1)} %get-tuple-element.56), channel_id=1, source_target_pairs={{0,4},{1,5},{2,6},{3,7},{4,0},{5,1},{6,2},{7,3},{8,12},{9,13},{10,... | collective-permute-start | bytes 1671176 | tf_op jit(solution)/shard_map/ppermute | solution.py:48
  67.4 4.3 %collective-permute-start.10 = (f32[80,512]{1,0:T(8,128)S(1)}, f32[80,512]{1,0:T(8,128)S(1)}, u32[]{:S(2)}, u32[]{:S(2)}) collective-permute-start(f32[80,512]{1,0:T(8,128)S(1)} %get-tuple-element.57.refs_9_), channel_id=1, source_target_pairs={{1,0},{2,1},{3,2},{5,4},{6,5},{7,6},{9,8},{10,9},{11,10},{13,12},{... | collective-permute-start | bytes 491528 | tf_op jit(solution)/shard_map/ppermute | solution.py:38
  68.7 4.0 %collective-permute-start.11 = (f32[64,512]{1,0:T(8,128)S(1)}, f32[64,512]{1,0:T(8,128)S(1)}, u32[]{:S(2)}, u32[]{:S(2)}) collective-permute-start(f32[64,512]{1,0:T(8,128)S(1)} %get-tuple-element.58), channel_id=1, source_target_pairs={{0,1},{1,2},{2,3},{4,5},{5,6},{6,7},{8,9},{9,10},{10,11},{12,13},{... | collective-permute-start | bytes 393224 | tf_op jit(solution)/shard_map/ppermute | solution.py:38

commit v8 on v7

--- a/solution.py
+++ b/solution.py
@@ -127,7 +127,7 @@
 
 def edge_kernel(
     per, a_hbm, reluct_hbm, lam_hbm, mag_hbm, reg_hbm, slots_hbm,
-    ax_far, ax_near, nu_ref, code_ref, offset_ref, static_ref,
+    ax_near, ax_far, nu_ref, code_ref, offset_ref, static_ref,
     first_ref, last_ref, lam_ref, mag_ref, reg_ref, slots_ref, sems,
 ):
     devs = a_hbm.shape[0]
@@ -205,7 +205,7 @@
     by_parity("az", body, far, near)
 
 
-def corner_kernel(end, devs, ax_far, ax_near, far_in, near_in, far, near, sems):
+def corner_kernel(end, devs, ax_near, ax_far, far_in, near_in, far, near, sems):
     at = pl.ds(end, devs)
 
     def body_ax(ax_ahead, ax_behind):
@@ -227,7 +227,7 @@
     by_parity("ax", body_ax, ax_far, ax_near)
 
 
-def settle_kernel(halo_far, halo_near, a_ref, ahead, behind, minus):
+def settle_kernel(halo_near, halo_far, a_ref, ahead, behind, minus):
     devs = a_ref.shape[0]
 
     def body(ahead_ref, behind_ref):
@@ -467,7 +467,7 @@
         jax.ShapeDtypeStruct(slot_map.shape, jnp.int32),
         f32(3 * cells_ax, radial),
     ]
-    ax_far, ax_near, nu, code, offset, static = pl.pallas_call(
+    ax_near, ax_far, nu, code, offset, static = pl.pallas_call(
         functools.partial(edge_kernel, per),
         out_shape=edges,
         in_specs=[HBM] * 6,
@@ -477,7 +477,7 @@
         + [pltpu.VMEM(slot_map.shape, jnp.int32), pltpu.SemaphoreType.DMA((15,))],
         compiler_params=pltpu.CompilerParams(vmem_limit_bytes=LIMIT_FIRST),
     )(start_field, reluctivity, lamination, magnets, region_ids, slot_map)
-    ax_halos = swapped_ax(ax_far, 1), swapped_ax(ax_near, 0)
+    ax_halos = swapped_ax(ax_near, 0), swapped_ax(ax_far, 1)
     planes = [f32(whole + devs + 3 * cells_ax, radial)] * 2
     packed = pl.pallas_call(
         plane_kernel,

time: 83.7 us -> 81.3 us (0.971)
  starting transfers between devices: 33.7 us -> 30.9 us
    ppermute x2, starting transfers between devices: 3.68 us -> 0.76 us  [swapped_ax(): lax.ppermute(value, 'ax', [(q, to) for q, to in pairs if 0 <= to < count])]
    ppermute x4, starting transfers between devices: 8.64 us -> 10.3 us  [moved(): return lax.ppermute(value, ('az', 'ax'), pairs)]
    ppermute x6, starting transfers between devices: 21.4 us -> 19.9 us  [swapped(): return lax.ppermute(value, ('az', 'ax'), pairs)]
where the time goes in v8:
time: 81.3 us; the launch traced here: 80.5 us
  starting transfers between devices  30.9 us (38%)
  waiting for transfers between devices  19.5 us (24%)
  blocking collectives  14.9 us (18%)
  Pallas kernels  11.7 us (14%)
  local copies, waits for them, and re-layouts  2.52 us (3%)
  between operations  0.85 us (1%)
    ppermute x6, starting transfers between devices, swapped(): return lax.ppermute(value, ('az', 'ax'), pairs)  19.9 us
    ppermute x6, waiting for transfers between devices, swapped(): return lax.ppermute(value, ('az', 'ax'), pairs)  18.7 us
    all_to_all x1, blocking collectives, shards(): lax.all_to_all(jnp.broadcast_to(flat, (count_az, comps * devs * per)), 'a...  14.9 us
    ppermute x4, starting transfers between devices, moved(): return lax.ppermute(value, ('az', 'ax'), pairs)  10.3 us
    pallas_call x3, Pallas kernels, step(): pl.pallas_call(functools.partial(step_kernel, stage, per), out_shape=outs...  6.4 us
    unnamed x15, local copies, waits for them, and re-layouts  2.31 us
    pallas_call x1, Pallas kernels, shards(): pl.pallas_call(functools.partial(edge_kernel, per), out_shape=edges, in_s...  2.08 us
  transfers between devices with their start and end apart: 12, of which 4 were waited for; matrix products, arithmetic and copies ran while one was open for 0% of the time, Pallas kernels for 3%

profile of v8, /device:TPU:0, one launch (start us, length us, event | category | flops | bytes accessed | tf_op | source)
XLA Modules:
  0.0 80.5 jit_solution(16932548041598949219)
XLA Ops:
  0.6 2.1 %shard_map.86 = (f32[88,512]{1,0:T(8,128)}, f32[88,512]{1,0:T(8,128)}, f32[3,2,8,512]{3,2,1,0:T(8,128)}, f32[2,8,512]{2,1,0:T(8,128)}, s32[16,128]{1,0:T(8,128)}, /*index=5*/f32[24,512]{1,0:T(8,128)}) custom-call(f32[16,3,2,8,512]{4,3,2,1,0:T(8,128)} %refs_14_.1, f32[3,2,8,512]{3,2,1,0:T(8,128)} %reluct_hbm.1, s32[2,8,512]{2,1,0:T(8,128)} %lam_hbm.1, ...), custom_call_target="tpu_custom_call" | custom-call | tf_op jit(solution)/shard_map/pallas_call | solution.py:470
  2.8 0.7 collective-permute-start.1
  3.5 1.4 %copy-done = f32[16,3,2,8,512]{4,3,2,1,0:T(8,128)S(1)} copy-done((f32[16,3,2,8,512]{4,3,2,1,0:T(8,128)S(1)}, f32[16,3,2,8,512]{4,3,2,1,0:T(8,128)}, u32[]{:S(2)}) %copy-start) | copy-done | bytes 1572888
  4.9 0.8 copy-done.3
  5.7 1.4 %shard_map.87 = (f32[296,512]{1,0:T(8,128)}, f32[296,512]{1,0:T(8,128)}) custom-call(f32[16,3,2,8,512]{4,3,2,1,0:T(8,128)S(1)} %copy-done, f32[24,512]{1,0:T(8,128)S(1)} %copy-done.3), custom_call_target="tpu_custom_call" | custom-call | flops 10000000 | bytes 3145728 | tf_op jit(solution)/shard_map/pallas_call | solution.py:482
  7.1 0.7 shard_map.88
  7.8 9.1 %collective-permute-start.2 = (f32[296,512]{1,0:T(8,128)}, f32[296,512]{1,0:T(8,128)S(1)}, u32[]{:S(2)}, u32[]{:S(2)}) collective-permute-start(f32[296,512]{1,0:T(8,128)} %get-tuple-element.38), channel_id=1, source_target_pairs={{0,124},{1,125},{2,126},{3,127},{4,8},{5,9},{6,10},{7,11},{8,4},{9... | collective-permute-start | bytes 1818632 | tf_op jit(solution)/shard_map/ppermute | solution.py:48
  17.0 0.1 broadcast_in_dim.7
  17.1 14.9 %all_to_all.6 = f32[32,1,192]{2,1,0:T(1,128)S(1)} all-to-all(f32[32,1,192]{2,1,0:T(1,128)S(1)} %broadcast_in_dim.8), channel_id=1, replica_groups=mesh['az'=32,'ax'=4] {'az'}, dimensions={0} | all-to-all | bytes 49152 | tf_op jit(solution)/shard_map/all_to_all | solution.py:509
  32.3 3.5 %shard_map.90 = (f32[16,3,2,8,512]{4,3,2,1,0:T(8,128)S(1)}, f32[272,512]{1,0:T(8,128)S(1)}, f32[272,512]{1,0:T(8,128)S(1)}, f32[80,512]{1,0:T(8,128)S(1)}, f32[6...) custom-call(f32[16,3,2,8,512]{4,3,2,1,0:T(8,128)S(1)} %copy-done.1, ...), custom_call_target="tpu_custom_call" | custom-call | tf_op jit(solution)/shard_map/pallas_call | solution.py:531
  35.8 5.6 %collective-permute-start.4 = (f32[272,512]{1,0:T(8,128)S(1)}, f32[272,512]{1,0:T(8,128)S(1)}, u32[]{:S(2)}, u32[]{:S(2)}) collective-permute-start(f32[272,512]{1,0:T(8,128)S(1)} %get-tuple-element.46), channel_id=1, source_target_pairs={{0,124},{1,125},{2,126},{3,127},{4,8},{5,9},{6,10},{7,11},{8,4},{9... | collective-permute-start | bytes 1671176 | tf_op jit(solution)/shard_map/ppermute | solution.py:48
  41.4 1.3 %collective-permute-start.6 = (f32[80,512]{1,0:T(8,128)S(1)}, f32[80,512]{1,0:T(8,128)S(1)}, u32[]{:S(2)}, u32[]{:S(2)}) collective-permute-start(f32[80,512]{1,0:T(8,128)S(1)} %get-tuple-element.48.refs_9_), channel_id=1, source_target_pairs={{1,0},{2,1},{3,2},{5,4},{6,5},{7,6},{9,8},{10,9},{11,10},{13,12},{... | collective-permute-start | bytes 491528 | tf_op jit(solution)/shard_map/ppermute | solution.py:38
  42.7 4.4 %collective-permute-start.7 = (f32[64,512]{1,0:T(8,128)S(1)}, f32[64,512]{1,0:T(8,128)S(1)}, u32[]{:S(2)}, u32[]{:S(2)}) collective-permute-start(f32[64,512]{1,0:T(8,128)S(1)} %get-tuple-element.49), channel_id=1, source_target_pairs={{0,1},{1,2},{2,3},{4,5},{5,6},{6,7},{8,9},{9,10},{10,11},{12,13},{... | collective-permute-start | bytes 393224 | tf_op jit(solution)/shard_map/ppermute | solution.py:38
  47.1 0.6 shard_map.91.refs_10_
  47.7 0.4 collective-permute-done.7.refs_8_
  48.1 8.2 %collective-permute-done.4.refs_4_ = f32[272,512]{1,0:T(8,128)S(1)} collective-permute-done((f32[272,512]{1,0:T(8,128)S(1)}, f32[272,512]{1,0:T(8,128)S(1)}, u32[]{:S(2)}, u32[]{:S(2)}) %collective-permute-start.4) | collective-permute-done | bytes 557088 | tf_op jit(solution)/shard_map/ppermute | solution.py:48
  56.3 1.3 %shard_map.92 = (f32[16,3,2,8,512]{4,3,2,1,0:T(8,128)S(1)}, f32[272,512]{1,0:T(8,128)S(1)}, f32[272,512]{1,0:T(8,128)S(1)}, f32[80,512]{1,0:T(8,128)S(1)}, f32[64,512]{1,0:T(8,128)S(1)}, /*index=5*/f32[64,512]{1,0:T(8,128)S(1)}) custom-call(f32[16,3,2,8,512]{4,3,2,1,0:T(8,128)S(1)} %get-tuple-element.45.a_ref.refs_0_, f32[3,2,8,512]{3,2,1,0:T(8,128)S(1)} %copy-done.2, ...), custom_call_target="tpu_custom_call" | custom-call | tf_op jit(solution)/shard_map/pallas_call | solution.py:531
  57.6 5.2 %collective-permute-start.8 = (f32[272,512]{1,0:T(8,128)S(1)}, f32[272,512]{1,0:T(8,128)S(1)}, u32[]{:S(2)}, u32[]{:S(2)}) collective-permute-start(f32[272,512]{1,0:T(8,128)S(1)} %get-tuple-element.55), channel_id=1, source_target_pairs={{0,124},{1,125},{2,126},{3,127},{4,8},{5,9},{6,10},{7,11},{8,4},{9... | collective-permute-start | bytes 1671176 | tf_op jit(solution)/shard_map/ppermute | solution.py:48
  62.8 1.3 %collective-permute-start.10 = (f32[80,512]{1,0:T(8,128)S(1)}, f32[80,512]{1,0:T(8,128)S(1)}, u32[]{:S(2)}, u32[]{:S(2)}) collective-permute-start(f32[80,512]{1,0:T(8,128)S(1)} %get-tuple-element.57.refs_9_), channel_id=1, source_target_pairs={{1,0},{2,1},{3,2},{5,4},{6,5},{7,6},{9,8},{10,9},{11,10},{13,12},{... | collective-permute-start | bytes 491528 | tf_op jit(solution)/shard_map/ppermute | solution.py:38
  64.1 3.3 %collective-permute-start.11 = (f32[64,512]{1,0:T(8,128)S(1)}, f32[64,512]{1,0:T(8,128)S(1)}, u32[]{:S(2)}, u32[]{:S(2)}) collective-permute-start(f32[64,512]{1,0:T(8,128)S(1)} %get-tuple-element.58), channel_id=1, source_target_pairs={{0,1},{1,2},{2,3},{4,5},{5,6},{6,7},{8,9},{9,10},{10,11},{12,13},{... | collective-permute-start | bytes 393224 | tf_op jit(solution)/shard_map/ppermute | solution.py:38
  67.4 0.6 shard_map.93.refs_10_
  68.0 0.4 collective-permute-done.11.refs_8_
  68.3 10.5 %collective-permute-done.8.refs_4_ = f32[272,512]{1,0:T(8,128)S(1)} collective-permute-done((f32[272,512]{1,0:T(8,128)S(1)}, f32[272,512]{1,0:T(8,128)S(1)}, u32[]{:S(2)}, u32[]{:S(2)}) %collective-permute-start.8) | collective-permute-done | bytes 557088 | tf_op jit(solution)/shard_map/ppermute | solution.py:48
  78.9 1.7 %shard_map.94 = (f32[16,3,2,8,512]{4,3,2,1,0:T(8,128)}, f32[16,3,2,8,512]{4,3,2,1,0:T(8,128)}) custom-call(f32[16,3,2,8,512]{4,3,2,1,0:T(8,128)S(1)} %get-tuple-element.54.a_ref.refs_0_, f32[3,2,8,512]{3,2,1,0:T(8,128)S(1)} %copy-done.2, f32[296,512]{1,0:T(8,128)S(1)} %collective-permute-done.2.refs_2_.refs_4_, ...), custom_call_target="tpu_custom_call" | custom-call | tf_op jit(solution)/shard_map/pallas_call | solution.py:531
  (29 shorter events, 0.5 us)
Async XLA Ops:
  2.7 4.4 %collective-permute-start = (f32[88,512]{1,0:T(8,128)}, f32[88,512]{1,0:T(8,128)S(1)}, u32[]{:S(2)}, u32[]{:S(2)}) collective-permute-start(f32[88,512]{1,0:T(8,128)} %get-tuple-element.33), channel_id=1, source_target_pairs={{0,1},{1,0},{2,3},{3,2},{4,5},{5,4},{6,7},{7,6},{8,9},{9,8},{10,11... | collective-permute-start | bytes 540680 | tf_op jit(solution)/shard_map/ppermute | solution.py:54
  2.8 4.3 %collective-permute-start.1 = (f32[88,512]{1,0:T(8,128)}, f32[88,512]{1,0:T(8,128)S(1)}, u32[]{:S(2)}, u32[]{:S(2)}) collective-permute-start(f32[88,512]{1,0:T(8,128)} %get-tuple-element.34), channel_id=1, source_target_pairs={{1,2},{2,1},{5,6},{6,5},{9,10},{10,9},{13,14},{14,13},{17,18},{18,... | collective-permute-start | bytes 540680 | tf_op jit(solution)/shard_map/ppermute | solution.py:54
  3.5 1.4 %copy-start = (f32[16,3,2,8,512]{4,3,2,1,0:T(8,128)S(1)}, f32[16,3,2,8,512]{4,3,2,1,0:T(8,128)}, u32[]{:S(2)}) copy-start(f32[16,3,2,8,512]{4,3,2,1,0:T(8,128)} %refs_14_.1) | copy-start | bytes 4718596
  4.9 0.8 copy-start.3
  5.7 11.2 %copy-start.6 = (f32[3,16,4]{1,2,0:T(4,128)S(1)}, f32[3,16,4]{1,2,0:T(4,128)}, u32[]{:S(2)}) copy-start(f32[3,16,4]{1,2,0:T(4,128)} %param.12) | copy-start | bytes 2308
  5.7 26.5 %copy-start.1 = (f32[16,3,2,8,512]{4,3,2,1,0:T(8,128)S(1)}, f32[16,3,2,8,512]{4,3,2,1,0:T(8,128)}, u32[]{:S(2)}) copy-start(f32[16,3,2,8,512]{4,3,2,1,0:T(8,128)} %refs_14_.1) | copy-start | bytes 4718596
  7.1 25.2 %copy-start.2 = (f32[3,2,8,512]{3,2,1,0:T(8,128)S(1)}, f32[3,2,8,512]{3,2,1,0:T(8,128)}, u32[]{:S(2)}) copy-start(f32[3,2,8,512]{3,2,1,0:T(8,128)} %get-tuple-element.32.refs_1_.nu_ref) | copy-start | bytes 294916
  7.1 25.2 %copy-start.4 = (f32[2,8,512]{2,1,0:T(8,128)S(1)}, f32[2,8,512]{2,1,0:T(8,128)}, u32[]{:S(2)}) copy-start(f32[2,8,512]{2,1,0:T(8,128)} %get-tuple-element.43.refs_10_) | copy-start | bytes 98308
  7.1 25.2 %copy-start.5 = (s32[16,128]{1,0:T(8,128)S(1)}, s32[16,128]{1,0:T(8,128)}, u32[]{:S(2)}) copy-start(s32[16,128]{1,0:T(8,128)} %get-tuple-element.44.refs_11_) | copy-start | bytes 24580
  7.8 24.5 %collective-permute-start.2 = (f32[296,512]{1,0:T(8,128)}, f32[296,512]{1,0:T(8,128)S(1)}, u32[]{:S(2)}, u32[]{:S(2)}) collective-permute-start(f32[296,512]{1,0:T(8,128)} %get-tuple-element.38), channel_id=1, source_target_pairs={{0,124},{1,125},{2,126},{3,127},{4,8},{5,9},{6,10},{7,11},{8,4},{9... | collective-permute-start | bytes 1818632 | tf_op jit(solution)/shard_map/ppermute | solution.py:48
  16.9 15.4 %collective-permute-start.3 = (f32[296,512]{1,0:T(8,128)}, f32[296,512]{1,0:T(8,128)S(1)}, u32[]{:S(2)}, u32[]{:S(2)}) collective-permute-start(f32[296,512]{1,0:T(8,128)} %get-tuple-element.39), channel_id=1, source_target_pairs={{0,4},{1,5},{2,6},{3,7},{4,0},{5,1},{6,2},{7,3},{8,12},{9,13},{10,... | collective-permute-start | bytes 1818632 | tf_op jit(solution)/shard_map/ppermute | solution.py:48
  35.8 20.5 %collective-permute-start.4 = (f32[272,512]{1,0:T(8,128)S(1)}, f32[272,512]{1,0:T(8,128)S(1)}, u32[]{:S(2)}, u32[]{:S(2)}) collective-permute-start(f32[272,512]{1,0:T(8,128)S(1)} %get-tuple-element.46), channel_id=1, source_target_pairs={{0,124},{1,125},{2,126},{3,127},{4,8},{5,9},{6,10},{7,11},{8,4},{9... | collective-permute-start | bytes 1671176 | tf_op jit(solution)/shard_map/ppermute | solution.py:48
  41.4 14.9 %collective-permute-start.5 = (f32[272,512]{1,0:T(8,128)S(1)}, f32[272,512]{1,0:T(8,128)S(1)}, u32[]{:S(2)}, u32[]{:S(2)}) collective-permute-start(f32[272,512]{1,0:T(8,128)S(1)} %get-tuple-element.47), channel_id=1, source_target_pairs={{0,4},{1,5},{2,6},{3,7},{4,0},{5,1},{6,2},{7,3},{8,12},{9,13},{10,... | collective-permute-start | bytes 1671176 | tf_op jit(solution)/shard_map/ppermute | solution.py:48
  41.4 5.7 %collective-permute-start.6 = (f32[80,512]{1,0:T(8,128)S(1)}, f32[80,512]{1,0:T(8,128)S(1)}, u32[]{:S(2)}, u32[]{:S(2)}) collective-permute-start(f32[80,512]{1,0:T(8,128)S(1)} %get-tuple-element.48.refs_9_), channel_id=1, source_target_pairs={{1,0},{2,1},{3,2},{5,4},{6,5},{7,6},{9,8},{10,9},{11,10},{13,12},{... | collective-permute-start | bytes 491528 | tf_op jit(solution)/shard_map/ppermute | solution.py:38
  42.7 5.4 %collective-permute-start.7 = (f32[64,512]{1,0:T(8,128)S(1)}, f32[64,512]{1,0:T(8,128)S(1)}, u32[]{:S(2)}, u32[]{:S(2)}) collective-permute-start(f32[64,512]{1,0:T(8,128)S(1)} %get-tuple-element.49), channel_id=1, source_target_pairs={{0,1},{1,2},{2,3},{4,5},{5,6},{6,7},{8,9},{9,10},{10,11},{12,13},{... | collective-permute-start | bytes 393224 | tf_op jit(solution)/shard_map/ppermute | solution.py:38
  57.6 21.3 %collective-permute-start.8 = (f32[272,512]{1,0:T(8,128)S(1)}, f32[272,512]{1,0:T(8,128)S(1)}, u32[]{:S(2)}, u32[]{:S(2)}) collective-permute-start(f32[272,512]{1,0:T(8,128)S(1)} %get-tuple-element.55), channel_id=1, source_target_pairs={{0,124},{1,125},{2,126},{3,127},{4,8},{5,9},{6,10},{7,11},{8,4},{9... | collective-permute-start | bytes 1671176 | tf_op jit(solution)/shard_map/ppermute | solution.py:48
  62.8 16.1 %collective-permute-start.9 = (f32[272,512]{1,0:T(8,128)S(1)}, f32[272,512]{1,0:T(8,128)S(1)}, u32[]{:S(2)}, u32[]{:S(2)}) collective-permute-start(f32[272,512]{1,0:T(8,128)S(1)} %get-tuple-element.56), channel_id=1, source_target_pairs={{0,4},{1,5},{2,6},{3,7},{4,0},{5,1},{6,2},{7,3},{8,12},{9,13},{10,... | collective-permute-start | bytes 1671176 | tf_op jit(solution)/shard_map/ppermute | solution.py:48
  62.8 4.6 %collective-permute-start.10 = (f32[80,512]{1,0:T(8,128)S(1)}, f32[80,512]{1,0:T(8,128)S(1)}, u32[]{:S(2)}, u32[]{:S(2)}) collective-permute-start(f32[80,512]{1,0:T(8,128)S(1)} %get-tuple-element.57.refs_9_), channel_id=1, source_target_pairs={{1,0},{2,1},{3,2},{5,4},{6,5},{7,6},{9,8},{10,9},{11,10},{13,12},{... | collective-permute-start | bytes 491528 | tf_op jit(solution)/shard_map/ppermute | solution.py:38
  64.1 4.3 %collective-permute-start.11 = (f32[64,512]{1,0:T(8,128)S(1)}, f32[64,512]{1,0:T(8,128)S(1)}, u32[]{:S(2)}, u32[]{:S(2)}) collective-permute-start(f32[64,512]{1,0:T(8,128)S(1)} %get-tuple-element.58), channel_id=1, source_target_pairs={{0,1},{1,2},{2,3},{4,5},{5,6},{6,7},{8,9},{9,10},{10,11},{12,13},{... | collective-permute-start | bytes 393224 | tf_op jit(solution)/shard_map/ppermute | solution.py:38

commit v9 on v8

--- a/solution.py
+++ b/solution.py
@@ -176,7 +176,7 @@
             ax_plus[pl.ds(at, 1)] = nu_ref[0, i, top:]
             ax_plus[pl.ds(at + 2, 1)] = nu_ref[2, i, top:]
             ax_plus[pl.ds(at + 4, 1)] = code_ref[i, top:]
-            ax_plus[pl.ds(at + 6, 1)] = jnp.zeros_like(code_ref[i, top:])
+            ax_plus[pl.ds(at + 6, 1)] = code_ref[i, top:]
 
         firsts = [first_ref[pl.ds(k * devs, devs)] for k in (0, 1, 4, 5)]
         lasts = [[last_ref[pl.ds((2 * c + i) * devs, devs)] for i in range(2)] for c in range(3)]
@@ -357,15 +357,16 @@
         ]
 
     if stage == 0:
+        nu_rows = nu_ax_ref[pl.ds(nu_ax, 4)]
+        code_rows = nu_ax_ref[pl.ds(nu_ax + 4, 4)]
+        upper = rows(nu_rows.shape) < 2
 
         @pl.loop(0, devs, unroll=UNROLL)
         def _(d):
-            for c in (0, 2):
-                own = values(d, c, per)
-                for i in range(2):
-                    src_ax_ref[pl.ds((c + i) * devs + d, 1)] = picked(
-                        nu_ax_ref[pl.ds(nu_ax + c + i, 1)], nu_ax_ref[pl.ds(nu_ax + 4 + i, 1)], own
-                    )
+            both = [jnp.where(upper, x, y) for x, y in zip(values(d, 0, per), values(d, 2, per))]
+            four = picked(nu_rows, code_rows, both)
+            for k in range(4):
+                src_ax_ref[pl.ds(k * devs + d, 1)] = four[k : k + 1]
 
     for at, own, sign in ((0, 2, 1.0), (1, 3, 1.0), (2, 0, -1.0), (3, 1, -1.0)):
         part = pl.ds(at * devs, devs)

time: 81.3 us -> 81.3 us (level)
  no operation moved by 1% of the time
where the time goes in v9:
time: 81.3 us; the launch traced here: 80.5 us
  starting transfers between devices  30.9 us (38%)
  waiting for transfers between devices  19.5 us (24%)
  blocking collectives  14.9 us (18%)
  Pallas kernels  11.7 us (14%)
  local copies, waits for them, and re-layouts  2.52 us (3%)
  between operations  0.85 us (1%)
    ppermute x6, starting transfers between devices, swapped(): return lax.ppermute(value, ('az', 'ax'), pairs)  19.9 us
    ppermute x6, waiting for transfers between devices, swapped(): return lax.ppermute(value, ('az', 'ax'), pairs)  18.7 us
    all_to_all x1, blocking collectives, shards(): lax.all_to_all(jnp.broadcast_to(flat, (count_az, comps * devs * per)), 'a...  14.9 us
    ppermute x4, starting transfers between devices, moved(): return lax.ppermute(value, ('az', 'ax'), pairs)  10.3 us
    pallas_call x3, Pallas kernels, step(): pl.pallas_call(functools.partial(step_kernel, stage, per), out_shape=outs...  6.34 us
    unnamed x15, local copies, waits for them, and re-layouts  2.31 us
    pallas_call x1, Pallas kernels, shards(): pl.pallas_call(functools.partial(edge_kernel, per), out_shape=edges, in_s...  2.08 us
  transfers between devices with their start and end apart: 12, of which 4 were waited for; matrix products, arithmetic and copies ran while one was open for 0% of the time, Pallas kernels for 3%

profile of v9, /device:TPU:0, one launch (start us, length us, event | category | flops | bytes accessed | tf_op | source)
XLA Modules:
  0.0 80.5 jit_solution(7053417440745007643)
XLA Ops:
  0.6 2.1 %shard_map.86 = (f32[88,512]{1,0:T(8,128)}, f32[88,512]{1,0:T(8,128)}, f32[3,2,8,512]{3,2,1,0:T(8,128)}, f32[2,8,512]{2,1,0:T(8,128)}, s32[16,128]{1,0:T(8,128)}, /*index=5*/f32[24,512]{1,0:T(8,128)}) custom-call(f32[16,3,2,8,512]{4,3,2,1,0:T(8,128)} %refs_14_.1, f32[3,2,8,512]{3,2,1,0:T(8,128)} %reluct_hbm.1, s32[2,8,512]{2,1,0:T(8,128)} %lam_hbm.1, ...), custom_call_target="tpu_custom_call" | custom-call | tf_op jit(solution)/shard_map/pallas_call | solution.py:471
  2.8 0.7 collective-permute-start.1
  3.5 1.4 %copy-done = f32[16,3,2,8,512]{4,3,2,1,0:T(8,128)S(1)} copy-done((f32[16,3,2,8,512]{4,3,2,1,0:T(8,128)S(1)}, f32[16,3,2,8,512]{4,3,2,1,0:T(8,128)}, u32[]{:S(2)}) %copy-start) | copy-done | bytes 1572888
  4.9 0.8 copy-done.3
  5.7 1.4 %shard_map.87 = (f32[296,512]{1,0:T(8,128)}, f32[296,512]{1,0:T(8,128)}) custom-call(f32[16,3,2,8,512]{4,3,2,1,0:T(8,128)S(1)} %copy-done, f32[24,512]{1,0:T(8,128)S(1)} %copy-done.3), custom_call_target="tpu_custom_call" | custom-call | flops 10000000 | bytes 3145728 | tf_op jit(solution)/shard_map/pallas_call | solution.py:483
  7.1 0.7 shard_map.88
  7.8 9.1 %collective-permute-start.2 = (f32[296,512]{1,0:T(8,128)}, f32[296,512]{1,0:T(8,128)S(1)}, u32[]{:S(2)}, u32[]{:S(2)}) collective-permute-start(f32[296,512]{1,0:T(8,128)} %get-tuple-element.38), channel_id=1, source_target_pairs={{0,124},{1,125},{2,126},{3,127},{4,8},{5,9},{6,10},{7,11},{8,4},{9... | collective-permute-start | bytes 1818632 | tf_op jit(solution)/shard_map/ppermute | solution.py:48
  17.0 0.1 broadcast_in_dim.7
  17.1 14.9 %all_to_all.6 = f32[32,1,192]{2,1,0:T(1,128)S(1)} all-to-all(f32[32,1,192]{2,1,0:T(1,128)S(1)} %broadcast_in_dim.8), channel_id=1, replica_groups=mesh['az'=32,'ax'=4] {'az'}, dimensions={0} | all-to-all | bytes 49152 | tf_op jit(solution)/shard_map/all_to_all | solution.py:510
  32.3 3.4 %shard_map.90 = (f32[16,3,2,8,512]{4,3,2,1,0:T(8,128)S(1)}, f32[272,512]{1,0:T(8,128)S(1)}, f32[272,512]{1,0:T(8,128)S(1)}, f32[80,512]{1,0:T(8,128)S(1)}, f32[6...) custom-call(f32[16,3,2,8,512]{4,3,2,1,0:T(8,128)S(1)} %copy-done.1, ...), custom_call_target="tpu_custom_call" | custom-call | tf_op jit(solution)/shard_map/pallas_call | solution.py:532
  35.8 5.6 %collective-permute-start.4 = (f32[272,512]{1,0:T(8,128)S(1)}, f32[272,512]{1,0:T(8,128)S(1)}, u32[]{:S(2)}, u32[]{:S(2)}) collective-permute-start(f32[272,512]{1,0:T(8,128)S(1)} %get-tuple-element.46), channel_id=1, source_target_pairs={{0,124},{1,125},{2,126},{3,127},{4,8},{5,9},{6,10},{7,11},{8,4},{9... | collective-permute-start | bytes 1671176 | tf_op jit(solution)/shard_map/ppermute | solution.py:48
  41.4 1.3 %collective-permute-start.6 = (f32[80,512]{1,0:T(8,128)S(1)}, f32[80,512]{1,0:T(8,128)S(1)}, u32[]{:S(2)}, u32[]{:S(2)}) collective-permute-start(f32[80,512]{1,0:T(8,128)S(1)} %get-tuple-element.48.refs_9_), channel_id=1, source_target_pairs={{1,0},{2,1},{3,2},{5,4},{6,5},{7,6},{9,8},{10,9},{11,10},{13,12},{... | collective-permute-start | bytes 491528 | tf_op jit(solution)/shard_map/ppermute | solution.py:38
  42.6 4.4 %collective-permute-start.7 = (f32[64,512]{1,0:T(8,128)S(1)}, f32[64,512]{1,0:T(8,128)S(1)}, u32[]{:S(2)}, u32[]{:S(2)}) collective-permute-start(f32[64,512]{1,0:T(8,128)S(1)} %get-tuple-element.49), channel_id=1, source_target_pairs={{0,1},{1,2},{2,3},{4,5},{5,6},{6,7},{8,9},{9,10},{10,11},{12,13},{... | collective-permute-start | bytes 393224 | tf_op jit(solution)/shard_map/ppermute | solution.py:38
  47.1 0.6 shard_map.91.refs_10_
  47.6 0.4 collective-permute-done.7.refs_8_
  48.0 8.2 %collective-permute-done.4.refs_4_ = f32[272,512]{1,0:T(8,128)S(1)} collective-permute-done((f32[272,512]{1,0:T(8,128)S(1)}, f32[272,512]{1,0:T(8,128)S(1)}, u32[]{:S(2)}, u32[]{:S(2)}) %collective-permute-start.4) | collective-permute-done | bytes 557088 | tf_op jit(solution)/shard_map/ppermute | solution.py:48
  56.2 1.3 %shard_map.92 = (f32[16,3,2,8,512]{4,3,2,1,0:T(8,128)S(1)}, f32[272,512]{1,0:T(8,128)S(1)}, f32[272,512]{1,0:T(8,128)S(1)}, f32[80,512]{1,0:T(8,128)S(1)}, f32[64,512]{1,0:T(8,128)S(1)}, /*index=5*/f32[64,512]{1,0:T(8,128)S(1)}) custom-call(f32[16,3,2,8,512]{4,3,2,1,0:T(8,128)S(1)} %get-tuple-element.45.a_ref.refs_0_, f32[3,2,8,512]{3,2,1,0:T(8,128)S(1)} %copy-done.2, ...), custom_call_target="tpu_custom_call" | custom-call | tf_op jit(solution)/shard_map/pallas_call | solution.py:532
  57.5 5.2 %collective-permute-start.8 = (f32[272,512]{1,0:T(8,128)S(1)}, f32[272,512]{1,0:T(8,128)S(1)}, u32[]{:S(2)}, u32[]{:S(2)}) collective-permute-start(f32[272,512]{1,0:T(8,128)S(1)} %get-tuple-element.55), channel_id=1, source_target_pairs={{0,124},{1,125},{2,126},{3,127},{4,8},{5,9},{6,10},{7,11},{8,4},{9... | collective-permute-start | bytes 1671176 | tf_op jit(solution)/shard_map/ppermute | solution.py:48
  62.7 1.3 %collective-permute-start.10 = (f32[80,512]{1,0:T(8,128)S(1)}, f32[80,512]{1,0:T(8,128)S(1)}, u32[]{:S(2)}, u32[]{:S(2)}) collective-permute-start(f32[80,512]{1,0:T(8,128)S(1)} %get-tuple-element.57.refs_9_), channel_id=1, source_target_pairs={{1,0},{2,1},{3,2},{5,4},{6,5},{7,6},{9,8},{10,9},{11,10},{13,12},{... | collective-permute-start | bytes 491528 | tf_op jit(solution)/shard_map/ppermute | solution.py:38
  64.0 3.3 %collective-permute-start.11 = (f32[64,512]{1,0:T(8,128)S(1)}, f32[64,512]{1,0:T(8,128)S(1)}, u32[]{:S(2)}, u32[]{:S(2)}) collective-permute-start(f32[64,512]{1,0:T(8,128)S(1)} %get-tuple-element.58), channel_id=1, source_target_pairs={{0,1},{1,2},{2,3},{4,5},{5,6},{6,7},{8,9},{9,10},{10,11},{12,13},{... | collective-permute-start | bytes 393224 | tf_op jit(solution)/shard_map/ppermute | solution.py:38
  67.3 0.6 shard_map.93.refs_10_
  67.9 0.4 collective-permute-done.11.refs_8_
  68.3 10.5 %collective-permute-done.8.refs_4_ = f32[272,512]{1,0:T(8,128)S(1)} collective-permute-done((f32[272,512]{1,0:T(8,128)S(1)}, f32[272,512]{1,0:T(8,128)S(1)}, u32[]{:S(2)}, u32[]{:S(2)}) %collective-permute-start.8) | collective-permute-done | bytes 557088 | tf_op jit(solution)/shard_map/ppermute | solution.py:48
  78.8 1.7 %shard_map.94 = (f32[16,3,2,8,512]{4,3,2,1,0:T(8,128)}, f32[16,3,2,8,512]{4,3,2,1,0:T(8,128)}) custom-call(f32[16,3,2,8,512]{4,3,2,1,0:T(8,128)S(1)} %get-tuple-element.54.a_ref.refs_0_, f32[3,2,8,512]{3,2,1,0:T(8,128)S(1)} %copy-done.2, f32[296,512]{1,0:T(8,128)S(1)} %collective-permute-done.2.refs_2_.refs_4_, ...), custom_call_target="tpu_custom_call" | custom-call | tf_op jit(solution)/shard_map/pallas_call | solution.py:532
  (29 shorter events, 0.5 us)
Async XLA Ops:
  2.7 4.4 %collective-permute-start = (f32[88,512]{1,0:T(8,128)}, f32[88,512]{1,0:T(8,128)S(1)}, u32[]{:S(2)}, u32[]{:S(2)}) collective-permute-start(f32[88,512]{1,0:T(8,128)} %get-tuple-element.33), channel_id=1, source_target_pairs={{0,1},{1,0},{2,3},{3,2},{4,5},{5,4},{6,7},{7,6},{8,9},{9,8},{10,11... | collective-permute-start | bytes 540680 | tf_op jit(solution)/shard_map/ppermute | solution.py:54
  2.8 4.3 %collective-permute-start.1 = (f32[88,512]{1,0:T(8,128)}, f32[88,512]{1,0:T(8,128)S(1)}, u32[]{:S(2)}, u32[]{:S(2)}) collective-permute-start(f32[88,512]{1,0:T(8,128)} %get-tuple-element.34), channel_id=1, source_target_pairs={{1,2},{2,1},{5,6},{6,5},{9,10},{10,9},{13,14},{14,13},{17,18},{18,... | collective-permute-start | bytes 540680 | tf_op jit(solution)/shard_map/ppermute | solution.py:54
  3.5 1.4 %copy-start = (f32[16,3,2,8,512]{4,3,2,1,0:T(8,128)S(1)}, f32[16,3,2,8,512]{4,3,2,1,0:T(8,128)}, u32[]{:S(2)}) copy-start(f32[16,3,2,8,512]{4,3,2,1,0:T(8,128)} %refs_14_.1) | copy-start | bytes 4718596
  4.9 0.8 copy-start.3
  5.7 11.2 %copy-start.6 = (f32[3,16,4]{1,2,0:T(4,128)S(1)}, f32[3,16,4]{1,2,0:T(4,128)}, u32[]{:S(2)}) copy-start(f32[3,16,4]{1,2,0:T(4,128)} %param.12) | copy-start | bytes 2308
  5.7 26.5 %copy-start.1 = (f32[16,3,2,8,512]{4,3,2,1,0:T(8,128)S(1)}, f32[16,3,2,8,512]{4,3,2,1,0:T(8,128)}, u32[]{:S(2)}) copy-start(f32[16,3,2,8,512]{4,3,2,1,0:T(8,128)} %refs_14_.1) | copy-start | bytes 4718596
  7.1 25.2 %copy-start.2 = (f32[3,2,8,512]{3,2,1,0:T(8,128)S(1)}, f32[3,2,8,512]{3,2,1,0:T(8,128)}, u32[]{:S(2)}) copy-start(f32[3,2,8,512]{3,2,1,0:T(8,128)} %get-tuple-element.32.refs_1_.nu_ref) | copy-start | bytes 294916
  7.1 25.2 %copy-start.4 = (f32[2,8,512]{2,1,0:T(8,128)S(1)}, f32[2,8,512]{2,1,0:T(8,128)}, u32[]{:S(2)}) copy-start(f32[2,8,512]{2,1,0:T(8,128)} %get-tuple-element.43.refs_10_) | copy-start | bytes 98308
  7.1 25.2 %copy-start.5 = (s32[16,128]{1,0:T(8,128)S(1)}, s32[16,128]{1,0:T(8,128)}, u32[]{:S(2)}) copy-start(s32[16,128]{1,0:T(8,128)} %get-tuple-element.44.refs_11_) | copy-start | bytes 24580
  7.8 24.5 %collective-permute-start.2 = (f32[296,512]{1,0:T(8,128)}, f32[296,512]{1,0:T(8,128)S(1)}, u32[]{:S(2)}, u32[]{:S(2)}) collective-permute-start(f32[296,512]{1,0:T(8,128)} %get-tuple-element.38), channel_id=1, source_target_pairs={{0,124},{1,125},{2,126},{3,127},{4,8},{5,9},{6,10},{7,11},{8,4},{9... | collective-permute-start | bytes 1818632 | tf_op jit(solution)/shard_map/ppermute | solution.py:48
  16.9 15.4 %collective-permute-start.3 = (f32[296,512]{1,0:T(8,128)}, f32[296,512]{1,0:T(8,128)S(1)}, u32[]{:S(2)}, u32[]{:S(2)}) collective-permute-start(f32[296,512]{1,0:T(8,128)} %get-tuple-element.39), channel_id=1, source_target_pairs={{0,4},{1,5},{2,6},{3,7},{4,0},{5,1},{6,2},{7,3},{8,12},{9,13},{10,... | collective-permute-start | bytes 1818632 | tf_op jit(solution)/shard_map/ppermute | solution.py:48
  35.8 20.5 %collective-permute-start.4 = (f32[272,512]{1,0:T(8,128)S(1)}, f32[272,512]{1,0:T(8,128)S(1)}, u32[]{:S(2)}, u32[]{:S(2)}) collective-permute-start(f32[272,512]{1,0:T(8,128)S(1)} %get-tuple-element.46), channel_id=1, source_target_pairs={{0,124},{1,125},{2,126},{3,127},{4,8},{5,9},{6,10},{7,11},{8,4},{9... | collective-permute-start | bytes 1671176 | tf_op jit(solution)/shard_map/ppermute | solution.py:48
  41.4 14.9 %collective-permute-start.5 = (f32[272,512]{1,0:T(8,128)S(1)}, f32[272,512]{1,0:T(8,128)S(1)}, u32[]{:S(2)}, u32[]{:S(2)}) collective-permute-start(f32[272,512]{1,0:T(8,128)S(1)} %get-tuple-element.47), channel_id=1, source_target_pairs={{0,4},{1,5},{2,6},{3,7},{4,0},{5,1},{6,2},{7,3},{8,12},{9,13},{10,... | collective-permute-start | bytes 1671176 | tf_op jit(solution)/shard_map/ppermute | solution.py:48
  41.4 5.7 %collective-permute-start.6 = (f32[80,512]{1,0:T(8,128)S(1)}, f32[80,512]{1,0:T(8,128)S(1)}, u32[]{:S(2)}, u32[]{:S(2)}) collective-permute-start(f32[80,512]{1,0:T(8,128)S(1)} %get-tuple-element.48.refs_9_), channel_id=1, source_target_pairs={{1,0},{2,1},{3,2},{5,4},{6,5},{7,6},{9,8},{10,9},{11,10},{13,12},{... | collective-permute-start | bytes 491528 | tf_op jit(solution)/shard_map/ppermute | solution.py:38
  42.6 5.4 %collective-permute-start.7 = (f32[64,512]{1,0:T(8,128)S(1)}, f32[64,512]{1,0:T(8,128)S(1)}, u32[]{:S(2)}, u32[]{:S(2)}) collective-permute-start(f32[64,512]{1,0:T(8,128)S(1)} %get-tuple-element.49), channel_id=1, source_target_pairs={{0,1},{1,2},{2,3},{4,5},{5,6},{6,7},{8,9},{9,10},{10,11},{12,13},{... | collective-permute-start | bytes 393224 | tf_op jit(solution)/shard_map/ppermute | solution.py:38
  57.5 21.3 %collective-permute-start.8 = (f32[272,512]{1,0:T(8,128)S(1)}, f32[272,512]{1,0:T(8,128)S(1)}, u32[]{:S(2)}, u32[]{:S(2)}) collective-permute-start(f32[272,512]{1,0:T(8,128)S(1)} %get-tuple-element.55), channel_id=1, source_target_pairs={{0,124},{1,125},{2,126},{3,127},{4,8},{5,9},{6,10},{7,11},{8,4},{9... | collective-permute-start | bytes 1671176 | tf_op jit(solution)/shard_map/ppermute | solution.py:48
  62.7 16.1 %collective-permute-start.9 = (f32[272,512]{1,0:T(8,128)S(1)}, f32[272,512]{1,0:T(8,128)S(1)}, u32[]{:S(2)}, u32[]{:S(2)}) collective-permute-start(f32[272,512]{1,0:T(8,128)S(1)} %get-tuple-element.56), channel_id=1, source_target_pairs={{0,4},{1,5},{2,6},{3,7},{4,0},{5,1},{6,2},{7,3},{8,12},{9,13},{10,... | collective-permute-start | bytes 1671176 | tf_op jit(solution)/shard_map/ppermute | solution.py:48
  62.7 4.6 %collective-permute-start.10 = (f32[80,512]{1,0:T(8,128)S(1)}, f32[80,512]{1,0:T(8,128)S(1)}, u32[]{:S(2)}, u32[]{:S(2)}) collective-permute-start(f32[80,512]{1,0:T(8,128)S(1)} %get-tuple-element.57.refs_9_), channel_id=1, source_target_pairs={{1,0},{2,1},{3,2},{5,4},{6,5},{7,6},{9,8},{10,9},{11,10},{13,12},{... | collective-permute-start | bytes 491528 | tf_op jit(solution)/shard_map/ppermute | solution.py:38
  64.0 4.3 %collective-permute-start.11 = (f32[64,512]{1,0:T(8,128)S(1)}, f32[64,512]{1,0:T(8,128)S(1)}, u32[]{:S(2)}, u32[]{:S(2)}) collective-permute-start(f32[64,512]{1,0:T(8,128)S(1)} %get-tuple-element.58), channel_id=1, source_target_pairs={{0,1},{1,2},{2,3},{4,5},{5,6},{6,7},{8,9},{9,10},{10,11},{12,13},{... | collective-permute-start | bytes 393224 | tf_op jit(solution)/shard_map/ppermute | solution.py:38
